TPU v7x, 256 devices: a whole 4x4x8 slice. The times are simulated.
256 devices in a mesh: src: 16 (over z, core), win: 4 (over y), ccd: 4 (over x).
Axes of the slice: x: 4, y: 4, z: 8, core: 2. Of those that a mesh axis runs over, the one named last changes fastest.
Arguments:
- block_bin: int32 [32768], P(('src', 'win', 'ccd')), may hold values from 0 to 7999, as said below
- block_rows: int32 [32768], P(('src', 'win', 'ccd')), may hold values from 16 to 128
- row_source: int32 [32768, 128], P(('src', 'win', 'ccd')), may hold values from 0 to 4095
- obs_resid: float32 [32768, 128], P(('src', 'win', 'ccd')), may hold values from -6 to 6
- obs_phase: float32 [32768, 128], P(('src', 'win', 'ccd')), may hold values from 0 to 1
- att_partial: float32 [32768, 4, 128], P(('src', 'win', 'ccd')), may hold values from -6 to 6
- src_partial: float32 [32768, 5, 128], P(('src', 'win', 'ccd')), may hold values from -6 to 6
Outputs:
- attitude_delta: float32 [64, 4, 128], P(('src', 'win'))
- source_delta: float32 [5, 262144], P(None, ('src', 'win'))
Inputs may be any that keep to these rules, and one draw needn't show every extreme that they name: Of the 128 blocks of one device, at most 4 fall in one window (block_bin // 125); in every draw some window receives exactly 4 blocks from every device, and every window receives blocks from some device.
All inputs are finite; a program needn't handle non-finite values.
Results may differ from a plain program's by a relative error of at most 0.029.
Values sent between devices are 32-bit elements; how exact they have to be, the bound alone decides.
No kernel may reach another device: no remote copies, remote signals or barrier semaphores. Data moves between devices by JAX's collectives and lax.ppermute only.
A program may use at most 64 MiB of HBM per device.

v0:
```python
import jax
import jax.numpy as jnp
from jax import lax
from jax.sharding import PartitionSpec as P

KNOTS_W = 128
SRC_DEV = 4096
ITERS = 8


KNOT_PRIOR = 1.0
SOURCE_PRIOR = 1.0
PRECISE = lax.Precision.HIGHEST
PAIR_LIST = [(first, second) for first in range(5) for second in range(first, 5)]


def spline_basis(phase_values):
    square = phase_values * phase_values
    third_power = square * phase_values
    remain = 1.0 - phase_values
    return jnp.stack(
        [
            remain * remain * remain / 6.0,
            (3.0 * third_power - 6.0 * square + 4.0) / 6.0,
            (-3.0 * third_power + 3.0 * square + 3.0 * phase_values + 1.0) / 6.0,
            third_power / 6.0,
        ],
        axis=-2,
    )


def design_rows(phase_values, partial_values):
    spline = spline_basis(phase_values)
    new_shape = spline.shape[:-2] + (16, spline.shape[-1])
    return (spline[..., :, None, :] * partial_values[..., None, :, :]).reshape(new_shape)


def block_normals(design, resid_values):
    grams = jnp.einsum("...ar,...br->...ab", design, design, precision=PRECISE)
    right_side = jnp.einsum("...ar,...r->...a", design, resid_values, precision=PRECISE)
    return (grams.reshape(grams.shape[:-2] + (256,)), right_side)


def spread_knots(values_in):
    summed = None
    for offset in range(4):
        piece_part = values_in[..., 4 * offset : 4 * offset + 4, :]
        widths = [(0, 0)] * (piece_part.ndim - 1) + [(offset, 3 - offset)]
        padded = jnp.pad(piece_part, widths)
        summed = padded if summed is None else summed + padded
    return summed


def apply_normal(gram_bins, vector):
    bin_count = gram_bins.shape[-1]
    gathered = jnp.concatenate(
        [vector[..., :, offset : offset + bin_count] for offset in range(4)], axis=-2
    )
    blocks = gram_bins.reshape(gram_bins.shape[:-2] + (16, 16, bin_count))
    product = jnp.sum(blocks * gathered[..., None, :, :], axis=-2)
    return KNOT_PRIOR * vector + spread_knots(product)


def solve_window(gram_bins, right_bins):
    right_side = spread_knots(right_bins)
    estimate = jnp.zeros_like(right_side)
    residual = right_side
    direction = right_side
    norm_now = jnp.sum(residual * residual, axis=(-2, -1), keepdims=True)
    for iteration in range(ITERS):
        applied = apply_normal(gram_bins, direction)
        step_size = norm_now / jnp.sum(direction * applied, axis=(-2, -1), keepdims=True)
        estimate = estimate + step_size * direction
        residual = residual - step_size * applied
        norm_next = jnp.sum(residual * residual, axis=(-2, -1), keepdims=True)
        direction = residual + norm_next / norm_now * direction
        norm_now = norm_next
    return estimate


def pick_knots(chosen, local_bin):
    knot_index = local_bin[:, None] + jnp.arange(4, dtype=jnp.int32)[None, :]
    knot_index = jnp.broadcast_to(knot_index[:, None, :], (local_bin.shape[0], 4, 4))
    picked = jnp.take_along_axis(chosen, knot_index, axis=2)
    return jnp.transpose(picked, (0, 2, 1)).reshape(local_bin.shape[0], 16)


def source_terms(gain_masked, corrected):
    columns = [gain_masked[:, pair[0]] * gain_masked[:, pair[1]] for pair in PAIR_LIST]
    columns = columns + [gain_masked[:, param] * corrected for param in range(5)]
    return jnp.stack(columns, axis=-1).reshape(-1, 20)


def solve_five(matrix, right_side):
    entries = {}
    for position, pair in enumerate(PAIR_LIST):
        diagonal_add = SOURCE_PRIOR if pair[0] == pair[1] else 0.0
        entries[pair] = matrix[position] + diagonal_add
    lower_part = {}
    for column in range(5):
        pivot_value = entries[column, column]
        for earlier in range(column):
            pivot_value = pivot_value - lower_part[column, earlier] * lower_part[column, earlier]
        lower_part[column, column] = jnp.sqrt(pivot_value)
        for row_at in range(column + 1, 5):
            running = entries[column, row_at]
            for earlier in range(column):
                running = running - lower_part[row_at, earlier] * lower_part[column, earlier]
            lower_part[row_at, column] = running / lower_part[column, column]
    forward = []
    for row_at in range(5):
        running = right_side[row_at]
        for earlier in range(row_at):
            running = running - lower_part[row_at, earlier] * forward[earlier]
        forward.append(running / lower_part[row_at, row_at])
    backward = [None] * 5
    for row_at in reversed(range(5)):
        running = forward[row_at]
        for later in range(row_at + 1, 5):
            running = running - lower_part[later, row_at] * backward[later]
        backward[row_at] = running / lower_part[row_at, row_at]
    return jnp.stack(backward, axis=0)


def route_out(floats, bin_ids, windows, capacity):
    trailing = floats.shape[1:]
    moved_floats, moved_bins = (
        lax.all_to_all(
            floats.reshape((windows, capacity) + trailing),
            ("src", "win"),
            split_axis=0,
            concat_axis=0,
            tiled=True,
        ),
        lax.all_to_all(
            bin_ids.reshape(windows, capacity),
            ("src", "win"),
            split_axis=0,
            concat_axis=0,
            tiled=True,
        ),
    )
    return (
        moved_floats.reshape((windows * capacity,) + trailing),
        moved_bins.reshape(windows * capacity),
    )


def local(block_bin, block_rows, row_source, obs_resid, obs_phase, att_partial, src_partial):
    block_count, row_width = obs_resid.shape
    windows = lax.axis_size(("src", "win"))
    capacity = max(2, 2 * block_count // windows)
    bins_window = KNOTS_W - 3
    slot_count = windows * capacity
    position = lax.broadcasted_iota(jnp.int32, (block_count, row_width), 1)
    mask_rows = (position < block_rows[:, None]).astype(jnp.float32)
    resid_masked = obs_resid * mask_rows
    partial_masked = att_partial * mask_rows[:, None, :]
    window_of = block_bin // bins_window
    local_bin = block_bin % bins_window
    owner_table = (window_of[:, None] == jnp.arange(windows, dtype=jnp.int32)[None, :]).astype(
        jnp.int32
    )
    slot_rank = jnp.sum((jnp.cumsum(owner_table, axis=0) - owner_table) * owner_table, axis=1)
    slot_of = window_of * capacity + slot_rank
    bin_buffer = jnp.zeros((slot_count,), jnp.int32).at[slot_of].set(local_bin)
    local_design = None
    local_design = design_rows(obs_phase, partial_masked)
    grams, right_side = block_normals(local_design, resid_masked)
    packed = jnp.concatenate([grams, right_side], axis=1)
    send_buffer = jnp.zeros((slot_count, 272), jnp.float32).at[slot_of].set(packed)
    got_floats, got_bins = route_out(send_buffer, bin_buffer, windows, capacity)
    got_grams = got_floats[:, :256]
    got_right = got_floats[:, 256:]
    bin_table = (got_bins[:, None] == jnp.arange(bins_window, dtype=jnp.int32)[None, :]).astype(
        jnp.float32
    )
    gram_part = jnp.dot(got_grams.T, bin_table, precision=PRECISE)
    right_part = jnp.dot(got_right.T, bin_table, precision=PRECISE)
    gram_bins, right_bins = lax.psum((gram_part, right_part), "ccd")
    attitude = solve_window(gram_bins, right_bins)
    every_window = lax.all_gather(attitude[None], ("src", "win"), axis=0, tiled=True)
    knots = pick_knots(every_window[window_of], local_bin)
    correction = jnp.sum(local_design * knots[:, :, None], axis=1)
    corrected = (obs_resid - correction) * mask_rows
    terms = source_terms(src_partial * mask_rows[:, None, :], corrected)
    source_part = jax.ops.segment_sum(terms, row_source.reshape(-1), num_segments=SRC_DEV)
    matrix_sum, source_right = lax.psum((source_part[:, :15].T, source_part[:, 15:].T), "ccd")
    source_delta = solve_five(matrix_sum, source_right)
    return (attitude[None], source_delta)


def solution(mesh):
    return jax.shard_map(
        local,
        mesh=mesh,
        in_specs=(
            P(("src", "win", "ccd")),
            P(("src", "win", "ccd")),
            P(("src", "win", "ccd"), None),
            P(("src", "win", "ccd"), None),
            P(("src", "win", "ccd"), None),
            P(("src", "win", "ccd"), None, None),
            P(("src", "win", "ccd"), None, None),
        ),
        out_specs=(P(("src", "win"), None, None), P(None, ("src", "win"))),
        check_vma=False,
    )
```

profile of v0, /device:TPU:1, one launch (start us, length us, event | category | flops | bytes accessed | tf_op | source)
XLA Modules:
  0.0 418.4 jit_solution(1503704204172414065)
XLA Ops:
  7.2 0.7 compare_select_fusion
  8.3 1.0 scatter_custom_fusion.1
  9.3 0.7 all_to_all.10
  10.0 13.2 %all-to-all-start.1 = ((s32[64,1,4]{2,1,0:T(1,128)}), s32[64,1,4]{2,1,0:T(1,128)S(1)}, u32[]{:S(2)}, u32[]{:S(2)}) async-start(s32[64,1,4]{2,1,0:T(1,128)} %bitcast.9), calls=%async_computation.1 | async-start | bytes 65536 | tf_op jit(solution)/shard_map/all_to_all | solution.py:135
  23.2 0.7 fusion.23
  23.9 0.9 fusion.22
  24.9 1.0 broadcast_multiply_fusion.2
  25.9 1.0 broadcast_multiply_fusion.1
  26.9 0.9 fusion.19
  28.0 0.3 broadcast_multiply_fusion
  28.3 1.7 fusion.82
  30.0 1.7 fusion.83
  31.8 0.4 copy.71
  32.8 0.3 reshape.417
  33.2 1.1 scatter_custom_fusion
  34.3 0.8 reshape.406
  35.2 10.3 %all-to-all-start = ((f32[64,4,272]{2,1,0:T(4,128)}), f32[64,4,272]{2,1,0:T(4,128)S(1)}, u32[]{:S(2)}, u32[]{:S(2)}) async-start(f32[64,4,272]{2,1,0:T(4,128)} %reshape.406), calls=%async_computation | async-start | bytes 786432 | tf_op jit(solution)/shard_map/all_to_all | solution.py:128
  45.6 0.5 broadcast.311
  46.1 0.7 reduce.4
  47.0 13.1 %all-to-all-done = f32[64,4,272]{2,1,0:T(4,128)S(1)} async-done(((f32[64,4,272]{2,1,0:T(4,128)}), f32[64,4,272]{2,1,0:T(4,128)S(1)}, u32[]{:S(2)}, u32[]{:S(2)}) %all-to-all-start) | async-done | bytes 278560 | tf_op jit(solution)/shard_map/all_to_all | solution.py:128
  60.2 0.3 fusion.7
  60.5 1.1 fusion.2
  61.6 8.5 %psum.28 = f32[16,125]{1,0:T(8,128)S(1)} all-reduce(f32[16,125]{1,0:T(8,128)S(1)} %fusion.7), channel_id=1, replica_groups=mesh['src'=16,'win'=4,'ccd'=4] {'ccd'}, use_global_device_ids=true, to_apply=%region_4.5 | all-reduce | flops 2000 | bytes 16000 | tf_op jit(solution)/shard_map/psum | solution.py:180
  70.5 40.6 %all-reduce.40.cloned.1.call-done = f32[16,16,125]{2,1,0:T(8,128)} async-done(((f32[16,16,125]{2,1,0:T(8,128)}), f32[16,16,125]{2,1,0:T(8,128)}) %all-reduce.40.cloned.1.call-update) | async-done | bytes 128016 | tf_op jit(solution)/shard_map/psum | solution.py:180
  111.1 0.9 multiply_reduce_fusion.8
  112.1 0.7 multiply_reduce_fusion.22
  114.1 0.6 multiply_reduce_fusion.21
  116.1 0.9 multiply_reduce_fusion.7
  117.1 0.7 multiply_reduce_fusion.20
  119.1 0.6 multiply_reduce_fusion.19
  121.1 0.9 multiply_reduce_fusion.6
  122.1 0.7 multiply_reduce_fusion.18
  124.1 0.6 multiply_reduce_fusion.17
  126.1 0.9 multiply_reduce_fusion.5
  127.1 0.7 multiply_reduce_fusion.16
  129.1 0.6 multiply_reduce_fusion.15
  131.1 0.9 multiply_reduce_fusion.4
  132.1 0.7 multiply_reduce_fusion.14
  134.1 0.6 multiply_reduce_fusion.13
  136.2 0.9 multiply_reduce_fusion.3
  137.1 0.7 multiply_reduce_fusion.12
  139.1 0.6 multiply_reduce_fusion.11
  141.2 0.9 multiply_reduce_fusion.2
  142.1 0.7 multiply_reduce_fusion.10
  144.1 0.6 multiply_reduce_fusion.9
  146.2 0.9 multiply_reduce_fusion.1
  147.1 0.7 fusion.53
  149.2 87.0 %all-gather.1 = f32[64,4,128]{2,1,0:T(4,128)S(1)} all-gather(f32[1,4,128]{2,1,0:T(4,128)S(1)} %add_bitcast_fusion), channel_id=2, replica_groups=mesh['src'=16,'win'=4,'ccd'=4] {'src','win'}, dimensions={0}, use_global_device_ids=true | all-gather | bytes 133120 | tf_op jit(solution)/shard_map/all_gather | solution.py:182
  236.2 0.8 gather_fusion
  236.9 18.7 %gather_fusion.1 = f32[2048]{0:T(1024)S(1)} fusion(f32[128,4,128]{2,1,0:T(4,128)S(1)} %gather_fusion, s32[2048]{0:T(1024)S(1)} %reshape.417), kind=kCustom, calls=%fused_computation.1 | custom fusion | bytes 40960 | tf_op jit(solution)/shard_map/jit(take_along_axis)/gather | solution.py:84
  255.7 0.3 reshape.420
  256.2 0.9 copy.78
  257.1 0.8 multiply_reduce_fusion
  258.0 2.1 stack.66
  260.2 4.7 %copy.79 = f32[16384,20]{1,0:T(8,128)} copy(f32[16384,20]{0,1:T(8,128)S(1)} %stack.66) | data formatting | bytes 2621440 | tf_op jit(solution)/shard_map/stack | solution.py:91
  264.8 88.1 %scatter_custom_fusion.2 = f32[4096,20]{1,0:T(8,128)S(1)} fusion(s32[16384]{0:T(1024)} %bitcast.91, f32[16384,20]{1,0:T(8,128)} %copy.79, f32[]{:T(128)} %constant.32.clone.1), kind=kCustom, calls=%fused_computation.6 | custom fusion | flops 327680 | bytes 328192 | tf_op jit(solution)/shard_map/scatter-add | solution.py:187
  352.9 2.0 slice.466
  354.9 1.3 copy.85
  356.2 2.9 copy.84
  359.1 46.1 %all-reduce.42.cloned.1.call-done = (f32[15,4096]{1,0:T(8,128)}, f32[5,4096]{1,0:T(8,128)}) async-done(((f32[15,4096]{1,0:T(8,128)}, f32[5,4096]{1,0:T(8,128)}), (f32[15,4096]{1,0:T(8,128)}, f32[5,4096]{1,0:T(8,128)})) %all-reduce.42.cloned.1.call-update) | async-done | bytes 327696 | tf_op jit(solution)/shard_map/psum | solution.py:188
  405.2 2.1 fusion.51
  407.3 1.8 fusion.52
  409.1 1.7 subtract_divide_fusion
  410.8 0.8 stack.67
  (69 shorter events, 3.0 us)
Async XLA Ops:
  10.0 25.2 %all-to-all-start.1 = ((s32[64,1,4]{2,1,0:T(1,128)}), s32[64,1,4]{2,1,0:T(1,128)S(1)}, u32[]{:S(2)}, u32[]{:S(2)}) async-start(s32[64,1,4]{2,1,0:T(1,128)} %bitcast.9), calls=%async_computation.1 | async-start | bytes 65536 | tf_op jit(solution)/shard_map/all_to_all | solution.py:135
  35.2 24.9 %all-to-all-start = ((f32[64,4,272]{2,1,0:T(4,128)}), f32[64,4,272]{2,1,0:T(4,128)S(1)}, u32[]{:S(2)}, u32[]{:S(2)}) async-start(f32[64,4,272]{2,1,0:T(4,128)} %reshape.406), calls=%async_computation | async-start | bytes 786432 | tf_op jit(solution)/shard_map/all_to_all | solution.py:128
  45.5 65.6 %all-reduce.40.cloned.1.call-start = ((), (), s32[]{:S(2)}) async-start(), calls=%async_computation.2 | async-start | bytes 262144 | tf_op jit(solution)/shard_map/psum | solution.py:180
  70.2 335.0 %all-reduce.42.cloned.1.call-start = ((), (), s32[]{:S(2)}) async-start(), calls=%async_computation.3 | async-start | bytes 786432 | tf_op jit(solution)/shard_map/psum | solution.py:188
  149.2 106.5 %copy-start.1 = (f32[1,4,128]{2,1,0:T(4,128)}, f32[1,4,128]{2,1,0:T(4,128)S(1)}, u32[]{:S(2)}) copy-start(f32[1,4,128]{2,1,0:T(4,128)S(1)} %add_bitcast_fusion) | copy-start | bytes 6148
  255.7 2.2 copy-start
  255.7 2.2 copy-start.2
Sparse Core Ops, SparseCore 0:
  70.4 40.6 all-reduce.39
  359.3 45.8 all-reduce.41
where the time goes:
time: 421 us; the launch traced here: 418 us
  other arithmetic  119 us (28%)
  waiting for transfers between devices  99.9 us (24%)
  blocking collectives  95.6 us (23%)
  local copies, waits for them, and re-layouts  41.1 us (10%)
  between operations  34.6 us (8%)
  starting transfers between devices  23.5 us (6%)
  matrix products  4.89 us (1%)
    scatter-add x1, other arithmetic, local(): jax.ops.segment_sum(terms, row_source.reshape(-1), num_segments=SRC_DEV)  88.1 us
    all_gather x1, blocking collectives, local(): lax.all_gather(attitude[None], ('src', 'win'), axis=0, tiled=True)  87 us
    psum x1, waiting for transfers between devices, local(): lax.psum((source_part[:, :15].T, source_part[:, 15:].T), 'ccd')  46.1 us
    psum x1, waiting for transfers between devices, local(): gram_bins, right_bins = lax.psum((gram_part, right_part), 'ccd')  40.6 us
    gather x4, local copies, waits for them, and re-layouts, pick_knots(): picked = jnp.take_along_axis(chosen, knot_index, axis=2)  19.5 us
    all_to_all x1, starting transfers between devices, route_out(): lax.all_to_all(bin_ids.reshape(windows, capacity), ('src', 'win'), split_...  13.2 us
    all_to_all x1, waiting for transfers between devices, route_out(): lax.all_to_all(floats.reshape((windows, capacity) + trailing), ('src', 'w...  13.1 us
    all_to_all x1, starting transfers between devices, route_out(): lax.all_to_all(floats.reshape((windows, capacity) + trailing), ('src', 'w...  10.3 us
  transfers between devices with their start and end apart: 4, of which 3 were waited for; matrix products, arithmetic and copies ran while one was open for 3% of the time, Pallas kernels for 0%

commit v1 on v0

v1 whole, which is shorter than its diff:
```python
import functools
import math

import jax
import jax.numpy as jnp
import numpy as np
from jax import lax
from jax.experimental import pallas as pl
from jax.experimental.pallas import tpu as pltpu
from jax.sharding import PartitionSpec as P

KNOTS_W = 128
BINS_W = 125
NBLK = 128
ROWS = 128
WINDOWS = 64
CAP = 4
SLOTS = WINDOWS * CAP
SRC_DEV = 4096
ITERS = 8
N_CCD = 4
HIGH = 16
LOW = 256
STEP_BLOCKS = 16

KNOT_PRIOR = 1.0
SOURCE_PRIOR = 1.0
PAIR_LIST = [(first, second) for first in range(5) for second in range(first, 5)]
ATT_PAIRS = [(first, second) for first in range(4) for second in range(first, 4)]
RHS_AT = 70
BIN_AT = 86
FEATS = 88

F32 = jnp.float32
BF16 = jnp.bfloat16
NT = (((1,), (1,)), ((), ()))
NN = (((1,), (0,)), ((), ()))

SPLINE = np.array([[1, 0, 0, 0], [4, 12, 6, 1], [1, 6, 12, 4], [0, 0, 0, 1]], np.float64) / 6.0


def knot_matrix():
    pair_at = {}
    for at, (first, second) in enumerate(ATT_PAIRS):
        pair_at[first, second] = pair_at[second, first] = at
    table = np.zeros((120, 4 * FEATS), np.float64)
    for d in range(-3, 4):
        for p in range(4):
            for q in range(4):
                row = ((d + 3) * 4 + p) * 4 + q
                for l in range(4):
                    j = l - d
                    if 0 <= j < 4:
                        for m, value in enumerate(np.convolve(SPLINE[j], SPLINE[l])):
                            table[row, l * FEATS + m * 10 + pair_at[q, p]] += value
    for q in range(4):
        for j in range(4):
            table[112 + q, j * FEATS + RHS_AT + 4 * j + q] = 1.0
            table[116 + q, j * FEATS + RHS_AT + 4 * j + q] = 1.0
    return table.astype(np.float32)


def split_parts(values, count):
    parts = []
    for at in range(count):
        part = values.astype(BF16)
        parts.append(part)
        if at + 1 < count:
            values = values - part.astype(F32)
    return parts


def exact_dot(values, ones, dims, swap=False):
    total = None
    for part in split_parts(values, 3):
        pair = (ones, part) if swap else (part, ones)
        piece = lax.dot_general(*pair, dims, preferred_element_type=F32)
        total = piece if total is None else total + piece
    return total


def indicator(condition):
    return jnp.where(condition, 1.0, 0.0).astype(BF16)


def iota(shape, axis):
    return lax.broadcasted_iota(jnp.int32, shape, axis)


def iota_f(shape, axis):
    return iota(shape, axis).astype(F32)


def normals_kernel(bin_ref, rows_ref, resid_ref, phase_ref, att_ref, send_ref, obs_ref, slot_ref, pay_ref):
    square = (NBLK, NBLK)
    bins = bin_ref[...].astype(F32)
    window = jnp.floor((bins + 0.5) * (1.0 / BINS_W))
    local_bin = bins - BINS_W * window
    mask = iota(square, 0) < rows_ref[...]
    u = phase_ref[...].T
    resid = jnp.where(mask, resid_ref[...].T, 0.0)
    att = [jnp.where(mask, att_ref[pl.ds(q, NBLK, stride=4), :].T, 0.0) for q in range(4)]
    obs_ref[0:128, :] = u
    obs_ref[128:256, :] = resid
    for q in range(4):
        obs_ref[256 + 128 * q : 384 + 128 * q, :] = att[q]
    v = 1.0 - u
    u2, v2 = u * u, v * v
    u3, v3 = u2 * u, v2 * v
    cubes = [v3, u * v2, u2 * v, u3]
    powers = [v3 * v3, u * v2 * v3, u2 * v2 * v2, u3 * v3, u2 * u2 * v2, u3 * u2 * v, u3 * u3]
    for at, (first, second) in enumerate(ATT_PAIRS):
        product = att[first] * att[second]
        for m in range(7):
            row = m * 10 + at
            pay_ref[row : row + 1, :] = jnp.sum(powers[m] * product, axis=0, keepdims=True)
    for q in range(4):
        product = att[q] * resid
        sums = [jnp.sum(cubes[i] * product, axis=0, keepdims=True) for i in range(4)]
        for j in range(4):
            total = None
            for i in range(4):
                if SPLINE[j, i] != 0.0:
                    piece = float(SPLINE[j, i]) * sums[i]
                    total = piece if total is None else total + piece
            row = RHS_AT + 4 * j + q
            pay_ref[row : row + 1, :] = total
    pay_ref[BIN_AT : BIN_AT + 1, :] = local_bin
    pay_ref[BIN_AT + 1 :, :] = jnp.zeros((NBLK - BIN_AT - 1, NBLK), F32)
    window_column = jnp.broadcast_to(window, square).T
    earlier = jnp.where(window_column == window, 1.0, 0.0) * jnp.where(iota(square, 0) < iota(square, 1), 1.0, 0.0)
    rank = jnp.sum(earlier, axis=0, keepdims=True)
    slot_ref[...] = jnp.concatenate([window, rank, jnp.zeros((6, NBLK), F32)], axis=0)
    place = indicator(iota_f((SLOTS, NBLK), 0) == CAP * window + rank)
    send_ref[...] = exact_dot(pay_ref[...], place, NT, swap=True)


def bins_kernel(got_ref, out_ref):
    got = got_ref[...].T
    place = indicator(iota_f((KNOTS_W, SLOTS), 0) == got[BIN_AT : BIN_AT + 1, :])
    out_ref[...] = exact_dot(got[:FEATS], place, NT)


def attitude_kernel(own_ref, one_ref, two_ref, three_ref, got_ref, table_ref, att_ref, reply_ref):
    total = (own_ref[...] + two_ref[...]) + (one_ref[...] + three_ref[...])
    moved = jnp.concatenate([total] + [pltpu.roll(total, l, 1) for l in range(1, 4)], axis=0)
    band = lax.dot_general(table_ref[...], moved, NN, precision=lax.Precision.HIGHEST, preferred_element_type=F32)
    groups = [band[8 * at : 8 * at + 8] for at in range(14)]
    lower_half = iota((8, KNOTS_W), 0) < 4

    def doubled(values):
        return values + pltpu.roll(values, 4, 0)

    def norm(values):
        return jnp.sum(jnp.sum(values, axis=1, keepdims=True), axis=0, keepdims=True)

    def apply(vector):
        spread = [
            jnp.where(lower_half, vector[2 * at : 2 * at + 1, :], vector[2 * at + 1 : 2 * at + 2, :]) for at in range(2)
        ]
        result = None
        for d in range(-3, 4):
            piece = groups[2 * (d + 3)] * spread[0] + groups[2 * (d + 3) + 1] * spread[1]
            if d:
                piece = pltpu.roll(piece, -d % KNOTS_W, 1)
            result = piece if result is None else result + piece
        return KNOT_PRIOR * vector + doubled(result)

    residual = band[112:120]
    direction = residual
    estimate = jnp.zeros_like(residual)
    norm_now = norm(residual * residual)
    for _ in range(ITERS):
        applied = apply(direction)
        step_size = norm_now / norm(direction * applied)
        estimate = estimate + step_size * direction
        residual = residual - step_size * applied
        norm_next = norm(residual * residual)
        direction = residual + norm_next / norm_now * direction
        norm_now = norm_next
    att_ref[0] = estimate[:4]
    moved = jnp.concatenate([estimate[:4]] + [pltpu.roll(estimate, KNOTS_W - j, 1)[:4] for j in range(1, 4)], axis=0)
    column = jnp.concatenate(
        [got_ref[pl.ds(s, WINDOWS, stride=CAP), :][:, BIN_AT : BIN_AT + 1] for s in range(CAP)], axis=0
    )
    place = indicator(iota_f((SLOTS, KNOTS_W), 1) == column)
    knots = exact_dot(moved, place, NT, swap=True)
    reply_ref[...] = jnp.zeros((WINDOWS, 128), F32)
    for s in range(CAP):
        reply_ref[:, 16 * s : 16 * s + 16] = knots[WINDOWS * s : WINDOWS * s + WINDOWS]


def source_sums(count, terms_ref, high_ref, low_ref, a_ref, b_ref, acc_ref):
    high_at = iota_f((HIGH, ROWS), 0)
    low_at = iota_f((LOW, ROWS), 0).astype(BF16)
    acc_ref[...] = jnp.zeros(acc_ref.shape, F32)

    def step(at, carry):
        for inner in range(STEP_BLOCKS):
            block = at * STEP_BLOCKS + inner
            lanes = slice(inner * ROWS, inner * ROWS + ROWS)
            here = high_at == high_ref[pl.ds(block, 1), :]
            low = jnp.broadcast_to(low_ref[pl.ds(block, 1), :], (HIGH, ROWS)).astype(BF16)
            low = jnp.concatenate([low] * (LOW // HIGH), axis=0)
            b_ref[:, lanes] = jnp.where(low_at == low, jnp.ones((), BF16), jnp.zeros((), BF16))
            for c in range(2 * count):
                term = jnp.where(here, terms_ref[pl.ds(c * NBLK + block, 1), :], 0.0)
                a_ref[c * HIGH : (c + 1) * HIGH, lanes] = term.astype(BF16)
        acc_ref[...] += lax.dot_general(a_ref[...], b_ref[...], NT, preferred_element_type=F32)
        return carry

    lax.fori_loop(0, NBLK // STEP_BLOCKS, step, 0)


def put_terms(terms_ref, c, values):
    large = values.astype(BF16).astype(F32)
    terms_ref[2 * c * NBLK : (2 * c + 1) * NBLK, :] = large
    terms_ref[(2 * c + 1) * NBLK : (2 * c + 2) * NBLK, :] = values - large


def put_sources(source_ref, high_ref, low_ref):
    source = source_ref[...]
    high = source >> 8
    high_ref[...] = high.astype(F32)
    low_ref[...] = (source - (high << 8)).astype(F32)


def source_normals_kernel(rows_ref, source_ref, gain_ref, out_ref, terms_ref, high_ref, low_ref, a_ref, b_ref, acc_ref):
    square = (NBLK, ROWS)
    used = jnp.broadcast_to(rows_ref[...].astype(F32), square).T
    mask = iota_f(square, 1) < used
    put_sources(source_ref, high_ref, low_ref)
    gains = [jnp.where(mask, gain_ref[NBLK * p : NBLK * p + NBLK, :], 0.0) for p in range(5)]
    for at, (first, second) in enumerate(PAIR_LIST):
        put_terms(terms_ref, at, gains[first] * gains[second])
    source_sums(15, terms_ref, high_ref, low_ref, a_ref, b_ref, acc_ref)
    for c in range(15):
        out_ref[HIGH * c : HIGH * c + HIGH, :] = (
            acc_ref[2 * c * HIGH : (2 * c + 1) * HIGH, :] + acc_ref[(2 * c + 1) * HIGH : (2 * c + 2) * HIGH, :]
        )


def source_right_kernel(
    reply_ref, slot_ref, obs_ref, source_ref, gain_ref, out_ref, terms_ref, high_ref, low_ref, a_ref, b_ref, acc_ref
):
    put_sources(source_ref, high_ref, low_ref)
    place = indicator(iota_f((WINDOWS, NBLK), 0) == slot_ref[0:1, :])
    rank = slot_ref[1:2, :]
    spread = exact_dot(reply_ref[...].T, place, NN)
    knots = None
    for s in range(CAP):
        piece = jnp.where(rank == float(s), spread[16 * s : 16 * s + 16, :], 0.0)
        knots = piece if knots is None else knots + piece
    u = obs_ref[0:128, :]
    att = [obs_ref[256 + 128 * q : 384 + 128 * q, :] for q in range(4)]
    v = 1.0 - u
    u2, v2 = u * u, v * v
    cubes = [v2 * v, u * v2, u2 * v, u2 * u]
    values = obs_ref[128:256, :]
    for j in range(4):
        spline = None
        for i in range(4):
            if SPLINE[j, i] != 0.0:
                piece = float(SPLINE[j, i]) * cubes[i]
                spline = piece if spline is None else spline + piece
        inner = None
        for q in range(4):
            piece = att[q] * knots[4 * j + q : 4 * j + q + 1, :]
            inner = piece if inner is None else inner + piece
        values = values - spline * inner
    values = values.T
    for p in range(5):
        put_terms(terms_ref, p, gain_ref[NBLK * p : NBLK * p + NBLK, :] * values)
    source_sums(5, terms_ref, high_ref, low_ref, a_ref, b_ref, acc_ref)
    for c in range(5):
        out_ref[HIGH * c : HIGH * c + HIGH, :] = (
            acc_ref[2 * c * HIGH : (2 * c + 1) * HIGH, :] + acc_ref[(2 * c + 1) * HIGH : (2 * c + 2) * HIGH, :]
        )


def factor_kernel(own_ref, one_ref, two_ref, three_ref, out_ref):
    entries = {}
    for at, pair in enumerate(PAIR_LIST):
        rows = slice(HIGH * at, HIGH * at + HIGH)
        total = (own_ref[rows, :] + two_ref[rows, :]) + (one_ref[rows, :] + three_ref[rows, :])
        entries[pair] = total + SOURCE_PRIOR if pair[0] == pair[1] else total
    lower = {}
    for column in range(5):
        pivot = entries[column, column]
        for before in range(column):
            pivot = pivot - lower[column, before] * lower[column, before]
        inverse = 1.0 / jnp.sqrt(pivot)
        lower[column, column] = inverse
        for row in range(column + 1, 5):
            running = entries[column, row]
            for before in range(column):
                running = running - lower[row, before] * lower[column, before]
            lower[row, column] = running * inverse
    for at, (first, second) in enumerate(PAIR_LIST):
        out_ref[HIGH * at : HIGH * at + HIGH, :] = lower[second, first]


def solve_kernel(factor_ref, own_ref, one_ref, two_ref, three_ref, out_ref):
    lower = {}
    for at, (first, second) in enumerate(PAIR_LIST):
        lower[second, first] = factor_ref[HIGH * at : HIGH * at + HIGH, :]
    values = []
    for row in range(5):
        rows = slice(HIGH * row, HIGH * row + HIGH)
        running = (own_ref[rows, :] + two_ref[rows, :]) + (one_ref[rows, :] + three_ref[rows, :])
        for before in range(row):
            running = running - lower[row, before] * values[before]
        values.append(running * lower[row, row])
    for row in reversed(range(5)):
        running = values[row]
        for later in range(row + 1, 5):
            running = running - lower[later, row] * values[later]
        values[row] = running * lower[row, row]
    for row in range(5):
        for high in range(HIGH):
            out_ref[row : row + 1, LOW * high : LOW * high + LOW] = values[row][high : high + 1, :]


def f32(*shape):
    return jax.ShapeDtypeStruct(shape, F32)


def kernel_call(body, name, outs, *args, scratch=(), flops=1_000_000):
    size = sum(math.prod(a.shape) * 4 for a in args)
    return pl.pallas_call(
        body,
        out_shape=outs,
        scratch_shapes=list(scratch),
        compiler_params=pltpu.CompilerParams(vmem_limit_bytes=32 * 1024 * 1024),
        cost_estimate=pl.CostEstimate(flops=flops, bytes_accessed=size, transcendentals=0),
        name=name,
    )(*args)


def segment_scratch(count):
    return (
        pltpu.VMEM((2 * count * NBLK, ROWS), F32),
        pltpu.VMEM((NBLK, ROWS), F32),
        pltpu.VMEM((NBLK, ROWS), F32),
        pltpu.VMEM((2 * count * HIGH, STEP_BLOCKS * ROWS), BF16),
        pltpu.VMEM((LOW, STEP_BLOCKS * ROWS), BF16),
        pltpu.VMEM((2 * count * HIGH, LOW), F32),
    )


def from_others(values):
    return [
        lax.ppermute(values, "ccd", [(at, (at + shift) % N_CCD) for at in range(N_CCD)]) for shift in range(1, N_CCD)
    ]


def to_windows(values):
    return lax.all_to_all(values, ("src", "win"), split_axis=0, concat_axis=0, tiled=True)


def local(block_bin, block_rows, row_source, obs_resid, obs_phase, att_partial, src_partial):
    bins = block_bin.reshape(1, NBLK)
    rows = block_rows.reshape(1, NBLK)
    gains = jnp.transpose(src_partial, (1, 0, 2)).reshape(5 * NBLK, ROWS)
    send, obs, slots = kernel_call(
        normals_kernel,
        "normals",
        (f32(SLOTS, 128), f32(6 * ROWS, NBLK), f32(8, NBLK)),
        bins,
        rows,
        obs_resid,
        obs_phase,
        att_partial.reshape(4 * NBLK, ROWS),
        scratch=(pltpu.VMEM((NBLK, NBLK), F32),),
    )
    got = to_windows(send.reshape(WINDOWS, CAP, 128)).reshape(SLOTS, 128)
    normal = kernel_call(
        source_normals_kernel,
        "source_normals",
        f32(15 * HIGH, LOW),
        rows,
        row_source,
        gains,
        scratch=segment_scratch(15),
        flops=2 * 480 * 256 * 16384,
    )
    moments = kernel_call(bins_kernel, "bins", f32(FEATS, KNOTS_W), got)
    attitude, reply = kernel_call(
        attitude_kernel,
        "attitude",
        (f32(1, 4, KNOTS_W), f32(WINDOWS, 128)),
        moments,
        *from_others(moments),
        got,
        jnp.asarray(knot_matrix()),
    )
    knots = to_windows(reply)
    factors = kernel_call(factor_kernel, "factors", f32(15 * HIGH, LOW), normal, *from_others(normal))
    right = kernel_call(
        source_right_kernel,
        "source_right",
        f32(5 * HIGH, LOW),
        knots,
        slots,
        obs,
        row_source,
        gains,
        scratch=segment_scratch(5),
        flops=2 * 160 * 256 * 16384,
    )
    source_delta = kernel_call(solve_kernel, "solve", f32(5, SRC_DEV), factors, right, *from_others(right))
    return attitude, source_delta


def solution(mesh):
    return jax.shard_map(
        local,
        mesh=mesh,
        in_specs=(
            P(("src", "win", "ccd")),
            P(("src", "win", "ccd")),
            P(("src", "win", "ccd"), None),
            P(("src", "win", "ccd"), None),
            P(("src", "win", "ccd"), None),
            P(("src", "win", "ccd"), None, None),
            P(("src", "win", "ccd"), None, None),
        ),
        out_specs=(P(("src", "win"), None, None), P(None, ("src", "win"))),
        check_vma=False,
    )
```

time: 421 us -> 74.2 us (0.18)
  other arithmetic: 119 us -> 0 us
  blocking collectives: 95.6 us -> 0 us
  waiting for transfers between devices: 99.9 us -> 13.9 us
  local copies, waits for them, and re-layouts: 41.1 us -> 3.3 us
  between operations: 34.6 us -> 0.73 us
  Pallas kernels: 0 us -> 18.1 us
  starting transfers between devices: 23.5 us -> 37.8 us
  matrix products: 4.89 us -> 0 us
    scatter-add x1 -> x0, other arithmetic: 88.1 us -> none  [local(): jax.ops.segment_sum(terms, row_source.reshape(-1), num_segments=SRC_DEV)]
    all_gather x1 -> x0, blocking collectives: 87 us -> none  [local(): lax.all_gather(attitude[None], ('src', 'win'), axis=0, tiled=True)]
    psum x2 -> x0, waiting for transfers between devices: 86.7 us -> none  [the longest x1 46.1 us: local(): lax.psum((source_part[:, :15].T, source_part[:, 15:].T), 'ccd')]
    gather x5 -> x0, local copies, waits for them, and re-layouts: 20.2 us -> none  [the longest x4 19.5 us: pick_knots(): picked = jnp.take_along_axis(chosen, knot_index, axis=2)]
    pallas_call x0 -> x7, Pallas kernels: none -> 18.1 us  [kernel_call(): pl.pallas_call(body, out_shape=outs, scratch_shapes=list(scratch), compil...]
    reduce_sum x25 -> x0, other arithmetic: 18.1 us -> none  [the longest x8 7.49 us: apply_normal(): product = jnp.sum(blocks * gathered[..., None, :, :], axis=-2)]
    ppermute x0 -> x9, starting transfers between devices: none -> 14.4 us  [from_others(): lax.ppermute(values, 'ccd', [(at, (at + shift) % N_CCD) for at in range(N...]
    ppermute x0 -> x9, waiting for transfers between devices: none -> 8.59 us  [from_others(): lax.ppermute(values, 'ccd', [(at, (at + shift) % N_CCD) for at in range(N...]
  transfers between devices with their start and end apart: 4 -> 11, of which waited for: 3 -> 8; matrix products, arithmetic and copies ran while one was open for 3% -> 0% of each run, Pallas kernels for 0% -> 22%
where the time goes in v1:
time: 74.2 us; the launch traced here: 73.8 us
  starting transfers between devices  37.8 us (51%)
  Pallas kernels  18.1 us (24%)
  waiting for transfers between devices  13.9 us (19%)
  local copies, waits for them, and re-layouts  3.3 us (4%)
    all_to_all x2, starting transfers between devices, to_windows(): lax.all_to_all(values, ('src', 'win'), split_axis=0, concat_axis=0, tiled...  23.3 us
    pallas_call x7, Pallas kernels, kernel_call(): pl.pallas_call(body, out_shape=outs, scratch_shapes=list(scratch), compil...  18.1 us
    ppermute x9, starting transfers between devices, from_others(): lax.ppermute(values, 'ccd', [(at, (at + shift) % N_CCD) for at in range(N...  14.4 us
    ppermute x9, waiting for transfers between devices, from_others(): lax.ppermute(values, 'ccd', [(at, (at + shift) % N_CCD) for at in range(N...  8.59 us
    all_to_all x2, waiting for transfers between devices, to_windows(): lax.all_to_all(values, ('src', 'win'), split_axis=0, concat_axis=0, tiled...  5.34 us
    unnamed x16, local copies, waits for them, and re-layouts  3.3 us
  transfers between devices with their start and end apart: 11, of which 8 were waited for; matrix products, arithmetic and copies ran while one was open for 0% of the time, Pallas kernels for 22%

profile of v1, /device:TPU:1, one launch (start us, length us, event | category | flops | bytes accessed | tf_op | source)
XLA Modules:
  0.0 73.8 jit_solution(8732719688357361574)
XLA Ops:
  0.6 0.0 copy-start.4
  0.6 0.0 copy-start.5
  0.7 0.6 copy-done.4
  1.3 0.0 copy-done.5
  1.3 0.0 copy-start
  1.3 0.9 %copy-done = f32[128,4,128]{2,1,0:T(4,128)S(1)} copy-done((f32[128,4,128]{2,1,0:T(4,128)S(1)}, f32[128,4,128]{2,1,0:T(4,128)}, u32[]{:S(2)}) %copy-start) | copy-done | bytes 262168
  2.3 0.0 copy-start.2
  2.3 0.8 %copy-done.2 = f32[128,128]{1,0:T(8,128)S(1)} copy-done((f32[128,128]{1,0:T(8,128)S(1)}, f32[128,128]{1,0:T(8,128)}, u32[]{:S(2)}) %copy-start.2) | copy-done | bytes 65560
  3.1 0.0 copy-start.3
  3.1 0.8 %copy-done.3 = f32[128,128]{1,0:T(8,128)S(1)} copy-done((f32[128,128]{1,0:T(8,128)S(1)}, f32[128,128]{1,0:T(8,128)}, u32[]{:S(2)}) %copy-start.3) | copy-done | bytes 65560
  3.9 0.0 copy-start.6
  3.9 1.5 %normals.1 = (f32[256,128]{1,0:T(8,128)}, f32[768,128]{1,0:T(8,128)S(1)}, f32[8,128]{1,0:T(8,128)S(1)}) custom-call(s32[1,128]{1,0:T(1,128)S(1)} %bitcast.16, s32[1,128]{1,0:T(1,128)S(1)} %bitcast.17, f32[128,128]{1,0:T(8,128)S(1)} %copy-done.2, f32[128,128]{1,0:T(8,128)S(1)} %copy-done.3, f32[512,128]{1,0:T(8,128)S(1)} %bitcast.14), custom_call_target="tpu_custom_call" | custom-call | flops 1000000 | bytes 394240 | tf_op jit(solution)/shard_map/normals/pallas_call | solution.py:330
  5.4 0.0 copy-start.7
  5.4 13.3 %all-to-all-start = ((f32[64,4,128]{2,1,0:T(4,128)}), f32[64,4,128]{2,1,0:T(4,128)S(1)}, u32[]{:S(2)}, u32[]{:S(2)}) async-start(f32[64,4,128]{2,1,0:T(4,128)} %bitcast.3), calls=%async_computation | async-start | bytes 262144 | tf_op jit(solution)/shard_map/all_to_all | solution.py:358
  18.7 0.0 copy-done.6
  18.7 0.0 copy-done.7
  18.8 0.0 copy-start.1
  18.8 7.0 %source_normals.1.own_ref = f32[240,256]{1,0:T(8,128)S(1)} custom-call(s32[1,128]{1,0:T(1,128)S(1)} %bitcast.18, s32[128,128]{1,0:T(8,128)S(1)} %copy-done.7, f32[640,128]{1,0:T(8,128)S(1)} %bitcast.19), custom_call_target="tpu_custom_call" | custom-call | flops 4026531840 | bytes 393728 | tf_op jit(solution)/shard_map/source_normals/pallas_call | solution.py:330
  25.8 2.6 %collective-permute-start.5 = (f32[240,256]{1,0:T(8,128)S(1)}, f32[240,256]{1,0:T(8,128)S(1)}, u32[]{:S(2)}, u32[]{:S(2)}) collective-permute-start(f32[240,256]{1,0:T(8,128)S(1)} %source_normals.1.own_ref), channel_id=1, source_target_pairs={{0,3},{1,0},{2,1},{3,2},{4,7},{5,4},{6,5},{7,6},{8,11},{9,8},{10,9... | collective-permute-start | bytes 737288 | tf_op jit(solution)/shard_map/ppermute | solution.py:353
  28.4 0.3 all-to-all-done
  28.7 0.3 bins.1.own_ref
  28.9 2.6 %collective-permute-start.2 = (f32[88,128]{1,0:T(8,128)S(1)}, f32[88,128]{1,0:T(8,128)S(1)}, u32[]{:S(2)}, u32[]{:S(2)}) collective-permute-start(f32[88,128]{1,0:T(8,128)S(1)} %bins.1.own_ref), channel_id=1, source_target_pairs={{0,3},{1,0},{2,1},{3,2},{4,7},{5,4},{6,5},{7,6},{8,11},{9,8},{10,9... | collective-permute-start | bytes 135176 | tf_op jit(solution)/shard_map/ppermute | solution.py:353
  31.5 0.5 collective-permute-start.1
  32.0 0.6 collective-permute-start
  32.6 1.9 %collective-permute-done.2.three_ref = f32[88,128]{1,0:T(8,128)S(1)} collective-permute-done((f32[88,128]{1,0:T(8,128)S(1)}, f32[88,128]{1,0:T(8,128)S(1)}, u32[]{:S(2)}, u32[]{:S(2)}) %collective-permute-start.2) | collective-permute-done | bytes 45088 | tf_op jit(solution)/shard_map/ppermute | solution.py:353
  34.5 1.4 %collective-permute-done.1.two_ref = f32[88,128]{1,0:T(8,128)S(1)} collective-permute-done((f32[88,128]{1,0:T(8,128)S(1)}, f32[88,128]{1,0:T(8,128)S(1)}, u32[]{:S(2)}, u32[]{:S(2)}) %collective-permute-start.1) | collective-permute-done | bytes 45088 | tf_op jit(solution)/shard_map/ppermute | solution.py:353
  35.9 0.5 collective-permute-done.one_ref
  36.4 0.0 copy-done.1
  36.4 3.5 %attitude.1 = (f32[1,4,128]{2,1,0:T(4,128)}, f32[64,128]{1,0:T(8,128)}) custom-call(f32[88,128]{1,0:T(8,128)S(1)} %bins.1.own_ref, f32[88,128]{1,0:T(8,128)S(1)} %collective-permute-done.one_ref, f32[88,128]{1,0:T(8,128)S(1)} %collective-permute-done.1.two_ref, f32[88,128]{1,0:T(8,128)S(1)} %collective-permute-done.2.three_ref, f32[256,128]{1,0:T(8,128)S(1)} %bitcast.13, ...), custom_call_target="tpu_custom_call" | custom-call | flops 1000000 | bytes 480256 | tf_op jit(solution)/shard_map/attitude/pallas_call | solution.py:330
  39.8 10.1 %all-to-all-start.1 = ((f32[64,1,128]{2,1,0:T(1,128)}), f32[64,1,128]{2,1,0:T(1,128)S(1)}, u32[]{:S(2)}, u32[]{:S(2)}) async-start(f32[64,1,128]{2,1,0:T(1,128)} %bitcast.8), calls=%async_computation.1 | async-start | bytes 65536 | tf_op jit(solution)/shard_map/all_to_all | solution.py:358
  49.9 2.0 %collective-permute-start.4 = (f32[240,256]{1,0:T(8,128)S(1)}, f32[240,256]{1,0:T(8,128)S(1)}, u32[]{:S(2)}, u32[]{:S(2)}) collective-permute-start(f32[240,256]{1,0:T(8,128)S(1)} %source_normals.1.own_ref), channel_id=1, source_target_pairs={{0,2},{1,3},{2,0},{3,1},{4,6},{5,7},{6,4},{7,5},{8,10},{9,11},{10,... | collective-permute-start | bytes 737288 | tf_op jit(solution)/shard_map/ppermute | solution.py:353
  51.9 2.0 %collective-permute-start.3 = (f32[240,256]{1,0:T(8,128)S(1)}, f32[240,256]{1,0:T(8,128)S(1)}, u32[]{:S(2)}, u32[]{:S(2)}) collective-permute-start(f32[240,256]{1,0:T(8,128)S(1)} %source_normals.1.own_ref), channel_id=1, source_target_pairs={{0,1},{1,2},{2,3},{3,0},{4,5},{5,6},{6,7},{7,4},{8,9},{9,10},{10,1... | collective-permute-start | bytes 737288 | tf_op jit(solution)/shard_map/ppermute | solution.py:353
  53.9 5.0 %all-to-all-done.1 = f32[64,1,128]{2,1,0:T(1,128)S(1)} async-done(((f32[64,1,128]{2,1,0:T(1,128)}), f32[64,1,128]{2,1,0:T(1,128)S(1)}, u32[]{:S(2)}, u32[]{:S(2)}) %all-to-all-start.1) | async-done | bytes 32800 | tf_op jit(solution)/shard_map/all_to_all | solution.py:358
  59.0 5.0 %source_right.1.own_ref = f32[80,256]{1,0:T(8,128)S(1)} custom-call(f32[64,128]{1,0:T(8,128)S(1)} %bitcast.15, f32[8,128]{1,0:T(8,128)S(1)} %get-tuple-element.10.slot_ref, f32[768,128]{1,0:T(8,128)S(1)} %get-tuple-element.11.obs_ref, s32[128,128]{1,0:T(8,128)S(1)} %copy-done.7, f32[640,128]{1,0:T(8,128)S(1)} %bitcast.20), custom_call_target="tpu_custom_call" | custom-call | flops 1342177280 | bytes 823296 | tf_op jit(solution)/shard_map/source_right/pallas_call | solution.py:330
  64.0 3.5 %collective-permute-start.8 = (f32[80,256]{1,0:T(8,128)S(1)}, f32[80,256]{1,0:T(8,128)S(1)}, u32[]{:S(2)}, u32[]{:S(2)}) collective-permute-start(f32[80,256]{1,0:T(8,128)S(1)} %source_right.1.own_ref), channel_id=1, source_target_pairs={{0,3},{1,0},{2,1},{3,2},{4,7},{5,4},{6,5},{7,6},{8,11},{9,8},{10,9... | collective-permute-start | bytes 245768 | tf_op jit(solution)/shard_map/ppermute | solution.py:353
  67.5 0.2 collective-permute-start.7
  67.7 0.0 collective-permute-done.5.three_ref
  67.7 0.4 collective-permute-start.6
  68.2 0.0 collective-permute-done.4.two_ref
  68.2 0.0 collective-permute-done.3.one_ref
  68.2 0.1 factors.1.factor_ref
  68.3 1.6 %collective-permute-done.8.three_ref = f32[80,256]{1,0:T(8,128)S(1)} collective-permute-done((f32[80,256]{1,0:T(8,128)S(1)}, f32[80,256]{1,0:T(8,128)S(1)}, u32[]{:S(2)}, u32[]{:S(2)}) %collective-permute-start.8) | collective-permute-done | bytes 81952 | tf_op jit(solution)/shard_map/ppermute | solution.py:353
  69.9 2.5 %collective-permute-done.7.two_ref = f32[80,256]{1,0:T(8,128)S(1)} collective-permute-done((f32[80,256]{1,0:T(8,128)S(1)}, f32[80,256]{1,0:T(8,128)S(1)}, u32[]{:S(2)}, u32[]{:S(2)}) %collective-permute-start.7) | collective-permute-done | bytes 81952 | tf_op jit(solution)/shard_map/ppermute | solution.py:353
  72.4 0.7 collective-permute-done.6.one_ref
  73.1 0.7 solve.1
Async XLA Ops:
  0.6 0.7 copy-start.4
  0.6 0.7 copy-start.5
  1.3 0.9 %copy-start = (f32[128,4,128]{2,1,0:T(4,128)S(1)}, f32[128,4,128]{2,1,0:T(4,128)}, u32[]{:S(2)}) copy-start(f32[128,4,128]{2,1,0:T(4,128)} %param.13) | copy-start | bytes 786436
  2.3 0.8 %copy-start.2 = (f32[128,128]{1,0:T(8,128)S(1)}, f32[128,128]{1,0:T(8,128)}, u32[]{:S(2)}) copy-start(f32[128,128]{1,0:T(8,128)} %resid_ref.1) | copy-start | bytes 196612
  3.1 0.8 %copy-start.3 = (f32[128,128]{1,0:T(8,128)S(1)}, f32[128,128]{1,0:T(8,128)}, u32[]{:S(2)}) copy-start(f32[128,128]{1,0:T(8,128)} %phase_ref.1) | copy-start | bytes 196612
  3.9 14.8 %copy-start.6 = (f32[128,5,128]{2,0,1:T(8,128)S(1)}, f32[128,5,128]{2,0,1:T(8,128)}, u32[]{:S(2)}) copy-start(f32[128,5,128]{2,0,1:T(8,128)} %param.14) | copy-start | bytes 983044
  5.4 13.3 %copy-start.7 = (s32[128,128]{1,0:T(8,128)S(1)}, s32[128,128]{1,0:T(8,128)}, u32[]{:S(2)}) copy-start(s32[128,128]{1,0:T(8,128)} %source_ref.3) | copy-start | bytes 196612
  5.4 23.2 %all-to-all-start = ((f32[64,4,128]{2,1,0:T(4,128)}), f32[64,4,128]{2,1,0:T(4,128)S(1)}, u32[]{:S(2)}, u32[]{:S(2)}) async-start(f32[64,4,128]{2,1,0:T(4,128)} %bitcast.3), calls=%async_computation | async-start | bytes 262144 | tf_op jit(solution)/shard_map/all_to_all | solution.py:358
  18.8 17.6 %copy-start.1 = (f32[120,352]{1,0:T(8,128)S(1)}, f32[120,352]{1,0:T(8,128)}, u32[]{:S(2)}) copy-start(f32[120,352]{1,0:T(8,128)} %constant.2.clone.table_ref) | copy-start | bytes 506884
  25.8 41.9 %collective-permute-start.5 = (f32[240,256]{1,0:T(8,128)S(1)}, f32[240,256]{1,0:T(8,128)S(1)}, u32[]{:S(2)}, u32[]{:S(2)}) collective-permute-start(f32[240,256]{1,0:T(8,128)S(1)} %source_normals.1.own_ref), channel_id=1, source_target_pairs={{0,3},{1,0},{2,1},{3,2},{4,7},{5,4},{6,5},{7,6},{8,11},{9,8},{10,9... | collective-permute-start | bytes 737288 | tf_op jit(solution)/shard_map/ppermute | solution.py:353
  28.9 5.6 %collective-permute-start.2 = (f32[88,128]{1,0:T(8,128)S(1)}, f32[88,128]{1,0:T(8,128)S(1)}, u32[]{:S(2)}, u32[]{:S(2)}) collective-permute-start(f32[88,128]{1,0:T(8,128)S(1)} %bins.1.own_ref), channel_id=1, source_target_pairs={{0,3},{1,0},{2,1},{3,2},{4,7},{5,4},{6,5},{7,6},{8,11},{9,8},{10,9... | collective-permute-start | bytes 135176 | tf_op jit(solution)/shard_map/ppermute | solution.py:353
  31.5 4.4 %collective-permute-start.1 = (f32[88,128]{1,0:T(8,128)S(1)}, f32[88,128]{1,0:T(8,128)S(1)}, u32[]{:S(2)}, u32[]{:S(2)}) collective-permute-start(f32[88,128]{1,0:T(8,128)S(1)} %bins.1.own_ref), channel_id=1, source_target_pairs={{0,2},{1,3},{2,0},{3,1},{4,6},{5,7},{6,4},{7,5},{8,10},{9,11},{10,... | collective-permute-start | bytes 135176 | tf_op jit(solution)/shard_map/ppermute | solution.py:353
  32.0 4.4 %collective-permute-start = (f32[88,128]{1,0:T(8,128)S(1)}, f32[88,128]{1,0:T(8,128)S(1)}, u32[]{:S(2)}, u32[]{:S(2)}) collective-permute-start(f32[88,128]{1,0:T(8,128)S(1)} %bins.1.own_ref), channel_id=1, source_target_pairs={{0,1},{1,2},{2,3},{3,0},{4,5},{5,6},{6,7},{7,4},{8,9},{9,10},{10,1... | collective-permute-start | bytes 135176 | tf_op jit(solution)/shard_map/ppermute | solution.py:353
  39.8 19.1 %all-to-all-start.1 = ((f32[64,1,128]{2,1,0:T(1,128)}), f32[64,1,128]{2,1,0:T(1,128)S(1)}, u32[]{:S(2)}, u32[]{:S(2)}) async-start(f32[64,1,128]{2,1,0:T(1,128)} %bitcast.8), calls=%async_computation.1 | async-start | bytes 65536 | tf_op jit(solution)/shard_map/all_to_all | solution.py:358
  49.9 18.3 %collective-permute-start.4 = (f32[240,256]{1,0:T(8,128)S(1)}, f32[240,256]{1,0:T(8,128)S(1)}, u32[]{:S(2)}, u32[]{:S(2)}) collective-permute-start(f32[240,256]{1,0:T(8,128)S(1)} %source_normals.1.own_ref), channel_id=1, source_target_pairs={{0,2},{1,3},{2,0},{3,1},{4,6},{5,7},{6,4},{7,5},{8,10},{9,11},{10,... | collective-permute-start | bytes 737288 | tf_op jit(solution)/shard_map/ppermute | solution.py:353
  51.9 16.2 %collective-permute-start.3 = (f32[240,256]{1,0:T(8,128)S(1)}, f32[240,256]{1,0:T(8,128)S(1)}, u32[]{:S(2)}, u32[]{:S(2)}) collective-permute-start(f32[240,256]{1,0:T(8,128)S(1)} %source_normals.1.own_ref), channel_id=1, source_target_pairs={{0,1},{1,2},{2,3},{3,0},{4,5},{5,6},{6,7},{7,4},{8,9},{9,10},{10,1... | collective-permute-start | bytes 737288 | tf_op jit(solution)/shard_map/ppermute | solution.py:353
  64.0 5.9 %collective-permute-start.8 = (f32[80,256]{1,0:T(8,128)S(1)}, f32[80,256]{1,0:T(8,128)S(1)}, u32[]{:S(2)}, u32[]{:S(2)}) collective-permute-start(f32[80,256]{1,0:T(8,128)S(1)} %source_right.1.own_ref), channel_id=1, source_target_pairs={{0,3},{1,0},{2,1},{3,2},{4,7},{5,4},{6,5},{7,6},{8,11},{9,8},{10,9... | collective-permute-start | bytes 245768 | tf_op jit(solution)/shard_map/ppermute | solution.py:353
  67.5 4.9 %collective-permute-start.7 = (f32[80,256]{1,0:T(8,128)S(1)}, f32[80,256]{1,0:T(8,128)S(1)}, u32[]{:S(2)}, u32[]{:S(2)}) collective-permute-start(f32[80,256]{1,0:T(8,128)S(1)} %source_right.1.own_ref), channel_id=1, source_target_pairs={{0,2},{1,3},{2,0},{3,1},{4,6},{5,7},{6,4},{7,5},{8,10},{9,11},{10,... | collective-permute-start | bytes 245768 | tf_op jit(solution)/shard_map/ppermute | solution.py:353
  67.7 5.4 %collective-permute-start.6 = (f32[80,256]{1,0:T(8,128)S(1)}, f32[80,256]{1,0:T(8,128)S(1)}, u32[]{:S(2)}, u32[]{:S(2)}) collective-permute-start(f32[80,256]{1,0:T(8,128)S(1)} %source_right.1.own_ref), channel_id=1, source_target_pairs={{0,1},{1,2},{2,3},{3,0},{4,5},{5,6},{6,7},{7,4},{8,9},{9,10},{10,1... | collective-permute-start | bytes 245768 | tf_op jit(solution)/shard_map/ppermute | solution.py:353

commit v2 on v1

--- a/solution.py
+++ b/solution.py
@@ -22,6 +22,7 @@
 HIGH = 16
 LOW = 256
 STEP_BLOCKS = 16
+STEPS = NBLK // STEP_BLOCKS
 
 KNOT_PRIOR = 1.0
 SOURCE_PRIOR = 1.0
@@ -91,7 +92,14 @@
     return iota(shape, axis).astype(F32)
 
 
-def normals_kernel(bin_ref, rows_ref, resid_ref, phase_ref, att_ref, send_ref, obs_ref, slot_ref, pay_ref):
+def normals_kernel(*refs):
+    given, (send_ref, obs_ref, slot_ref), here, (pay_ref, done_ref) = refs[:5], refs[5:8], refs[8:13], refs[13:]
+    copies = [pltpu.make_async_copy(given[at], here[at], done_ref.at[at]) for at in range(5)]
+    for copy in copies:
+        copy.start()
+    for copy in copies:
+        copy.wait()
+    bin_ref, rows_ref, resid_ref, phase_ref, att_ref = here
     square = (NBLK, NBLK)
     bins = bin_ref[...].astype(F32)
     window = jnp.floor((bins + 0.5) * (1.0 / BINS_W))
@@ -190,26 +198,44 @@
         reply_ref[:, 16 * s : 16 * s + 16] = knots[WINDOWS * s : WINDOWS * s + WINDOWS]
 
 
-def source_sums(count, terms_ref, high_ref, low_ref, a_ref, b_ref, acc_ref):
+def source_sums(count, terms_ref, high_ref, low_ref, out_ref, acc_ref, *buffers):
     high_at = iota_f((HIGH, ROWS), 0)
     low_at = iota_f((LOW, ROWS), 0).astype(BF16)
-    acc_ref[...] = jnp.zeros(acc_ref.shape, F32)
-
-    def step(at, carry):
+    one, zero = jnp.ones((), BF16), jnp.zeros((), BF16)
+
+    def build(at, slot):
+        a_ref, b_ref = buffers[slot], buffers[2 + slot]
         for inner in range(STEP_BLOCKS):
             block = at * STEP_BLOCKS + inner
             lanes = slice(inner * ROWS, inner * ROWS + ROWS)
             here = high_at == high_ref[pl.ds(block, 1), :]
             low = jnp.broadcast_to(low_ref[pl.ds(block, 1), :], (HIGH, ROWS)).astype(BF16)
             low = jnp.concatenate([low] * (LOW // HIGH), axis=0)
-            b_ref[:, lanes] = jnp.where(low_at == low, jnp.ones((), BF16), jnp.zeros((), BF16))
+            b_ref[:, lanes] = jnp.where(low_at == low, one, zero)
             for c in range(2 * count):
                 term = jnp.where(here, terms_ref[pl.ds(c * NBLK + block, 1), :], 0.0)
                 a_ref[c * HIGH : (c + 1) * HIGH, lanes] = term.astype(BF16)
-        acc_ref[...] += lax.dot_general(a_ref[...], b_ref[...], NT, preferred_element_type=F32)
+
+    def multiply(slot):
+        acc_ref[...] += lax.dot_general(buffers[2 + slot][...], buffers[slot][...], NT, preferred_element_type=F32)
+
+    def step(pair, carry):
+        multiply(0)
+        build(2 * pair + 1, 1)
+        multiply(1)
+        build(2 * pair + 2, 0)
         return carry
 
-    lax.fori_loop(0, NBLK // STEP_BLOCKS, step, 0)
+    acc_ref[...] = jnp.zeros(acc_ref.shape, F32)
+    build(0, 0)
+    lax.fori_loop(0, STEPS // 2 - 1, step, 0)
+    multiply(0)
+    build(STEPS - 1, 1)
+    multiply(1)
+    sums = acc_ref[...].T
+    for c in range(count):
+        at = 2 * c * HIGH
+        out_ref[HIGH * c : HIGH * c + HIGH, :] = sums[at : at + HIGH] + sums[at + HIGH : at + 2 * HIGH]
 
 
 def put_terms(terms_ref, c, values):
@@ -225,7 +251,7 @@
     low_ref[...] = (source - (high << 8)).astype(F32)
 
 
-def source_normals_kernel(rows_ref, source_ref, gain_ref, out_ref, terms_ref, high_ref, low_ref, a_ref, b_ref, acc_ref):
+def source_normals_kernel(rows_ref, source_ref, gain_ref, out_ref, terms_ref, high_ref, low_ref, *work):
     square = (NBLK, ROWS)
     used = jnp.broadcast_to(rows_ref[...].astype(F32), square).T
     mask = iota_f(square, 1) < used
@@ -233,15 +259,11 @@
     gains = [jnp.where(mask, gain_ref[NBLK * p : NBLK * p + NBLK, :], 0.0) for p in range(5)]
     for at, (first, second) in enumerate(PAIR_LIST):
         put_terms(terms_ref, at, gains[first] * gains[second])
-    source_sums(15, terms_ref, high_ref, low_ref, a_ref, b_ref, acc_ref)
-    for c in range(15):
-        out_ref[HIGH * c : HIGH * c + HIGH, :] = (
-            acc_ref[2 * c * HIGH : (2 * c + 1) * HIGH, :] + acc_ref[(2 * c + 1) * HIGH : (2 * c + 2) * HIGH, :]
-        )
+    source_sums(15, terms_ref, high_ref, low_ref, out_ref, *work)
 
 
 def source_right_kernel(
-    reply_ref, slot_ref, obs_ref, source_ref, gain_ref, out_ref, terms_ref, high_ref, low_ref, a_ref, b_ref, acc_ref
+    reply_ref, slot_ref, obs_ref, source_ref, gain_ref, out_ref, terms_ref, high_ref, low_ref, *work
 ):
     put_sources(source_ref, high_ref, low_ref)
     place = indicator(iota_f((WINDOWS, NBLK), 0) == slot_ref[0:1, :])
@@ -271,11 +293,7 @@
     values = values.T
     for p in range(5):
         put_terms(terms_ref, p, gain_ref[NBLK * p : NBLK * p + NBLK, :] * values)
-    source_sums(5, terms_ref, high_ref, low_ref, a_ref, b_ref, acc_ref)
-    for c in range(5):
-        out_ref[HIGH * c : HIGH * c + HIGH, :] = (
-            acc_ref[2 * c * HIGH : (2 * c + 1) * HIGH, :] + acc_ref[(2 * c + 1) * HIGH : (2 * c + 2) * HIGH, :]
-        )
+    source_sums(5, terms_ref, high_ref, low_ref, out_ref, *work)
 
 
 def factor_kernel(own_ref, one_ref, two_ref, three_ref, out_ref):
@@ -325,13 +343,14 @@
     return jax.ShapeDtypeStruct(shape, F32)
 
 
-def kernel_call(body, name, outs, *args, scratch=(), flops=1_000_000):
+def kernel_call(body, name, outs, *args, scratch=(), flops=1_000_000, in_specs=None, grant=32):
     size = sum(math.prod(a.shape) * 4 for a in args)
     return pl.pallas_call(
         body,
         out_shape=outs,
+        in_specs=in_specs or [pl.BlockSpec(memory_space=pltpu.MemorySpace.VMEM)] * len(args),
         scratch_shapes=list(scratch),
-        compiler_params=pltpu.CompilerParams(vmem_limit_bytes=32 * 1024 * 1024),
+        compiler_params=pltpu.CompilerParams(vmem_limit_bytes=grant * 1024 * 1024),
         cost_estimate=pl.CostEstimate(flops=flops, bytes_accessed=size, transcendentals=0),
         name=name,
     )(*args)
@@ -342,9 +361,11 @@
         pltpu.VMEM((2 * count * NBLK, ROWS), F32),
         pltpu.VMEM((NBLK, ROWS), F32),
         pltpu.VMEM((NBLK, ROWS), F32),
+        pltpu.VMEM((LOW, 2 * count * HIGH), F32),
+        pltpu.VMEM((2 * count * HIGH, STEP_BLOCKS * ROWS), BF16),
         pltpu.VMEM((2 * count * HIGH, STEP_BLOCKS * ROWS), BF16),
         pltpu.VMEM((LOW, STEP_BLOCKS * ROWS), BF16),
-        pltpu.VMEM((2 * count * HIGH, LOW), F32),
+        pltpu.VMEM((LOW, STEP_BLOCKS * ROWS), BF16),
     )
 
 
@@ -371,7 +392,17 @@
         obs_resid,
         obs_phase,
         att_partial.reshape(4 * NBLK, ROWS),
-        scratch=(pltpu.VMEM((NBLK, NBLK), F32),),
+        scratch=(
+            pltpu.VMEM((1, NBLK), jnp.int32),
+            pltpu.VMEM((1, NBLK), jnp.int32),
+            pltpu.VMEM((NBLK, ROWS), F32),
+            pltpu.VMEM((NBLK, ROWS), F32),
+            pltpu.VMEM((4 * NBLK, ROWS), F32),
+            pltpu.VMEM((NBLK, NBLK), F32),
+            pltpu.SemaphoreType.DMA((5,)),
+        ),
+        in_specs=[pl.BlockSpec(memory_space=pl.ANY)] * 5,
+        grant=56,
     )
     got = to_windows(send.reshape(WINDOWS, CAP, 128)).reshape(SLOTS, 128)
     normal = kernel_call(

time: 74.2 us -> 72.2 us (0.973)
  local copies, waits for them, and re-layouts: 3.3 us -> 0.65 us
    unnamed x16 -> x12, local copies, waits for them, and re-layouts: 3.3 us -> 0.65 us
  transfers between devices with their start and end apart: 11 -> 11, of which waited for: 8 -> 7; matrix products, arithmetic and copies ran while one was open for 0% -> 0% of each run, Pallas kernels for 22% -> 22%
where the time goes in v2:
time: 72.2 us; the launch traced here: 71.9 us
  starting transfers between devices  38.1 us (53%)
  Pallas kernels  18.8 us (26%)
  waiting for transfers between devices  13.6 us (19%)
  between operations  0.75 us (1%)
    all_to_all x2, starting transfers between devices, to_windows(): lax.all_to_all(values, ('src', 'win'), split_axis=0, concat_axis=0, tiled...  24 us
    pallas_call x7, Pallas kernels, kernel_call(): pl.pallas_call(body, out_shape=outs, in_specs=in_specs or [pl.BlockSpec(m...  18.8 us
    ppermute x9, starting transfers between devices, from_others(): lax.ppermute(values, 'ccd', [(at, (at + shift) % N_CCD) for at in range(N...  14.1 us
    ppermute x9, waiting for transfers between devices, from_others(): lax.ppermute(values, 'ccd', [(at, (at + shift) % N_CCD) for at in range(N...  8.59 us
    all_to_all x2, waiting for transfers between devices, to_windows(): lax.all_to_all(values, ('src', 'win'), split_axis=0, concat_axis=0, tiled...  5.02 us
  transfers between devices with their start and end apart: 11, of which 7 were waited for; matrix products, arithmetic and copies ran while one was open for 0% of the time, Pallas kernels for 22%

profile of v2, /device:TPU:1, one launch (start us, length us, event | category | flops | bytes accessed | tf_op | source)
XLA Modules:
  0.0 71.9 jit_solution(4640746849559242352)
XLA Ops:
  0.6 0.0 copy-start.3
  0.6 2.6 %normals.1 = (f32[256,128]{1,0:T(8,128)}, f32[768,128]{1,0:T(8,128)}, f32[8,128]{1,0:T(8,128)}) custom-call(s32[1,128]{1,0:T(1,128)} %bitcast.21, s32[1,128]{1,0:T(1,128)} %bitcast.15, f32[128,128]{1,0:T(8,128)} %refs_2_.1, f32[128,128]{1,0:T(8,128)} %refs_3_.1, f32[512,128]{1,0:T(8,128)} %bitcast.19), custom_call_target="tpu_custom_call" | custom-call | flops 1000000 | bytes 394240 | tf_op jit(solution)/shard_map/normals/pallas_call | solution.py:348
  3.3 0.0 copy-start.4
  3.3 13.3 %all-to-all-start = ((f32[64,4,128]{2,1,0:T(4,128)}), f32[64,4,128]{2,1,0:T(4,128)S(1)}, u32[]{:S(2)}, u32[]{:S(2)}) async-start(f32[64,4,128]{2,1,0:T(4,128)} %bitcast.20), calls=%async_computation | async-start | bytes 262144 | tf_op jit(solution)/shard_map/all_to_all | solution.py:379
  16.6 0.0 copy-start.1
  16.6 0.0 copy-done.3
  16.6 0.0 copy-done.4
  16.6 0.6 copy-done.1
  17.3 0.0 copy-start
  17.3 7.1 %source_normals.1.own_ref = f32[240,256]{1,0:T(8,128)S(1)} custom-call(s32[1,128]{1,0:T(1,128)S(1)} %bitcast.16, s32[128,128]{1,0:T(8,128)S(1)} %copy-done.4, f32[640,128]{1,0:T(8,128)S(1)} %bitcast.17), custom_call_target="tpu_custom_call" | custom-call | flops 4026531840 | bytes 393728 | tf_op jit(solution)/shard_map/source_normals/pallas_call | solution.py:348
  24.3 0.0 copy-start.2
  24.3 2.6 %collective-permute-start.5 = (f32[240,256]{1,0:T(8,128)S(1)}, f32[240,256]{1,0:T(8,128)S(1)}, u32[]{:S(2)}, u32[]{:S(2)}) collective-permute-start(f32[240,256]{1,0:T(8,128)S(1)} %source_normals.1.own_ref), channel_id=1, source_target_pairs={{0,3},{1,0},{2,1},{3,2},{4,7},{5,4},{6,5},{7,6},{8,11},{9,8},{10,9... | collective-permute-start | bytes 737288 | tf_op jit(solution)/shard_map/ppermute | solution.py:374
  26.9 0.0 all-to-all-done
  26.9 0.3 bins.1.own_ref
  27.2 2.2 %collective-permute-start.2 = (f32[88,128]{1,0:T(8,128)S(1)}, f32[88,128]{1,0:T(8,128)S(1)}, u32[]{:S(2)}, u32[]{:S(2)}) collective-permute-start(f32[88,128]{1,0:T(8,128)S(1)} %bins.1.own_ref), channel_id=1, source_target_pairs={{0,3},{1,0},{2,1},{3,2},{4,7},{5,4},{6,5},{7,6},{8,11},{9,8},{10,9... | collective-permute-start | bytes 135176 | tf_op jit(solution)/shard_map/ppermute | solution.py:374
  29.4 0.5 collective-permute-start.1
  29.9 0.6 collective-permute-start
  30.5 2.6 %collective-permute-done.2.three_ref = f32[88,128]{1,0:T(8,128)S(1)} collective-permute-done((f32[88,128]{1,0:T(8,128)S(1)}, f32[88,128]{1,0:T(8,128)S(1)}, u32[]{:S(2)}, u32[]{:S(2)}) %collective-permute-start.2) | collective-permute-done | bytes 45088 | tf_op jit(solution)/shard_map/ppermute | solution.py:374
  33.1 0.7 collective-permute-done.1.two_ref
  33.8 0.5 collective-permute-done.one_ref
  34.2 0.0 copy-done
  34.3 3.5 %attitude.1 = (f32[1,4,128]{2,1,0:T(4,128)}, f32[64,128]{1,0:T(8,128)}) custom-call(f32[88,128]{1,0:T(8,128)S(1)} %bins.1.own_ref, f32[88,128]{1,0:T(8,128)S(1)} %collective-permute-done.one_ref, f32[88,128]{1,0:T(8,128)S(1)} %collective-permute-done.1.two_ref, f32[88,128]{1,0:T(8,128)S(1)} %collective-permute-done.2.three_ref, f32[256,128]{1,0:T(8,128)S(1)} %bitcast.13, ...), custom_call_target="tpu_custom_call" | custom-call | flops 1000000 | bytes 480256 | tf_op jit(solution)/shard_map/attitude/pallas_call | solution.py:348
  37.7 10.7 %all-to-all-start.1 = ((f32[64,1,128]{2,1,0:T(1,128)}), f32[64,1,128]{2,1,0:T(1,128)S(1)}, u32[]{:S(2)}, u32[]{:S(2)}) async-start(f32[64,1,128]{2,1,0:T(1,128)} %bitcast.8), calls=%async_computation.1 | async-start | bytes 65536 | tf_op jit(solution)/shard_map/all_to_all | solution.py:379
  48.4 0.0 copy-start.5
  48.4 2.0 %collective-permute-start.4 = (f32[240,256]{1,0:T(8,128)S(1)}, f32[240,256]{1,0:T(8,128)S(1)}, u32[]{:S(2)}, u32[]{:S(2)}) collective-permute-start(f32[240,256]{1,0:T(8,128)S(1)} %source_normals.1.own_ref), channel_id=1, source_target_pairs={{0,2},{1,3},{2,0},{3,1},{4,6},{5,7},{6,4},{7,5},{8,10},{9,11},{10,... | collective-permute-start | bytes 737288 | tf_op jit(solution)/shard_map/ppermute | solution.py:374
  50.5 2.0 %collective-permute-start.3 = (f32[240,256]{1,0:T(8,128)S(1)}, f32[240,256]{1,0:T(8,128)S(1)}, u32[]{:S(2)}, u32[]{:S(2)}) collective-permute-start(f32[240,256]{1,0:T(8,128)S(1)} %source_normals.1.own_ref), channel_id=1, source_target_pairs={{0,1},{1,2},{2,3},{3,0},{4,5},{5,6},{6,7},{7,4},{8,9},{9,10},{10,1... | collective-permute-start | bytes 737288 | tf_op jit(solution)/shard_map/ppermute | solution.py:374
  52.5 5.0 %all-to-all-done.1 = f32[64,1,128]{2,1,0:T(1,128)S(1)} async-done(((f32[64,1,128]{2,1,0:T(1,128)}), f32[64,1,128]{2,1,0:T(1,128)S(1)}, u32[]{:S(2)}, u32[]{:S(2)}) %all-to-all-start.1) | async-done | bytes 32800 | tf_op jit(solution)/shard_map/all_to_all | solution.py:379
  57.5 0.0 copy-done.2
  57.5 0.0 copy-done.5
  57.5 4.6 %source_right.1.own_ref = f32[80,256]{1,0:T(8,128)S(1)} custom-call(f32[64,128]{1,0:T(8,128)S(1)} %bitcast.14, f32[8,128]{1,0:T(8,128)S(1)} %copy-done.5, f32[768,128]{1,0:T(8,128)S(1)} %copy-done.2, s32[128,128]{1,0:T(8,128)S(1)} %copy-done.4, f32[640,128]{1,0:T(8,128)S(1)} %bitcast.18), custom_call_target="tpu_custom_call" | custom-call | flops 1342177280 | bytes 823296 | tf_op jit(solution)/shard_map/source_right/pallas_call | solution.py:348
  62.1 3.5 %collective-permute-start.8 = (f32[80,256]{1,0:T(8,128)S(1)}, f32[80,256]{1,0:T(8,128)S(1)}, u32[]{:S(2)}, u32[]{:S(2)}) collective-permute-start(f32[80,256]{1,0:T(8,128)S(1)} %source_right.1.own_ref), channel_id=1, source_target_pairs={{0,3},{1,0},{2,1},{3,2},{4,7},{5,4},{6,5},{7,6},{8,11},{9,8},{10,9... | collective-permute-start | bytes 245768 | tf_op jit(solution)/shard_map/ppermute | solution.py:374
  65.6 0.2 collective-permute-start.7
  65.8 0.0 collective-permute-done.5.three_ref
  65.8 0.4 collective-permute-start.6
  66.3 0.0 collective-permute-done.4.two_ref
  66.3 0.0 collective-permute-done.3.one_ref
  66.3 0.1 factors.1.factor_ref
  66.4 1.6 %collective-permute-done.8.three_ref = f32[80,256]{1,0:T(8,128)S(1)} collective-permute-done((f32[80,256]{1,0:T(8,128)S(1)}, f32[80,256]{1,0:T(8,128)S(1)}, u32[]{:S(2)}, u32[]{:S(2)}) %collective-permute-start.8) | collective-permute-done | bytes 81952 | tf_op jit(solution)/shard_map/ppermute | solution.py:374
  68.0 2.5 %collective-permute-done.7.two_ref = f32[80,256]{1,0:T(8,128)S(1)} collective-permute-done((f32[80,256]{1,0:T(8,128)S(1)}, f32[80,256]{1,0:T(8,128)S(1)}, u32[]{:S(2)}, u32[]{:S(2)}) %collective-permute-start.7) | collective-permute-done | bytes 81952 | tf_op jit(solution)/shard_map/ppermute | solution.py:374
  70.5 0.7 collective-permute-done.6.one_ref
  71.2 0.7 %solve.1 = f32[5,4096]{1,0:T(8,128)} custom-call(f32[240,256]{1,0:T(8,128)S(1)} %factors.1.factor_ref, f32[80,256]{1,0:T(8,128)S(1)} %source_right.1.own_ref, f32[80,256]{1,0:T(8,128)S(1)} %collective-permute-done.6.one_ref, f32[80,256]{1,0:T(8,128)S(1)} %collective-permute-done.7.two_ref, f32[80,256]{1,0:T(8,128)S(1)} %collective-permute-done.8.three_ref), custom_call_target="tpu_custom_call" | custom-call | flops 1000000 | bytes 573440 | tf_op jit(solution)/shard_map/solve/pallas_call | solution.py:348
Async XLA Ops:
  0.6 16.0 %copy-start.3 = (f32[128,5,128]{2,0,1:T(8,128)S(1)}, f32[128,5,128]{2,0,1:T(8,128)}, u32[]{:S(2)}) copy-start(f32[128,5,128]{2,0,1:T(8,128)} %param.14) | copy-start | bytes 983044
  3.3 13.3 %copy-start.4 = (s32[128,128]{1,0:T(8,128)S(1)}, s32[128,128]{1,0:T(8,128)}, u32[]{:S(2)}) copy-start(s32[128,128]{1,0:T(8,128)} %source_ref.3) | copy-start | bytes 196612
  3.3 23.6 %all-to-all-start = ((f32[64,4,128]{2,1,0:T(4,128)}), f32[64,4,128]{2,1,0:T(4,128)S(1)}, u32[]{:S(2)}, u32[]{:S(2)}) async-start(f32[64,4,128]{2,1,0:T(4,128)} %bitcast.20), calls=%async_computation | async-start | bytes 262144 | tf_op jit(solution)/shard_map/all_to_all | solution.py:379
  16.6 0.7 copy-start.1
  17.3 17.0 %copy-start = (f32[120,352]{1,0:T(8,128)S(1)}, f32[120,352]{1,0:T(8,128)}, u32[]{:S(2)}) copy-start(f32[120,352]{1,0:T(8,128)} %constant.2.clone.table_ref) | copy-start | bytes 506884
  24.3 33.2 %copy-start.2 = (f32[768,128]{1,0:T(8,128)S(1)}, f32[768,128]{1,0:T(8,128)}, u32[]{:S(2)}) copy-start(f32[768,128]{1,0:T(8,128)} %get-tuple-element.11.obs_ref) | copy-start | bytes 1179652
  24.3 41.5 %collective-permute-start.5 = (f32[240,256]{1,0:T(8,128)S(1)}, f32[240,256]{1,0:T(8,128)S(1)}, u32[]{:S(2)}, u32[]{:S(2)}) collective-permute-start(f32[240,256]{1,0:T(8,128)S(1)} %source_normals.1.own_ref), channel_id=1, source_target_pairs={{0,3},{1,0},{2,1},{3,2},{4,7},{5,4},{6,5},{7,6},{8,11},{9,8},{10,9... | collective-permute-start | bytes 737288 | tf_op jit(solution)/shard_map/ppermute | solution.py:374
  27.2 5.9 %collective-permute-start.2 = (f32[88,128]{1,0:T(8,128)S(1)}, f32[88,128]{1,0:T(8,128)S(1)}, u32[]{:S(2)}, u32[]{:S(2)}) collective-permute-start(f32[88,128]{1,0:T(8,128)S(1)} %bins.1.own_ref), channel_id=1, source_target_pairs={{0,3},{1,0},{2,1},{3,2},{4,7},{5,4},{6,5},{7,6},{8,11},{9,8},{10,9... | collective-permute-start | bytes 135176 | tf_op jit(solution)/shard_map/ppermute | solution.py:374
  29.4 4.4 %collective-permute-start.1 = (f32[88,128]{1,0:T(8,128)S(1)}, f32[88,128]{1,0:T(8,128)S(1)}, u32[]{:S(2)}, u32[]{:S(2)}) collective-permute-start(f32[88,128]{1,0:T(8,128)S(1)} %bins.1.own_ref), channel_id=1, source_target_pairs={{0,2},{1,3},{2,0},{3,1},{4,6},{5,7},{6,4},{7,5},{8,10},{9,11},{10,... | collective-permute-start | bytes 135176 | tf_op jit(solution)/shard_map/ppermute | solution.py:374
  29.9 4.4 %collective-permute-start = (f32[88,128]{1,0:T(8,128)S(1)}, f32[88,128]{1,0:T(8,128)S(1)}, u32[]{:S(2)}, u32[]{:S(2)}) collective-permute-start(f32[88,128]{1,0:T(8,128)S(1)} %bins.1.own_ref), channel_id=1, source_target_pairs={{0,1},{1,2},{2,3},{3,0},{4,5},{5,6},{6,7},{7,4},{8,9},{9,10},{10,1... | collective-permute-start | bytes 135176 | tf_op jit(solution)/shard_map/ppermute | solution.py:374
  37.7 19.8 %all-to-all-start.1 = ((f32[64,1,128]{2,1,0:T(1,128)}), f32[64,1,128]{2,1,0:T(1,128)S(1)}, u32[]{:S(2)}, u32[]{:S(2)}) async-start(f32[64,1,128]{2,1,0:T(1,128)} %bitcast.8), calls=%async_computation.1 | async-start | bytes 65536 | tf_op jit(solution)/shard_map/all_to_all | solution.py:379
  48.4 9.1 %copy-start.5 = (f32[8,128]{1,0:T(8,128)S(1)}, f32[8,128]{1,0:T(8,128)}, u32[]{:S(2)}) copy-start(f32[8,128]{1,0:T(8,128)} %get-tuple-element.10.slot_ref) | copy-start | bytes 12292
  48.4 17.8 %collective-permute-start.4 = (f32[240,256]{1,0:T(8,128)S(1)}, f32[240,256]{1,0:T(8,128)S(1)}, u32[]{:S(2)}, u32[]{:S(2)}) collective-permute-start(f32[240,256]{1,0:T(8,128)S(1)} %source_normals.1.own_ref), channel_id=1, source_target_pairs={{0,2},{1,3},{2,0},{3,1},{4,6},{5,7},{6,4},{7,5},{8,10},{9,11},{10,... | collective-permute-start | bytes 737288 | tf_op jit(solution)/shard_map/ppermute | solution.py:374
  50.5 15.8 %collective-permute-start.3 = (f32[240,256]{1,0:T(8,128)S(1)}, f32[240,256]{1,0:T(8,128)S(1)}, u32[]{:S(2)}, u32[]{:S(2)}) collective-permute-start(f32[240,256]{1,0:T(8,128)S(1)} %source_normals.1.own_ref), channel_id=1, source_target_pairs={{0,1},{1,2},{2,3},{3,0},{4,5},{5,6},{6,7},{7,4},{8,9},{9,10},{10,1... | collective-permute-start | bytes 737288 | tf_op jit(solution)/shard_map/ppermute | solution.py:374
  62.1 5.9 %collective-permute-start.8 = (f32[80,256]{1,0:T(8,128)S(1)}, f32[80,256]{1,0:T(8,128)S(1)}, u32[]{:S(2)}, u32[]{:S(2)}) collective-permute-start(f32[80,256]{1,0:T(8,128)S(1)} %source_right.1.own_ref), channel_id=1, source_target_pairs={{0,3},{1,0},{2,1},{3,2},{4,7},{5,4},{6,5},{7,6},{8,11},{9,8},{10,9... | collective-permute-start | bytes 245768 | tf_op jit(solution)/shard_map/ppermute | solution.py:374
  65.6 4.9 %collective-permute-start.7 = (f32[80,256]{1,0:T(8,128)S(1)}, f32[80,256]{1,0:T(8,128)S(1)}, u32[]{:S(2)}, u32[]{:S(2)}) collective-permute-start(f32[80,256]{1,0:T(8,128)S(1)} %source_right.1.own_ref), channel_id=1, source_target_pairs={{0,2},{1,3},{2,0},{3,1},{4,6},{5,7},{6,4},{7,5},{8,10},{9,11},{10,... | collective-permute-start | bytes 245768 | tf_op jit(solution)/shard_map/ppermute | solution.py:374
  65.8 5.4 %collective-permute-start.6 = (f32[80,256]{1,0:T(8,128)S(1)}, f32[80,256]{1,0:T(8,128)S(1)}, u32[]{:S(2)}, u32[]{:S(2)}) collective-permute-start(f32[80,256]{1,0:T(8,128)S(1)} %source_right.1.own_ref), channel_id=1, source_target_pairs={{0,1},{1,2},{2,3},{3,0},{4,5},{5,6},{6,7},{7,4},{8,9},{9,10},{10,1... | collective-permute-start | bytes 245768 | tf_op jit(solution)/shard_map/ppermute | solution.py:374

commit v3 on v2

--- a/solution.py
+++ b/solution.py
@@ -1,8 +1,8 @@
-import functools
 import math
 
 import jax
 import jax.numpy as jnp
+import ml_dtypes
 import numpy as np
 from jax import lax
 from jax.experimental import pallas as pl
@@ -22,6 +22,7 @@
 HIGH = 16
 LOW = 256
 STEP_BLOCKS = 16
+EARLY = 5
 STEPS = NBLK // STEP_BLOCKS
 
 KNOT_PRIOR = 1.0
@@ -37,7 +38,8 @@
 NT = (((1,), (1,)), ((), ()))
 NN = (((1,), (0,)), ((), ()))
 
-SPLINE = np.array([[1, 0, 0, 0], [4, 12, 6, 1], [1, 6, 12, 4], [0, 0, 0, 1]], np.float64) / 6.0
+PIECES = np.array([[1, 0, 0, 0], [4, 12, 6, 1], [1, 6, 12, 4], [0, 0, 0, 1]], np.int64)
+SPLINE = PIECES / 6.0
 
 
 def knot_matrix():
@@ -52,13 +54,13 @@
                 for l in range(4):
                     j = l - d
                     if 0 <= j < 4:
-                        for m, value in enumerate(np.convolve(SPLINE[j], SPLINE[l])):
+                        for m, value in enumerate(np.convolve(PIECES[j], PIECES[l])):
                             table[row, l * FEATS + m * 10 + pair_at[q, p]] += value
     for q in range(4):
         for j in range(4):
-            table[112 + q, j * FEATS + RHS_AT + 4 * j + q] = 1.0
-            table[116 + q, j * FEATS + RHS_AT + 4 * j + q] = 1.0
-    return table.astype(np.float32)
+            table[112 + q, j * FEATS + RHS_AT + 4 * j + q] = 36.0
+            table[116 + q, j * FEATS + RHS_AT + 4 * j + q] = 36.0
+    return table.astype(ml_dtypes.bfloat16)
 
 
 def split_parts(values, count):
@@ -93,18 +95,28 @@
 
 
 def normals_kernel(*refs):
-    given, (send_ref, obs_ref, slot_ref), here, (pay_ref, done_ref) = refs[:5], refs[5:8], refs[8:13], refs[13:]
-    copies = [pltpu.make_async_copy(given[at], here[at], done_ref.at[at]) for at in range(5)]
+    given, (send_ref, obs_ref, slot_ref, marked_ref), here = refs[:6], refs[6:10], refs[10:16]
+    pay_ref, done_ref = refs[16:]
+    bin_ref, rows_ref, phase_ref, att_ref, resid_ref, source_ref = here
+    copies = [pltpu.make_async_copy(given[at], here[at], done_ref.at[at]) for at in range(6)]
     for copy in copies:
         copy.start()
-    for copy in copies:
-        copy.wait()
-    bin_ref, rows_ref, resid_ref, phase_ref, att_ref = here
     square = (NBLK, NBLK)
+    copies[0].wait()
     bins = bin_ref[...].astype(F32)
     window = jnp.floor((bins + 0.5) * (1.0 / BINS_W))
     local_bin = bins - BINS_W * window
+    window_column = jnp.broadcast_to(window, square).T
+    earlier = jnp.where(window_column == window, 1.0, 0.0) * jnp.where(iota(square, 0) < iota(square, 1), 1.0, 0.0)
+    rank = jnp.sum(earlier, axis=0, keepdims=True)
+    slot_ref[...] = jnp.concatenate([window, rank, jnp.zeros((6, NBLK), F32)], axis=0)
+    place = indicator(iota_f((SLOTS, NBLK), 0) == CAP * window + rank)
+    copies[1].wait()
     mask = iota(square, 0) < rows_ref[...]
+    used = jnp.broadcast_to(rows_ref[...].astype(F32), square).T
+    for copy in copies[2:]:
+        copy.wait()
+    marked_ref[...] = jnp.where(iota_f(square, 1) < used, source_ref[...], -LOW)
     u = phase_ref[...].T
     resid = jnp.where(mask, resid_ref[...].T, 0.0)
     att = [jnp.where(mask, att_ref[pl.ds(q, NBLK, stride=4), :].T, 0.0) for q in range(4)]
@@ -135,11 +147,6 @@
             pay_ref[row : row + 1, :] = total
     pay_ref[BIN_AT : BIN_AT + 1, :] = local_bin
     pay_ref[BIN_AT + 1 :, :] = jnp.zeros((NBLK - BIN_AT - 1, NBLK), F32)
-    window_column = jnp.broadcast_to(window, square).T
-    earlier = jnp.where(window_column == window, 1.0, 0.0) * jnp.where(iota(square, 0) < iota(square, 1), 1.0, 0.0)
-    rank = jnp.sum(earlier, axis=0, keepdims=True)
-    slot_ref[...] = jnp.concatenate([window, rank, jnp.zeros((6, NBLK), F32)], axis=0)
-    place = indicator(iota_f((SLOTS, NBLK), 0) == CAP * window + rank)
     send_ref[...] = exact_dot(pay_ref[...], place, NT, swap=True)
 
 
@@ -149,10 +156,11 @@
     out_ref[...] = exact_dot(got[:FEATS], place, NT)
 
 
-def attitude_kernel(own_ref, one_ref, two_ref, three_ref, got_ref, table_ref, att_ref, reply_ref):
-    total = (own_ref[...] + two_ref[...]) + (one_ref[...] + three_ref[...])
+def attitude_kernel(own_ref, one_ref, two_ref, three_ref, got_ref, table_ref, *rest):
+    att_ref, reply_ref = rest[1:3]
+    total = ((own_ref[...] + two_ref[...]) + (one_ref[...] + three_ref[...])) * (1.0 / 36.0)
     moved = jnp.concatenate([total] + [pltpu.roll(total, l, 1) for l in range(1, 4)], axis=0)
-    band = lax.dot_general(table_ref[...], moved, NN, precision=lax.Precision.HIGHEST, preferred_element_type=F32)
+    band = exact_dot(moved, table_ref[...], NN, swap=True)
     groups = [band[8 * at : 8 * at + 8] for at in range(14)]
     lower_half = iota((8, KNOTS_W), 0) < 4
 
@@ -166,26 +174,28 @@
         spread = [
             jnp.where(lower_half, vector[2 * at : 2 * at + 1, :], vector[2 * at + 1 : 2 * at + 2, :]) for at in range(2)
         ]
-        result = None
+        pieces = []
         for d in range(-3, 4):
             piece = groups[2 * (d + 3)] * spread[0] + groups[2 * (d + 3) + 1] * spread[1]
-            if d:
-                piece = pltpu.roll(piece, -d % KNOTS_W, 1)
-            result = piece if result is None else result + piece
-        return KNOT_PRIOR * vector + doubled(result)
+            pieces.append(pltpu.roll(piece, -d % KNOTS_W, 1) if d else piece)
+        outer = (pieces[0] + pieces[1]) + (pieces[2] + pieces[4])
+        return KNOT_PRIOR * vector + doubled(outer + ((pieces[5] + pieces[6]) + pieces[3]))
 
     residual = band[112:120]
     direction = residual
     estimate = jnp.zeros_like(residual)
-    norm_now = norm(residual * residual)
-    for _ in range(ITERS):
+    for iteration in range(ITERS):
         applied = apply(direction)
-        step_size = norm_now / norm(direction * applied)
+        norm_now = norm(residual * residual)
+        inverse = 1.0 / norm(direction * applied)
+        across = norm(residual * applied)
+        applied_norm = norm(applied * applied)
+        step_size = norm_now * inverse
         estimate = estimate + step_size * direction
         residual = residual - step_size * applied
-        norm_next = norm(residual * residual)
-        direction = residual + norm_next / norm_now * direction
-        norm_now = norm_next
+        if iteration + 1 < ITERS:
+            ratio = 1.0 - 2.0 * (across * inverse) + step_size * (applied_norm * inverse)
+            direction = residual + ratio * direction
     att_ref[0] = estimate[:4]
     moved = jnp.concatenate([estimate[:4]] + [pltpu.roll(estimate, KNOTS_W - j, 1)[:4] for j in range(1, 4)], axis=0)
     column = jnp.concatenate(
@@ -244,28 +254,38 @@
     terms_ref[(2 * c + 1) * NBLK : (2 * c + 2) * NBLK, :] = values - large
 
 
-def put_sources(source_ref, high_ref, low_ref):
-    source = source_ref[...]
+def put_sources(marked_ref, high_ref, low_ref):
+    source = marked_ref[...]
     high = source >> 8
     high_ref[...] = high.astype(F32)
     low_ref[...] = (source - (high << 8)).astype(F32)
 
 
-def source_normals_kernel(rows_ref, source_ref, gain_ref, out_ref, terms_ref, high_ref, low_ref, *work):
-    square = (NBLK, ROWS)
-    used = jnp.broadcast_to(rows_ref[...].astype(F32), square).T
-    mask = iota_f(square, 1) < used
-    put_sources(source_ref, high_ref, low_ref)
-    gains = [jnp.where(mask, gain_ref[NBLK * p : NBLK * p + NBLK, :], 0.0) for p in range(5)]
-    for at, (first, second) in enumerate(PAIR_LIST):
+def put_pairs(gain_ref, terms_ref, pairs):
+    gains = [gain_ref[NBLK * p : NBLK * p + NBLK, :] for p in range(5)]
+    for at, (first, second) in enumerate(pairs):
         put_terms(terms_ref, at, gains[first] * gains[second])
-    source_sums(15, terms_ref, high_ref, low_ref, out_ref, *work)
+
+
+def early_normals_kernel(marked_ref, gain_ref, out_ref, terms_ref, high_ref, low_ref, *work):
+    put_sources(marked_ref, high_ref, low_ref)
+    put_pairs(gain_ref, terms_ref, PAIR_LIST[:EARLY])
+    source_sums(EARLY, terms_ref, high_ref, low_ref, out_ref, *work)
+
+
+def rest_normals_kernel(marked_ref, gain_ref, early_ref, after_ref, out_ref, done_ref, terms_ref, high_ref, low_ref, *work):
+    copy = pltpu.make_async_copy(early_ref, out_ref.at[: HIGH * EARLY], done_ref)
+    copy.start()
+    put_sources(marked_ref, high_ref, low_ref)
+    put_pairs(gain_ref, terms_ref, PAIR_LIST[EARLY:])
+    source_sums(15 - EARLY, terms_ref, high_ref, low_ref, out_ref.at[HIGH * EARLY :], *work)
+    copy.wait()
 
 
 def source_right_kernel(
-    reply_ref, slot_ref, obs_ref, source_ref, gain_ref, out_ref, terms_ref, high_ref, low_ref, *work
+    reply_ref, slot_ref, obs_ref, marked_ref, gain_ref, out_ref, terms_ref, high_ref, low_ref, *work
 ):
-    put_sources(source_ref, high_ref, low_ref)
+    put_sources(marked_ref, high_ref, low_ref)
     place = indicator(iota_f((WINDOWS, NBLK), 0) == slot_ref[0:1, :])
     rank = slot_ref[1:2, :]
     spread = exact_dot(reply_ref[...].T, place, NN)
@@ -343,12 +363,18 @@
     return jax.ShapeDtypeStruct(shape, F32)
 
 
-def kernel_call(body, name, outs, *args, scratch=(), flops=1_000_000, in_specs=None, grant=32):
+def kernel_call(body, name, outs, *args, scratch=(), flops=1_000_000, far=(), grant=32, passed=None):
+    passed = passed or {}
+    place = [pl.ANY if at in far else pltpu.MemorySpace.VMEM for at in range(len(args))]
+    out_place = [pl.ANY if at in passed.values() else pltpu.MemorySpace.VMEM for at in range(len(jax.tree.leaves(outs)))]
+    out_specs = [pl.BlockSpec(memory_space=at) for at in out_place]
     size = sum(math.prod(a.shape) * 4 for a in args)
     return pl.pallas_call(
         body,
         out_shape=outs,
-        in_specs=in_specs or [pl.BlockSpec(memory_space=pltpu.MemorySpace.VMEM)] * len(args),
+        in_specs=[pl.BlockSpec(memory_space=at) for at in place],
+        out_specs=tuple(out_specs) if isinstance(outs, tuple) else out_specs[0],
+        input_output_aliases=passed,
         scratch_shapes=list(scratch),
         compiler_params=pltpu.CompilerParams(vmem_limit_bytes=grant * 1024 * 1024),
         cost_estimate=pl.CostEstimate(flops=flops, bytes_accessed=size, transcendentals=0),
@@ -383,47 +409,63 @@
     bins = block_bin.reshape(1, NBLK)
     rows = block_rows.reshape(1, NBLK)
     gains = jnp.transpose(src_partial, (1, 0, 2)).reshape(5 * NBLK, ROWS)
-    send, obs, slots = kernel_call(
+    send, obs, slots, marked = kernel_call(
         normals_kernel,
         "normals",
-        (f32(SLOTS, 128), f32(6 * ROWS, NBLK), f32(8, NBLK)),
+        (f32(SLOTS, 128), f32(6 * ROWS, NBLK), f32(8, NBLK), jax.ShapeDtypeStruct((NBLK, ROWS), jnp.int32)),
         bins,
         rows,
-        obs_resid,
         obs_phase,
         att_partial.reshape(4 * NBLK, ROWS),
+        obs_resid,
+        row_source,
         scratch=(
             pltpu.VMEM((1, NBLK), jnp.int32),
             pltpu.VMEM((1, NBLK), jnp.int32),
             pltpu.VMEM((NBLK, ROWS), F32),
+            pltpu.VMEM((4 * NBLK, ROWS), F32),
             pltpu.VMEM((NBLK, ROWS), F32),
-            pltpu.VMEM((4 * NBLK, ROWS), F32),
+            pltpu.VMEM((NBLK, ROWS), jnp.int32),
             pltpu.VMEM((NBLK, NBLK), F32),
-            pltpu.SemaphoreType.DMA((5,)),
+            pltpu.SemaphoreType.DMA((6,)),
         ),
-        in_specs=[pl.BlockSpec(memory_space=pl.ANY)] * 5,
+        far=range(6),
         grant=56,
     )
     got = to_windows(send.reshape(WINDOWS, CAP, 128)).reshape(SLOTS, 128)
+    early = kernel_call(
+        early_normals_kernel,
+        "early_normals",
+        f32(EARLY * HIGH, LOW),
+        marked,
+        gains,
+        scratch=segment_scratch(EARLY),
+        flops=2 * 32 * EARLY * 256 * 16384,
+    )
+    moments = kernel_call(bins_kernel, "bins", f32(FEATS, KNOTS_W), got)
     normal = kernel_call(
-        source_normals_kernel,
-        "source_normals",
+        rest_normals_kernel,
+        "rest_normals",
         f32(15 * HIGH, LOW),
-        rows,
-        row_source,
+        marked,
         gains,
-        scratch=segment_scratch(15),
-        flops=2 * 480 * 256 * 16384,
-    )
-    moments = kernel_call(bins_kernel, "bins", f32(FEATS, KNOTS_W), got)
-    attitude, reply = kernel_call(
+        early,
+        moments,
+        scratch=(pltpu.SemaphoreType.DMA, *segment_scratch(15 - EARLY)),
+        flops=2 * 32 * (15 - EARLY) * 256 * 16384,
+        far=(2, 3),
+    )
+    attitude, reply, normal = kernel_call(
         attitude_kernel,
         "attitude",
-        (f32(1, 4, KNOTS_W), f32(WINDOWS, 128)),
+        (f32(1, 4, KNOTS_W), f32(WINDOWS, 128), f32(15 * HIGH, LOW)),
         moments,
         *from_others(moments),
         got,
         jnp.asarray(knot_matrix()),
+        normal,
+        far=(6,),
+        passed={6: 2},
     )
     knots = to_windows(reply)
     factors = kernel_call(factor_kernel, "factors", f32(15 * HIGH, LOW), normal, *from_others(normal))
@@ -434,7 +476,7 @@
         knots,
         slots,
         obs,
-        row_source,
+        marked,
         gains,
         scratch=segment_scratch(5),
         flops=2 * 160 * 256 * 16384,

time: 72.2 us -> 70.7 us (0.979)
  starting transfers between devices: 38.1 us -> 29.6 us
  waiting for transfers between devices: 13.6 us -> 18.1 us
  Pallas kernels: 18.8 us -> 21.9 us
    all_to_all x2, waiting for transfers between devices: 5.02 us -> 13.4 us  [to_windows(): lax.all_to_all(values, ('src', 'win'), split_axis=0, concat_axis=0, tiled...]
    ppermute x9, starting transfers between devices: 14.1 us -> 9.26 us  [from_others(): lax.ppermute(values, 'ccd', [(at, (at + shift) % N_CCD) for at in range(N...]
    ppermute x9, waiting for transfers between devices: 8.59 us -> 4.67 us  [from_others(): lax.ppermute(values, 'ccd', [(at, (at + shift) % N_CCD) for at in range(N...]
    all_to_all x2, starting transfers between devices: 24 us -> 20.4 us  [to_windows(): lax.all_to_all(values, ('src', 'win'), split_axis=0, concat_axis=0, tiled...]
    pallas_call x7 -> x8, Pallas kernels: 18.8 us -> 21.9 us  [kernel_call(): pl.pallas_call(body, out_shape=outs, in_specs=[pl.BlockSpec(memory_space=...]
  transfers between devices with their start and end apart: 11 -> 11, of which waited for: 7 -> 5; matrix products, arithmetic and copies ran while one was open for 0% -> 0% of each run, Pallas kernels for 22% -> 22%
where the time goes in v3:
time: 70.7 us; the launch traced here: 70.4 us
  starting transfers between devices  29.6 us (42%)
  Pallas kernels  21.9 us (31%)
  waiting for transfers between devices  18.1 us (26%)
  between operations  0.79 us (1%)
    pallas_call x8, Pallas kernels, kernel_call(): pl.pallas_call(body, out_shape=outs, in_specs=[pl.BlockSpec(memory_space=...  21.9 us
    all_to_all x2, starting transfers between devices, to_windows(): lax.all_to_all(values, ('src', 'win'), split_axis=0, concat_axis=0, tiled...  20.4 us
    all_to_all x2, waiting for transfers between devices, to_windows(): lax.all_to_all(values, ('src', 'win'), split_axis=0, concat_axis=0, tiled...  13.4 us
    ppermute x9, starting transfers between devices, from_others(): lax.ppermute(values, 'ccd', [(at, (at + shift) % N_CCD) for at in range(N...  9.26 us
    ppermute x9, waiting for transfers between devices, from_others(): lax.ppermute(values, 'ccd', [(at, (at + shift) % N_CCD) for at in range(N...  4.67 us
  transfers between devices with their start and end apart: 11, of which 5 were waited for; matrix products, arithmetic and copies ran while one was open for 0% of the time, Pallas kernels for 22%

profile of v3, /device:TPU:1, one launch (start us, length us, event | category | flops | bytes accessed | tf_op | source)
XLA Modules:
  0.0 70.4 jit_solution(16408187527513373085)
XLA Ops:
  0.6 0.0 copy-start.2
  0.6 2.6 %normals.1 = (f32[256,128]{1,0:T(8,128)}, f32[768,128]{1,0:T(8,128)}, f32[8,128]{1,0:T(8,128)}, s32[128,128]{1,0:T(8,128)}) custom-call(s32[1,128]{1,0:T(1,128)} %bitcast.20, s32[1,128]{1,0:T(1,128)} %bitcast.21, f32[128,128]{1,0:T(8,128)} %refs_2_.1, f32[512,128]{1,0:T(8,128)} %bitcast.18, f32[128,128]{1,0:T(8,128)} %refs_4_.1, s32[128,128]{1,0:T(8,128)} %refs_5_.1), custom_call_target="tpu_custom_call" | custom-call | flops 1000000 | bytes 459776 | tf_op jit(solution)/shard_map/normals/pallas_call | solution.py:372
  3.3 0.0 copy-start.3
  3.3 13.3 %all-to-all-start = ((f32[64,4,128]{2,1,0:T(4,128)}), f32[64,4,128]{2,1,0:T(4,128)S(1)}, u32[]{:S(2)}, u32[]{:S(2)}) async-start(f32[64,4,128]{2,1,0:T(4,128)} %bitcast.19), calls=%async_computation | async-start | bytes 262144 | tf_op jit(solution)/shard_map/all_to_all | solution.py:405
  16.6 0.0 copy-done.2
  16.6 0.0 copy-done.3
  16.6 4.3 %early_normals.1.early_ref = f32[80,256]{1,0:T(8,128)S(1)} custom-call(s32[128,128]{1,0:T(8,128)S(1)} %copy-done.3, f32[640,128]{1,0:T(8,128)S(1)} %bitcast.15), custom_call_target="tpu_custom_call" | custom-call | flops 1342177280 | bytes 393216 | tf_op jit(solution)/shard_map/early_normals/pallas_call | solution.py:372
  20.9 5.6 %all-to-all-done = f32[64,4,128]{2,1,0:T(4,128)S(1)} async-done(((f32[64,4,128]{2,1,0:T(4,128)}), f32[64,4,128]{2,1,0:T(4,128)S(1)}, u32[]{:S(2)}, u32[]{:S(2)}) %all-to-all-start) | async-done | bytes 131104 | tf_op jit(solution)/shard_map/all_to_all | solution.py:405
  26.5 0.3 bins.1.after_ref.own_ref
  26.8 0.0 copy-start
  26.8 2.6 %collective-permute-start.2 = (f32[88,128]{1,0:T(8,128)S(1)}, f32[88,128]{1,0:T(8,128)S(1)}, u32[]{:S(2)}, u32[]{:S(2)}) collective-permute-start(f32[88,128]{1,0:T(8,128)S(1)} %bins.1.after_ref.own_ref), channel_id=1, source_target_pairs={{0,3},{1,0},{2,1},{3,2},{4,7},{5,4},{6,5},{7,6},{8,11},{9,8},{10,9... | collective-permute-start | bytes 135176 | tf_op jit(solution)/shard_map/ppermute | solution.py:400
  29.4 0.5 collective-permute-start.1
  29.9 0.6 collective-permute-start
  30.5 6.5 %rest_normals.1.rest_0_ = f32[240,256]{1,0:T(8,128)S(1)} custom-call(s32[128,128]{1,0:T(8,128)S(1)} %copy-done.3, f32[640,128]{1,0:T(8,128)S(1)} %bitcast.16, f32[80,256]{1,0:T(8,128)S(1)} %early_normals.1.early_ref, f32[88,128]{1,0:T(8,128)S(1)} %bins.1.after_ref.own_ref), custom_call_target="tpu_custom_call" | custom-call | flops 2684354560 | bytes 520192 | tf_op jit(solution)/shard_map/rest_normals/pallas_call | solution.py:372
  37.0 0.0 copy-start.1
  37.0 0.0 collective-permute-done.2.three_ref
  37.0 0.0 collective-permute-done.1.two_ref
  37.1 0.0 collective-permute-done.one_ref
  37.1 0.0 copy-done
  37.1 2.7 %attitude.1 = (f32[1,4,128]{2,1,0:T(4,128)}, f32[64,128]{1,0:T(8,128)}, f32[240,256]{1,0:T(8,128)S(1)}) custom-call(f32[88,128]{1,0:T(8,128)S(1)} %bins.1.after_ref.own_ref, f32[88,128]{1,0:T(8,128)S(1)} %collective-permute-done.one_ref, f32[88,128]{1,0:T(8,128)S(1)} %collective-permute-done.1.two_ref, ...), custom_call_target="tpu_custom_call", output_to_operand_aliasing={{2}: (6, {})} | custom-call | flops 1000000 | bytes 726016 | tf_op jit(solution)/shard_map/attitude/pallas_call | solution.py:372
  39.8 2.1 %collective-permute-start.5 = (f32[240,256]{1,0:T(8,128)S(1)}, f32[240,256]{1,0:T(8,128)S(1)}, u32[]{:S(2)}, u32[]{:S(2)}) collective-permute-start(f32[240,256]{1,0:T(8,128)S(1)} %get-tuple-element.12.own_ref), channel_id=1, source_target_pairs={{0,3},{1,0},{2,1},{3,2},{4,7},{5,4},{6,5},{7,6},{8,11},{9,8},{10,9... | collective-permute-start | bytes 737288 | tf_op jit(solution)/shard_map/ppermute | solution.py:400
  41.9 7.1 %all-to-all-start.1 = ((f32[64,1,128]{2,1,0:T(1,128)}), f32[64,1,128]{2,1,0:T(1,128)S(1)}, u32[]{:S(2)}, u32[]{:S(2)}) async-start(f32[64,1,128]{2,1,0:T(1,128)} %bitcast.9), calls=%async_computation.1 | async-start | bytes 65536 | tf_op jit(solution)/shard_map/all_to_all | solution.py:405
  48.9 0.0 copy-start.4
  49.0 1.3 %collective-permute-start.4 = (f32[240,256]{1,0:T(8,128)S(1)}, f32[240,256]{1,0:T(8,128)S(1)}, u32[]{:S(2)}, u32[]{:S(2)}) collective-permute-start(f32[240,256]{1,0:T(8,128)S(1)} %get-tuple-element.12.own_ref), channel_id=1, source_target_pairs={{0,2},{1,3},{2,0},{3,1},{4,6},{5,7},{6,4},{7,5},{8,10},{9,11},{10,... | collective-permute-start | bytes 737288 | tf_op jit(solution)/shard_map/ppermute | solution.py:400
  50.3 0.0 collective-permute-start.3
  50.3 7.9 %all-to-all-done.1 = f32[64,1,128]{2,1,0:T(1,128)S(1)} async-done(((f32[64,1,128]{2,1,0:T(1,128)}), f32[64,1,128]{2,1,0:T(1,128)S(1)}, u32[]{:S(2)}, u32[]{:S(2)}) %all-to-all-start.1) | async-done | bytes 32800 | tf_op jit(solution)/shard_map/all_to_all | solution.py:405
  58.1 0.0 copy-done.1
  58.2 0.0 copy-done.4
  58.2 4.6 %source_right.1.own_ref = f32[80,256]{1,0:T(8,128)S(1)} custom-call(f32[64,128]{1,0:T(8,128)S(1)} %bitcast.14, f32[8,128]{1,0:T(8,128)S(1)} %copy-done.4, f32[768,128]{1,0:T(8,128)S(1)} %copy-done.1, s32[128,128]{1,0:T(8,128)S(1)} %copy-done.3, f32[640,128]{1,0:T(8,128)S(1)} %bitcast.17), custom_call_target="tpu_custom_call" | custom-call | flops 1342177280 | bytes 823296 | tf_op jit(solution)/shard_map/source_right/pallas_call | solution.py:372
  62.7 0.1 collective-permute-start.8
  62.8 1.3 %collective-permute-start.7 = (f32[80,256]{1,0:T(8,128)S(1)}, f32[80,256]{1,0:T(8,128)S(1)}, u32[]{:S(2)}, u32[]{:S(2)}) collective-permute-start(f32[80,256]{1,0:T(8,128)S(1)} %source_right.1.own_ref), channel_id=1, source_target_pairs={{0,2},{1,3},{2,0},{3,1},{4,6},{5,7},{6,4},{7,5},{8,10},{9,11},{10,... | collective-permute-start | bytes 245768 | tf_op jit(solution)/shard_map/ppermute | solution.py:400
  64.2 0.0 collective-permute-done.5.three_ref
  64.2 0.8 %collective-permute-start.6 = (f32[80,256]{1,0:T(8,128)S(1)}, f32[80,256]{1,0:T(8,128)S(1)}, u32[]{:S(2)}, u32[]{:S(2)}) collective-permute-start(f32[80,256]{1,0:T(8,128)S(1)} %source_right.1.own_ref), channel_id=1, source_target_pairs={{0,1},{1,2},{2,3},{3,0},{4,5},{5,6},{6,7},{7,4},{8,9},{9,10},{10,1... | collective-permute-start | bytes 245768 | tf_op jit(solution)/shard_map/ppermute | solution.py:400
  64.9 0.0 collective-permute-done.4.two_ref
  64.9 0.0 collective-permute-done.3.one_ref
  64.9 0.1 factors.1.factor_ref
  65.0 1.1 %collective-permute-done.8.three_ref = f32[80,256]{1,0:T(8,128)S(1)} collective-permute-done((f32[80,256]{1,0:T(8,128)S(1)}, f32[80,256]{1,0:T(8,128)S(1)}, u32[]{:S(2)}, u32[]{:S(2)}) %collective-permute-start.8) | collective-permute-done | bytes 81952 | tf_op jit(solution)/shard_map/ppermute | solution.py:400
  66.1 1.6 %collective-permute-done.7.two_ref = f32[80,256]{1,0:T(8,128)S(1)} collective-permute-done((f32[80,256]{1,0:T(8,128)S(1)}, f32[80,256]{1,0:T(8,128)S(1)}, u32[]{:S(2)}, u32[]{:S(2)}) %collective-permute-start.7) | collective-permute-done | bytes 81952 | tf_op jit(solution)/shard_map/ppermute | solution.py:400
  67.7 2.0 %collective-permute-done.6.one_ref = f32[80,256]{1,0:T(8,128)S(1)} collective-permute-done((f32[80,256]{1,0:T(8,128)S(1)}, f32[80,256]{1,0:T(8,128)S(1)}, u32[]{:S(2)}, u32[]{:S(2)}) %collective-permute-start.6) | collective-permute-done | bytes 81952 | tf_op jit(solution)/shard_map/ppermute | solution.py:400
  69.7 0.7 %solve.1 = f32[5,4096]{1,0:T(8,128)} custom-call(f32[240,256]{1,0:T(8,128)S(1)} %factors.1.factor_ref, f32[80,256]{1,0:T(8,128)S(1)} %source_right.1.own_ref, f32[80,256]{1,0:T(8,128)S(1)} %collective-permute-done.6.one_ref, f32[80,256]{1,0:T(8,128)S(1)} %collective-permute-done.7.two_ref, f32[80,256]{1,0:T(8,128)S(1)} %collective-permute-done.8.three_ref), custom_call_target="tpu_custom_call" | custom-call | flops 1000000 | bytes 573440 | tf_op jit(solution)/shard_map/solve/pallas_call | solution.py:372
Async XLA Ops:
  0.6 15.9 %copy-start.2 = (f32[128,5,128]{2,0,1:T(8,128)S(1)}, f32[128,5,128]{2,0,1:T(8,128)}, u32[]{:S(2)}) copy-start(f32[128,5,128]{2,0,1:T(8,128)} %param.14) | copy-start | bytes 983044
  3.3 13.3 %copy-start.3 = (s32[128,128]{1,0:T(8,128)S(1)}, s32[128,128]{1,0:T(8,128)}, u32[]{:S(2)}) copy-start(s32[128,128]{1,0:T(8,128)} %get-tuple-element.10.marked_ref) | copy-start | bytes 196612
  3.3 23.2 %all-to-all-start = ((f32[64,4,128]{2,1,0:T(4,128)}), f32[64,4,128]{2,1,0:T(4,128)S(1)}, u32[]{:S(2)}, u32[]{:S(2)}) async-start(f32[64,4,128]{2,1,0:T(4,128)} %bitcast.19), calls=%async_computation | async-start | bytes 262144 | tf_op jit(solution)/shard_map/all_to_all | solution.py:405
  26.8 10.3 %copy-start = (bf16[120,352]{1,0:T(8,128)(2,1)S(1)}, bf16[120,352]{1,0:T(8,128)(2,1)}, u32[]{:S(2)}) copy-start(bf16[120,352]{1,0:T(8,128)(2,1)} %constant.2.clone.table_ref) | copy-start | bytes 253444
  26.8 10.2 %collective-permute-start.2 = (f32[88,128]{1,0:T(8,128)S(1)}, f32[88,128]{1,0:T(8,128)S(1)}, u32[]{:S(2)}, u32[]{:S(2)}) collective-permute-start(f32[88,128]{1,0:T(8,128)S(1)} %bins.1.after_ref.own_ref), channel_id=1, source_target_pairs={{0,3},{1,0},{2,1},{3,2},{4,7},{5,4},{6,5},{7,6},{8,11},{9,8},{10,9... | collective-permute-start | bytes 135176 | tf_op jit(solution)/shard_map/ppermute | solution.py:400
  29.4 7.7 %collective-permute-start.1 = (f32[88,128]{1,0:T(8,128)S(1)}, f32[88,128]{1,0:T(8,128)S(1)}, u32[]{:S(2)}, u32[]{:S(2)}) collective-permute-start(f32[88,128]{1,0:T(8,128)S(1)} %bins.1.after_ref.own_ref), channel_id=1, source_target_pairs={{0,2},{1,3},{2,0},{3,1},{4,6},{5,7},{6,4},{7,5},{8,10},{9,11},{10,... | collective-permute-start | bytes 135176 | tf_op jit(solution)/shard_map/ppermute | solution.py:400
  29.9 7.2 %collective-permute-start = (f32[88,128]{1,0:T(8,128)S(1)}, f32[88,128]{1,0:T(8,128)S(1)}, u32[]{:S(2)}, u32[]{:S(2)}) collective-permute-start(f32[88,128]{1,0:T(8,128)S(1)} %bins.1.after_ref.own_ref), channel_id=1, source_target_pairs={{0,1},{1,2},{2,3},{3,0},{4,5},{5,6},{6,7},{7,4},{8,9},{9,10},{10,1... | collective-permute-start | bytes 135176 | tf_op jit(solution)/shard_map/ppermute | solution.py:400
  37.0 21.1 %copy-start.1 = (f32[768,128]{1,0:T(8,128)S(1)}, f32[768,128]{1,0:T(8,128)}, u32[]{:S(2)}) copy-start(f32[768,128]{1,0:T(8,128)} %get-tuple-element.15.obs_ref) | copy-start | bytes 1179652
  39.8 24.4 %collective-permute-start.5 = (f32[240,256]{1,0:T(8,128)S(1)}, f32[240,256]{1,0:T(8,128)S(1)}, u32[]{:S(2)}, u32[]{:S(2)}) collective-permute-start(f32[240,256]{1,0:T(8,128)S(1)} %get-tuple-element.12.own_ref), channel_id=1, source_target_pairs={{0,3},{1,0},{2,1},{3,2},{4,7},{5,4},{6,5},{7,6},{8,11},{9,8},{10,9... | collective-permute-start | bytes 737288 | tf_op jit(solution)/shard_map/ppermute | solution.py:400
  41.9 16.3 %all-to-all-start.1 = ((f32[64,1,128]{2,1,0:T(1,128)}), f32[64,1,128]{2,1,0:T(1,128)S(1)}, u32[]{:S(2)}, u32[]{:S(2)}) async-start(f32[64,1,128]{2,1,0:T(1,128)} %bitcast.9), calls=%async_computation.1 | async-start | bytes 65536 | tf_op jit(solution)/shard_map/all_to_all | solution.py:405
  48.9 9.2 %copy-start.4 = (f32[8,128]{1,0:T(8,128)S(1)}, f32[8,128]{1,0:T(8,128)}, u32[]{:S(2)}) copy-start(f32[8,128]{1,0:T(8,128)} %get-tuple-element.14.slot_ref) | copy-start | bytes 12292
  49.0 16.0 %collective-permute-start.4 = (f32[240,256]{1,0:T(8,128)S(1)}, f32[240,256]{1,0:T(8,128)S(1)}, u32[]{:S(2)}, u32[]{:S(2)}) collective-permute-start(f32[240,256]{1,0:T(8,128)S(1)} %get-tuple-element.12.own_ref), channel_id=1, source_target_pairs={{0,2},{1,3},{2,0},{3,1},{4,6},{5,7},{6,4},{7,5},{8,10},{9,11},{10,... | collective-permute-start | bytes 737288 | tf_op jit(solution)/shard_map/ppermute | solution.py:400
  50.3 14.7 %collective-permute-start.3 = (f32[240,256]{1,0:T(8,128)S(1)}, f32[240,256]{1,0:T(8,128)S(1)}, u32[]{:S(2)}, u32[]{:S(2)}) collective-permute-start(f32[240,256]{1,0:T(8,128)S(1)} %get-tuple-element.12.own_ref), channel_id=1, source_target_pairs={{0,1},{1,2},{2,3},{3,0},{4,5},{5,6},{6,7},{7,4},{8,9},{9,10},{10,1... | collective-permute-start | bytes 737288 | tf_op jit(solution)/shard_map/ppermute | solution.py:400
  62.7 3.4 %collective-permute-start.8 = (f32[80,256]{1,0:T(8,128)S(1)}, f32[80,256]{1,0:T(8,128)S(1)}, u32[]{:S(2)}, u32[]{:S(2)}) collective-permute-start(f32[80,256]{1,0:T(8,128)S(1)} %source_right.1.own_ref), channel_id=1, source_target_pairs={{0,3},{1,0},{2,1},{3,2},{4,7},{5,4},{6,5},{7,6},{8,11},{9,8},{10,9... | collective-permute-start | bytes 245768 | tf_op jit(solution)/shard_map/ppermute | solution.py:400
  62.8 4.9 %collective-permute-start.7 = (f32[80,256]{1,0:T(8,128)S(1)}, f32[80,256]{1,0:T(8,128)S(1)}, u32[]{:S(2)}, u32[]{:S(2)}) collective-permute-start(f32[80,256]{1,0:T(8,128)S(1)} %source_right.1.own_ref), channel_id=1, source_target_pairs={{0,2},{1,3},{2,0},{3,1},{4,6},{5,7},{6,4},{7,5},{8,10},{9,11},{10,... | collective-permute-start | bytes 245768 | tf_op jit(solution)/shard_map/ppermute | solution.py:400
  64.2 5.5 %collective-permute-start.6 = (f32[80,256]{1,0:T(8,128)S(1)}, f32[80,256]{1,0:T(8,128)S(1)}, u32[]{:S(2)}, u32[]{:S(2)}) collective-permute-start(f32[80,256]{1,0:T(8,128)S(1)} %source_right.1.own_ref), channel_id=1, source_target_pairs={{0,1},{1,2},{2,3},{3,0},{4,5},{5,6},{6,7},{7,4},{8,9},{9,10},{10,1... | collective-permute-start | bytes 245768 | tf_op jit(solution)/shard_map/ppermute | solution.py:400

commit v4 on v3

--- a/solution.py
+++ b/solution.py
@@ -22,7 +22,6 @@
 HIGH = 16
 LOW = 256
 STEP_BLOCKS = 16
-EARLY = 5
 STEPS = NBLK // STEP_BLOCKS
 
 KNOT_PRIOR = 1.0
@@ -150,14 +149,14 @@
     send_ref[...] = exact_dot(pay_ref[...], place, NT, swap=True)
 
 
-def bins_kernel(got_ref, out_ref):
+def bins_kernel(got_ref, after_ref, out_ref):
+    del after_ref
     got = got_ref[...].T
     place = indicator(iota_f((KNOTS_W, SLOTS), 0) == got[BIN_AT : BIN_AT + 1, :])
     out_ref[...] = exact_dot(got[:FEATS], place, NT)
 
 
-def attitude_kernel(own_ref, one_ref, two_ref, three_ref, got_ref, table_ref, *rest):
-    att_ref, reply_ref = rest[1:3]
+def attitude_kernel(own_ref, one_ref, two_ref, three_ref, got_ref, table_ref, att_ref, reply_ref):
     total = ((own_ref[...] + two_ref[...]) + (one_ref[...] + three_ref[...])) * (1.0 / 36.0)
     moved = jnp.concatenate([total] + [pltpu.roll(total, l, 1) for l in range(1, 4)], axis=0)
     band = exact_dot(moved, table_ref[...], NN, swap=True)
@@ -261,25 +260,12 @@
     low_ref[...] = (source - (high << 8)).astype(F32)
 
 
-def put_pairs(gain_ref, terms_ref, pairs):
+def source_normals_kernel(marked_ref, gain_ref, out_ref, terms_ref, high_ref, low_ref, *work):
+    put_sources(marked_ref, high_ref, low_ref)
     gains = [gain_ref[NBLK * p : NBLK * p + NBLK, :] for p in range(5)]
-    for at, (first, second) in enumerate(pairs):
+    for at, (first, second) in enumerate(PAIR_LIST):
         put_terms(terms_ref, at, gains[first] * gains[second])
-
-
-def early_normals_kernel(marked_ref, gain_ref, out_ref, terms_ref, high_ref, low_ref, *work):
-    put_sources(marked_ref, high_ref, low_ref)
-    put_pairs(gain_ref, terms_ref, PAIR_LIST[:EARLY])
-    source_sums(EARLY, terms_ref, high_ref, low_ref, out_ref, *work)
-
-
-def rest_normals_kernel(marked_ref, gain_ref, early_ref, after_ref, out_ref, done_ref, terms_ref, high_ref, low_ref, *work):
-    copy = pltpu.make_async_copy(early_ref, out_ref.at[: HIGH * EARLY], done_ref)
-    copy.start()
-    put_sources(marked_ref, high_ref, low_ref)
-    put_pairs(gain_ref, terms_ref, PAIR_LIST[EARLY:])
-    source_sums(15 - EARLY, terms_ref, high_ref, low_ref, out_ref.at[HIGH * EARLY :], *work)
-    copy.wait()
+    source_sums(15, terms_ref, high_ref, low_ref, out_ref, *work)
 
 
 def source_right_kernel(
@@ -433,39 +419,24 @@
         grant=56,
     )
     got = to_windows(send.reshape(WINDOWS, CAP, 128)).reshape(SLOTS, 128)
-    early = kernel_call(
-        early_normals_kernel,
-        "early_normals",
-        f32(EARLY * HIGH, LOW),
-        marked,
-        gains,
-        scratch=segment_scratch(EARLY),
-        flops=2 * 32 * EARLY * 256 * 16384,
-    )
-    moments = kernel_call(bins_kernel, "bins", f32(FEATS, KNOTS_W), got)
     normal = kernel_call(
-        rest_normals_kernel,
-        "rest_normals",
+        source_normals_kernel,
+        "source_normals",
         f32(15 * HIGH, LOW),
         marked,
         gains,
-        early,
-        moments,
-        scratch=(pltpu.SemaphoreType.DMA, *segment_scratch(15 - EARLY)),
-        flops=2 * 32 * (15 - EARLY) * 256 * 16384,
-        far=(2, 3),
-    )
-    attitude, reply, normal = kernel_call(
+        scratch=segment_scratch(15),
+        flops=2 * 480 * 256 * 16384,
+    )
+    moments = kernel_call(bins_kernel, "bins", f32(FEATS, KNOTS_W), got, normal, far=(1,))
+    attitude, reply = kernel_call(
         attitude_kernel,
         "attitude",
-        (f32(1, 4, KNOTS_W), f32(WINDOWS, 128), f32(15 * HIGH, LOW)),
+        (f32(1, 4, KNOTS_W), f32(WINDOWS, 128)),
         moments,
         *from_others(moments),
         got,
         jnp.asarray(knot_matrix()),
-        normal,
-        far=(6,),
-        passed={6: 2},
     )
     knots = to_windows(reply)
     factors = kernel_call(factor_kernel, "factors", f32(15 * HIGH, LOW), normal, *from_others(normal))

time: 70.7 us -> 70.7 us (level)
  starting transfers between devices: 29.6 us -> 37.7 us
  waiting for transfers between devices: 18.1 us -> 14 us
  Pallas kernels: 21.9 us -> 18 us
    all_to_all x2, waiting for transfers between devices: 13.4 us -> 5.39 us  [to_windows(): lax.all_to_all(values, ('src', 'win'), split_axis=0, concat_axis=0, tiled...]
    ppermute x9, starting transfers between devices: 9.26 us -> 14.4 us  [from_others(): lax.ppermute(values, 'ccd', [(at, (at + shift) % N_CCD) for at in range(N...]
    ppermute x9, waiting for transfers between devices: 4.67 us -> 8.59 us  [from_others(): lax.ppermute(values, 'ccd', [(at, (at + shift) % N_CCD) for at in range(N...]
    pallas_call x8 -> x7, Pallas kernels: 21.9 us -> 18 us  [kernel_call(): pl.pallas_call(body, out_shape=outs, in_specs=[pl.BlockSpec(memory_space=...]
    all_to_all x2, starting transfers between devices: 20.4 us -> 23.3 us  [to_windows(): lax.all_to_all(values, ('src', 'win'), split_axis=0, concat_axis=0, tiled...]
  transfers between devices with their start and end apart: 11 -> 11, of which waited for: 5 -> 8; matrix products, arithmetic and copies ran while one was open for 0% -> 0% of each run, Pallas kernels for 22% -> 21%
where the time goes in v4:
time: 70.7 us; the launch traced here: 70.4 us
  starting transfers between devices  37.7 us (53%)
  Pallas kernels  18 us (25%)
  waiting for transfers between devices  14 us (20%)
  between operations  0.73 us (1%)
    all_to_all x2, starting transfers between devices, to_windows(): lax.all_to_all(values, ('src', 'win'), split_axis=0, concat_axis=0, tiled...  23.3 us
    pallas_call x7, Pallas kernels, kernel_call(): pl.pallas_call(body, out_shape=outs, in_specs=[pl.BlockSpec(memory_space=...  18 us
    ppermute x9, starting transfers between devices, from_others(): lax.ppermute(values, 'ccd', [(at, (at + shift) % N_CCD) for at in range(N...  14.4 us
    ppermute x9, waiting for transfers between devices, from_others(): lax.ppermute(values, 'ccd', [(at, (at + shift) % N_CCD) for at in range(N...  8.59 us
    all_to_all x2, waiting for transfers between devices, to_windows(): lax.all_to_all(values, ('src', 'win'), split_axis=0, concat_axis=0, tiled...  5.39 us
  transfers between devices with their start and end apart: 11, of which 8 were waited for; matrix products, arithmetic and copies ran while one was open for 0% of the time, Pallas kernels for 21%

profile of v4, /device:TPU:1, one launch (start us, length us, event | category | flops | bytes accessed | tf_op | source)
XLA Modules:
  0.0 70.4 jit_solution(663184148920218314)
XLA Ops:
  0.6 0.0 copy-start.2
  0.6 2.6 %normals.1 = (f32[256,128]{1,0:T(8,128)}, f32[768,128]{1,0:T(8,128)}, f32[8,128]{1,0:T(8,128)}, s32[128,128]{1,0:T(8,128)}) custom-call(s32[1,128]{1,0:T(1,128)} %bitcast.19, s32[1,128]{1,0:T(1,128)} %bitcast.20, f32[128,128]{1,0:T(8,128)} %refs_2_.1, f32[512,128]{1,0:T(8,128)} %bitcast.17, f32[128,128]{1,0:T(8,128)} %refs_4_.1, s32[128,128]{1,0:T(8,128)} %refs_5_.1), custom_call_target="tpu_custom_call" | custom-call | flops 1000000 | bytes 459776 | tf_op jit(solution)/shard_map/normals/pallas_call | solution.py:358
  3.3 0.0 copy-start.3
  3.3 13.3 %all-to-all-start = ((f32[64,4,128]{2,1,0:T(4,128)}), f32[64,4,128]{2,1,0:T(4,128)S(1)}, u32[]{:S(2)}, u32[]{:S(2)}) async-start(f32[64,4,128]{2,1,0:T(4,128)} %bitcast.18), calls=%async_computation | async-start | bytes 262144 | tf_op jit(solution)/shard_map/all_to_all | solution.py:391
  16.6 0.0 copy-done.2
  16.6 0.0 copy-done.3
  16.6 7.0 %source_normals.1.after_ref.own_ref = f32[240,256]{1,0:T(8,128)S(1)} custom-call(s32[128,128]{1,0:T(8,128)S(1)} %copy-done.3, f32[640,128]{1,0:T(8,128)S(1)} %bitcast.15), custom_call_target="tpu_custom_call" | custom-call | flops 4026531840 | bytes 393216 | tf_op jit(solution)/shard_map/source_normals/pallas_call | solution.py:358
  23.6 2.6 %collective-permute-start.5 = (f32[240,256]{1,0:T(8,128)S(1)}, f32[240,256]{1,0:T(8,128)S(1)}, u32[]{:S(2)}, u32[]{:S(2)}) collective-permute-start(f32[240,256]{1,0:T(8,128)S(1)} %source_normals.1.after_ref.own_ref), channel_id=1, source_target_pairs={{0,3},{1,0},{2,1},{3,2},{4,7},{5,4},{6,5},{7,6},{8,11},{9,8},{10,9... | collective-permute-start | bytes 737288 | tf_op jit(solution)/shard_map/ppermute | solution.py:386
  26.1 0.4 all-to-all-done
  26.5 0.0 copy-start
  26.5 0.0 copy-start.1
  26.5 0.3 bins.1.own_ref
  26.8 2.6 %collective-permute-start.2 = (f32[88,128]{1,0:T(8,128)S(1)}, f32[88,128]{1,0:T(8,128)S(1)}, u32[]{:S(2)}, u32[]{:S(2)}) collective-permute-start(f32[88,128]{1,0:T(8,128)S(1)} %bins.1.own_ref), channel_id=1, source_target_pairs={{0,3},{1,0},{2,1},{3,2},{4,7},{5,4},{6,5},{7,6},{8,11},{9,8},{10,9... | collective-permute-start | bytes 135176 | tf_op jit(solution)/shard_map/ppermute | solution.py:386
  29.3 0.5 collective-permute-start.1
  29.9 0.6 collective-permute-start
  30.5 1.9 %collective-permute-done.2.three_ref = f32[88,128]{1,0:T(8,128)S(1)} collective-permute-done((f32[88,128]{1,0:T(8,128)S(1)}, f32[88,128]{1,0:T(8,128)S(1)}, u32[]{:S(2)}, u32[]{:S(2)}) %collective-permute-start.2) | collective-permute-done | bytes 45088 | tf_op jit(solution)/shard_map/ppermute | solution.py:386
  32.3 1.4 %collective-permute-done.1.two_ref = f32[88,128]{1,0:T(8,128)S(1)} collective-permute-done((f32[88,128]{1,0:T(8,128)S(1)}, f32[88,128]{1,0:T(8,128)S(1)}, u32[]{:S(2)}, u32[]{:S(2)}) %collective-permute-start.1) | collective-permute-done | bytes 45088 | tf_op jit(solution)/shard_map/ppermute | solution.py:386
  33.8 0.5 collective-permute-done.one_ref
  34.2 0.0 copy-done
  34.2 2.7 %attitude.1 = (f32[1,4,128]{2,1,0:T(4,128)}, f32[64,128]{1,0:T(8,128)}) custom-call(f32[88,128]{1,0:T(8,128)S(1)} %bins.1.own_ref, f32[88,128]{1,0:T(8,128)S(1)} %collective-permute-done.one_ref, f32[88,128]{1,0:T(8,128)S(1)} %collective-permute-done.1.two_ref, f32[88,128]{1,0:T(8,128)S(1)} %collective-permute-done.2.three_ref, f32[256,128]{1,0:T(8,128)S(1)} %bitcast.13, ...), custom_call_target="tpu_custom_call" | custom-call | flops 1000000 | bytes 480256 | tf_op jit(solution)/shard_map/attitude/pallas_call | solution.py:358
  37.0 10.0 %all-to-all-start.1 = ((f32[64,1,128]{2,1,0:T(1,128)}), f32[64,1,128]{2,1,0:T(1,128)S(1)}, u32[]{:S(2)}, u32[]{:S(2)}) async-start(f32[64,1,128]{2,1,0:T(1,128)} %bitcast.8), calls=%async_computation.1 | async-start | bytes 65536 | tf_op jit(solution)/shard_map/all_to_all | solution.py:391
  47.0 0.0 copy-start.4
  47.0 2.0 %collective-permute-start.4 = (f32[240,256]{1,0:T(8,128)S(1)}, f32[240,256]{1,0:T(8,128)S(1)}, u32[]{:S(2)}, u32[]{:S(2)}) collective-permute-start(f32[240,256]{1,0:T(8,128)S(1)} %source_normals.1.after_ref.own_ref), channel_id=1, source_target_pairs={{0,2},{1,3},{2,0},{3,1},{4,6},{5,7},{6,4},{7,5},{8,10},{9,11},{10,... | collective-permute-start | bytes 737288 | tf_op jit(solution)/shard_map/ppermute | solution.py:386
  49.0 2.0 %collective-permute-start.3 = (f32[240,256]{1,0:T(8,128)S(1)}, f32[240,256]{1,0:T(8,128)S(1)}, u32[]{:S(2)}, u32[]{:S(2)}) collective-permute-start(f32[240,256]{1,0:T(8,128)S(1)} %source_normals.1.after_ref.own_ref), channel_id=1, source_target_pairs={{0,1},{1,2},{2,3},{3,0},{4,5},{5,6},{6,7},{7,4},{8,9},{9,10},{10,1... | collective-permute-start | bytes 737288 | tf_op jit(solution)/shard_map/ppermute | solution.py:386
  51.0 5.0 %all-to-all-done.1 = f32[64,1,128]{2,1,0:T(1,128)S(1)} async-done(((f32[64,1,128]{2,1,0:T(1,128)}), f32[64,1,128]{2,1,0:T(1,128)S(1)}, u32[]{:S(2)}, u32[]{:S(2)}) %all-to-all-start.1) | async-done | bytes 32800 | tf_op jit(solution)/shard_map/all_to_all | solution.py:391
  56.0 0.0 copy-done.1
  56.0 0.0 copy-done.4
  56.0 4.6 %source_right.1.own_ref = f32[80,256]{1,0:T(8,128)S(1)} custom-call(f32[64,128]{1,0:T(8,128)S(1)} %bitcast.14, f32[8,128]{1,0:T(8,128)S(1)} %copy-done.4, f32[768,128]{1,0:T(8,128)S(1)} %copy-done.1, s32[128,128]{1,0:T(8,128)S(1)} %copy-done.3, f32[640,128]{1,0:T(8,128)S(1)} %bitcast.16), custom_call_target="tpu_custom_call" | custom-call | flops 1342177280 | bytes 823296 | tf_op jit(solution)/shard_map/source_right/pallas_call | solution.py:358
  60.6 3.5 %collective-permute-start.8 = (f32[80,256]{1,0:T(8,128)S(1)}, f32[80,256]{1,0:T(8,128)S(1)}, u32[]{:S(2)}, u32[]{:S(2)}) collective-permute-start(f32[80,256]{1,0:T(8,128)S(1)} %source_right.1.own_ref), channel_id=1, source_target_pairs={{0,3},{1,0},{2,1},{3,2},{4,7},{5,4},{6,5},{7,6},{8,11},{9,8},{10,9... | collective-permute-start | bytes 245768 | tf_op jit(solution)/shard_map/ppermute | solution.py:386
  64.1 0.2 collective-permute-start.7
  64.3 0.0 collective-permute-done.5.three_ref
  64.3 0.5 collective-permute-start.6
  64.8 0.0 collective-permute-done.4.two_ref
  64.8 0.0 collective-permute-done.3.one_ref
  64.8 0.1 factors.1.factor_ref
  64.9 1.6 %collective-permute-done.8.three_ref = f32[80,256]{1,0:T(8,128)S(1)} collective-permute-done((f32[80,256]{1,0:T(8,128)S(1)}, f32[80,256]{1,0:T(8,128)S(1)}, u32[]{:S(2)}, u32[]{:S(2)}) %collective-permute-start.8) | collective-permute-done | bytes 81952 | tf_op jit(solution)/shard_map/ppermute | solution.py:386
  66.5 2.5 %collective-permute-done.7.two_ref = f32[80,256]{1,0:T(8,128)S(1)} collective-permute-done((f32[80,256]{1,0:T(8,128)S(1)}, f32[80,256]{1,0:T(8,128)S(1)}, u32[]{:S(2)}, u32[]{:S(2)}) %collective-permute-start.7) | collective-permute-done | bytes 81952 | tf_op jit(solution)/shard_map/ppermute | solution.py:386
  69.0 0.7 %collective-permute-done.6.one_ref = f32[80,256]{1,0:T(8,128)S(1)} collective-permute-done((f32[80,256]{1,0:T(8,128)S(1)}, f32[80,256]{1,0:T(8,128)S(1)}, u32[]{:S(2)}, u32[]{:S(2)}) %collective-permute-start.6) | collective-permute-done | bytes 81952 | tf_op jit(solution)/shard_map/ppermute | solution.py:386
  69.7 0.7 %solve.1 = f32[5,4096]{1,0:T(8,128)} custom-call(f32[240,256]{1,0:T(8,128)S(1)} %factors.1.factor_ref, f32[80,256]{1,0:T(8,128)S(1)} %source_right.1.own_ref, f32[80,256]{1,0:T(8,128)S(1)} %collective-permute-done.6.one_ref, f32[80,256]{1,0:T(8,128)S(1)} %collective-permute-done.7.two_ref, f32[80,256]{1,0:T(8,128)S(1)} %collective-permute-done.8.three_ref), custom_call_target="tpu_custom_call" | custom-call | flops 1000000 | bytes 573440 | tf_op jit(solution)/shard_map/solve/pallas_call | solution.py:358
Async XLA Ops:
  0.6 15.9 %copy-start.2 = (f32[128,5,128]{2,0,1:T(8,128)S(1)}, f32[128,5,128]{2,0,1:T(8,128)}, u32[]{:S(2)}) copy-start(f32[128,5,128]{2,0,1:T(8,128)} %param.14) | copy-start | bytes 983044
  3.3 13.3 %copy-start.3 = (s32[128,128]{1,0:T(8,128)S(1)}, s32[128,128]{1,0:T(8,128)}, u32[]{:S(2)}) copy-start(s32[128,128]{1,0:T(8,128)} %get-tuple-element.9.marked_ref) | copy-start | bytes 196612
  3.3 23.2 %all-to-all-start = ((f32[64,4,128]{2,1,0:T(4,128)}), f32[64,4,128]{2,1,0:T(4,128)S(1)}, u32[]{:S(2)}, u32[]{:S(2)}) async-start(f32[64,4,128]{2,1,0:T(4,128)} %bitcast.18), calls=%async_computation | async-start | bytes 262144 | tf_op jit(solution)/shard_map/all_to_all | solution.py:391
  23.6 40.7 %collective-permute-start.5 = (f32[240,256]{1,0:T(8,128)S(1)}, f32[240,256]{1,0:T(8,128)S(1)}, u32[]{:S(2)}, u32[]{:S(2)}) collective-permute-start(f32[240,256]{1,0:T(8,128)S(1)} %source_normals.1.after_ref.own_ref), channel_id=1, source_target_pairs={{0,3},{1,0},{2,1},{3,2},{4,7},{5,4},{6,5},{7,6},{8,11},{9,8},{10,9... | collective-permute-start | bytes 737288 | tf_op jit(solution)/shard_map/ppermute | solution.py:386
  26.5 7.7 %copy-start = (bf16[120,352]{1,0:T(8,128)(2,1)S(1)}, bf16[120,352]{1,0:T(8,128)(2,1)}, u32[]{:S(2)}) copy-start(bf16[120,352]{1,0:T(8,128)(2,1)} %constant.2.clone.table_ref) | copy-start | bytes 253444
  26.5 29.5 %copy-start.1 = (f32[768,128]{1,0:T(8,128)S(1)}, f32[768,128]{1,0:T(8,128)}, u32[]{:S(2)}) copy-start(f32[768,128]{1,0:T(8,128)} %get-tuple-element.13.obs_ref) | copy-start | bytes 1179652
  26.8 5.5 %collective-permute-start.2 = (f32[88,128]{1,0:T(8,128)S(1)}, f32[88,128]{1,0:T(8,128)S(1)}, u32[]{:S(2)}, u32[]{:S(2)}) collective-permute-start(f32[88,128]{1,0:T(8,128)S(1)} %bins.1.own_ref), channel_id=1, source_target_pairs={{0,3},{1,0},{2,1},{3,2},{4,7},{5,4},{6,5},{7,6},{8,11},{9,8},{10,9... | collective-permute-start | bytes 135176 | tf_op jit(solution)/shard_map/ppermute | solution.py:386
  29.3 4.4 %collective-permute-start.1 = (f32[88,128]{1,0:T(8,128)S(1)}, f32[88,128]{1,0:T(8,128)S(1)}, u32[]{:S(2)}, u32[]{:S(2)}) collective-permute-start(f32[88,128]{1,0:T(8,128)S(1)} %bins.1.own_ref), channel_id=1, source_target_pairs={{0,2},{1,3},{2,0},{3,1},{4,6},{5,7},{6,4},{7,5},{8,10},{9,11},{10,... | collective-permute-start | bytes 135176 | tf_op jit(solution)/shard_map/ppermute | solution.py:386
  29.9 4.4 %collective-permute-start = (f32[88,128]{1,0:T(8,128)S(1)}, f32[88,128]{1,0:T(8,128)S(1)}, u32[]{:S(2)}, u32[]{:S(2)}) collective-permute-start(f32[88,128]{1,0:T(8,128)S(1)} %bins.1.own_ref), channel_id=1, source_target_pairs={{0,1},{1,2},{2,3},{3,0},{4,5},{5,6},{6,7},{7,4},{8,9},{9,10},{10,1... | collective-permute-start | bytes 135176 | tf_op jit(solution)/shard_map/ppermute | solution.py:386
  37.0 19.1 %all-to-all-start.1 = ((f32[64,1,128]{2,1,0:T(1,128)}), f32[64,1,128]{2,1,0:T(1,128)S(1)}, u32[]{:S(2)}, u32[]{:S(2)}) async-start(f32[64,1,128]{2,1,0:T(1,128)} %bitcast.8), calls=%async_computation.1 | async-start | bytes 65536 | tf_op jit(solution)/shard_map/all_to_all | solution.py:391
  47.0 9.1 %copy-start.4 = (f32[8,128]{1,0:T(8,128)S(1)}, f32[8,128]{1,0:T(8,128)}, u32[]{:S(2)}) copy-start(f32[8,128]{1,0:T(8,128)} %get-tuple-element.12.slot_ref) | copy-start | bytes 12292
  47.0 17.8 %collective-permute-start.4 = (f32[240,256]{1,0:T(8,128)S(1)}, f32[240,256]{1,0:T(8,128)S(1)}, u32[]{:S(2)}, u32[]{:S(2)}) collective-permute-start(f32[240,256]{1,0:T(8,128)S(1)} %source_normals.1.after_ref.own_ref), channel_id=1, source_target_pairs={{0,2},{1,3},{2,0},{3,1},{4,6},{5,7},{6,4},{7,5},{8,10},{9,11},{10,... | collective-permute-start | bytes 737288 | tf_op jit(solution)/shard_map/ppermute | solution.py:386
  49.0 15.8 %collective-permute-start.3 = (f32[240,256]{1,0:T(8,128)S(1)}, f32[240,256]{1,0:T(8,128)S(1)}, u32[]{:S(2)}, u32[]{:S(2)}) collective-permute-start(f32[240,256]{1,0:T(8,128)S(1)} %source_normals.1.after_ref.own_ref), channel_id=1, source_target_pairs={{0,1},{1,2},{2,3},{3,0},{4,5},{5,6},{6,7},{7,4},{8,9},{9,10},{10,1... | collective-permute-start | bytes 737288 | tf_op jit(solution)/shard_map/ppermute | solution.py:386
  60.6 5.9 %collective-permute-start.8 = (f32[80,256]{1,0:T(8,128)S(1)}, f32[80,256]{1,0:T(8,128)S(1)}, u32[]{:S(2)}, u32[]{:S(2)}) collective-permute-start(f32[80,256]{1,0:T(8,128)S(1)} %source_right.1.own_ref), channel_id=1, source_target_pairs={{0,3},{1,0},{2,1},{3,2},{4,7},{5,4},{6,5},{7,6},{8,11},{9,8},{10,9... | collective-permute-start | bytes 245768 | tf_op jit(solution)/shard_map/ppermute | solution.py:386
  64.1 4.9 %collective-permute-start.7 = (f32[80,256]{1,0:T(8,128)S(1)}, f32[80,256]{1,0:T(8,128)S(1)}, u32[]{:S(2)}, u32[]{:S(2)}) collective-permute-start(f32[80,256]{1,0:T(8,128)S(1)} %source_right.1.own_ref), channel_id=1, source_target_pairs={{0,2},{1,3},{2,0},{3,1},{4,6},{5,7},{6,4},{7,5},{8,10},{9,11},{10,... | collective-permute-start | bytes 245768 | tf_op jit(solution)/shard_map/ppermute | solution.py:386
  64.3 5.4 %collective-permute-start.6 = (f32[80,256]{1,0:T(8,128)S(1)}, f32[80,256]{1,0:T(8,128)S(1)}, u32[]{:S(2)}, u32[]{:S(2)}) collective-permute-start(f32[80,256]{1,0:T(8,128)S(1)} %source_right.1.own_ref), channel_id=1, source_target_pairs={{0,1},{1,2},{2,3},{3,0},{4,5},{5,6},{6,7},{7,4},{8,9},{9,10},{10,1... | collective-permute-start | bytes 245768 | tf_op jit(solution)/shard_map/ppermute | solution.py:386

commit v5 on v4

--- a/solution.py
+++ b/solution.py
@@ -153,11 +153,13 @@
     del after_ref
     got = got_ref[...].T
     place = indicator(iota_f((KNOTS_W, SLOTS), 0) == got[BIN_AT : BIN_AT + 1, :])
-    out_ref[...] = exact_dot(got[:FEATS], place, NT)
-
-
-def attitude_kernel(own_ref, one_ref, two_ref, three_ref, got_ref, table_ref, att_ref, reply_ref):
-    total = ((own_ref[...] + two_ref[...]) + (one_ref[...] + three_ref[...])) * (1.0 / 36.0)
+    moments = exact_dot(got[:FEATS], place, NT)
+    for at in range(N_CCD):
+        out_ref[at] = moments
+
+
+def attitude_kernel(parts_ref, got_ref, table_ref, att_ref, reply_ref):
+    total = ((parts_ref[0] + parts_ref[1]) + (parts_ref[2] + parts_ref[3])) * (1.0 / 36.0)
     moved = jnp.concatenate([total] + [pltpu.roll(total, l, 1) for l in range(1, 4)], axis=0)
     band = exact_dot(moved, table_ref[...], NN, swap=True)
     groups = [band[8 * at : 8 * at + 8] for at in range(14)]
@@ -299,7 +301,9 @@
     values = values.T
     for p in range(5):
         put_terms(terms_ref, p, gain_ref[NBLK * p : NBLK * p + NBLK, :] * values)
-    source_sums(5, terms_ref, high_ref, low_ref, out_ref, *work)
+    source_sums(5, terms_ref, high_ref, low_ref, out_ref.at[0], *work)
+    for at in range(1, N_CCD):
+        out_ref[at] = out_ref[0]
 
 
 def factor_kernel(own_ref, one_ref, two_ref, three_ref, out_ref):
@@ -324,14 +328,14 @@
         out_ref[HIGH * at : HIGH * at + HIGH, :] = lower[second, first]
 
 
-def solve_kernel(factor_ref, own_ref, one_ref, two_ref, three_ref, out_ref):
+def solve_kernel(factor_ref, parts_ref, out_ref):
     lower = {}
     for at, (first, second) in enumerate(PAIR_LIST):
         lower[second, first] = factor_ref[HIGH * at : HIGH * at + HIGH, :]
     values = []
     for row in range(5):
         rows = slice(HIGH * row, HIGH * row + HIGH)
-        running = (own_ref[rows, :] + two_ref[rows, :]) + (one_ref[rows, :] + three_ref[rows, :])
+        running = (parts_ref[0, rows, :] + parts_ref[1, rows, :]) + (parts_ref[2, rows, :] + parts_ref[3, rows, :])
         for before in range(row):
             running = running - lower[row, before] * values[before]
         values.append(running * lower[row, row])
@@ -385,6 +389,10 @@
     return [
         lax.ppermute(values, "ccd", [(at, (at + shift) % N_CCD) for at in range(N_CCD)]) for shift in range(1, N_CCD)
     ]
+
+
+def among_ccd(copies):
+    return lax.all_to_all(copies, "ccd", split_axis=0, concat_axis=0, tiled=True)
 
 
 def to_windows(values):
@@ -428,13 +436,12 @@
         scratch=segment_scratch(15),
         flops=2 * 480 * 256 * 16384,
     )
-    moments = kernel_call(bins_kernel, "bins", f32(FEATS, KNOTS_W), got, normal, far=(1,))
+    moments = kernel_call(bins_kernel, "bins", f32(N_CCD, FEATS, KNOTS_W), got, normal, far=(1,))
     attitude, reply = kernel_call(
         attitude_kernel,
         "attitude",
         (f32(1, 4, KNOTS_W), f32(WINDOWS, 128)),
-        moments,
-        *from_others(moments),
+        among_ccd(moments),
         got,
         jnp.asarray(knot_matrix()),
     )
@@ -443,7 +450,7 @@
     right = kernel_call(
         source_right_kernel,
         "source_right",
-        f32(5 * HIGH, LOW),
+        f32(N_CCD, 5 * HIGH, LOW),
         knots,
         slots,
         obs,
@@ -452,7 +459,7 @@
         scratch=segment_scratch(5),
         flops=2 * 160 * 256 * 16384,
     )
-    source_delta = kernel_call(solve_kernel, "solve", f32(5, SRC_DEV), factors, right, *from_others(right))
+    source_delta = kernel_call(solve_kernel, "solve", f32(5, SRC_DEV), factors, among_ccd(right))
     return attitude, source_delta
 
 

time: 70.7 us -> 72.5 us (1.025)
  starting transfers between devices: 37.7 us -> 27.7 us
  blocking collectives: 0 us -> 9.04 us
  waiting for transfers between devices: 14 us -> 15.8 us
  Pallas kernels: 18 us -> 18.8 us
    ppermute x9 -> x3, starting transfers between devices: 14.4 us -> 2.15 us  [from_others(): lax.ppermute(values, 'ccd', [(at, (at + shift) % N_CCD) for at in range(N...]
    all_to_all x0 -> x1, blocking collectives: none -> 9.04 us  [among_ccd(): lax.all_to_all(copies, 'ccd', split_axis=0, concat_axis=0, tiled=True)]
    ppermute x9 -> x3, waiting for transfers between devices: 8.59 us -> 0.01 us  [from_others(): lax.ppermute(values, 'ccd', [(at, (at + shift) % N_CCD) for at in range(N...]
    all_to_all x0 -> x1, waiting for transfers between devices: none -> 6 us  [among_ccd(): lax.all_to_all(copies, 'ccd', split_axis=0, concat_axis=0, tiled=True)]
    all_to_all x2, waiting for transfers between devices: 5.39 us -> 9.84 us  [to_windows(): lax.all_to_all(values, ('src', 'win'), split_axis=0, concat_axis=0, tiled...]
    all_to_all x0 -> x1, starting transfers between devices: none -> 3.45 us  [among_ccd(): lax.all_to_all(copies, 'ccd', split_axis=0, concat_axis=0, tiled=True)]
    all_to_all x2, starting transfers between devices: 23.3 us -> 22.1 us  [to_windows(): lax.all_to_all(values, ('src', 'win'), split_axis=0, concat_axis=0, tiled...]
    pallas_call x7, Pallas kernels: 18 us -> 18.8 us  [kernel_call(): pl.pallas_call(body, out_shape=outs, in_specs=[pl.BlockSpec(memory_space=...]
  transfers between devices with their start and end apart: 11 -> 6, of which waited for: 8 -> 3; matrix products, arithmetic and copies ran while one was open for 0% -> 0% of each run, Pallas kernels for 21% -> 17%
where the time goes in v5:
time: 72.5 us; the launch traced here: 72.2 us
  starting transfers between devices  27.7 us (38%)
  Pallas kernels  18.8 us (26%)
  waiting for transfers between devices  15.8 us (22%)
  blocking collectives  9.04 us (12%)
  between operations  0.77 us (1%)
    all_to_all x2, starting transfers between devices, to_windows(): lax.all_to_all(values, ('src', 'win'), split_axis=0, concat_axis=0, tiled...  22.1 us
    pallas_call x7, Pallas kernels, kernel_call(): pl.pallas_call(body, out_shape=outs, in_specs=[pl.BlockSpec(memory_space=...  18.8 us
    all_to_all x2, waiting for transfers between devices, to_windows(): lax.all_to_all(values, ('src', 'win'), split_axis=0, concat_axis=0, tiled...  9.84 us
    all_to_all x1, blocking collectives, among_ccd(): lax.all_to_all(copies, 'ccd', split_axis=0, concat_axis=0, tiled=True)  9.04 us
    all_to_all x1, waiting for transfers between devices, among_ccd(): lax.all_to_all(copies, 'ccd', split_axis=0, concat_axis=0, tiled=True)  6 us
    all_to_all x1, starting transfers between devices, among_ccd(): lax.all_to_all(copies, 'ccd', split_axis=0, concat_axis=0, tiled=True)  3.45 us
    ppermute x3, starting transfers between devices, from_others(): lax.ppermute(values, 'ccd', [(at, (at + shift) % N_CCD) for at in range(N...  2.15 us
  transfers between devices with their start and end apart: 6, of which 3 were waited for; matrix products, arithmetic and copies ran while one was open for 0% of the time, Pallas kernels for 17%

profile of v5, /device:TPU:1, one launch (start us, length us, event | category | flops | bytes accessed | tf_op | source)
XLA Modules:
  0.0 72.2 jit_solution(4786303650612051065)
XLA Ops:
  0.6 0.0 copy-start.2
  0.6 2.6 %normals.1 = (f32[256,128]{1,0:T(8,128)}, f32[768,128]{1,0:T(8,128)}, f32[8,128]{1,0:T(8,128)}, s32[128,128]{1,0:T(8,128)}) custom-call(s32[1,128]{1,0:T(1,128)} %bitcast.19, s32[1,128]{1,0:T(1,128)} %bitcast.20, f32[128,128]{1,0:T(8,128)} %refs_2_.1, f32[512,128]{1,0:T(8,128)} %bitcast.17, f32[128,128]{1,0:T(8,128)} %refs_4_.1, s32[128,128]{1,0:T(8,128)} %refs_5_.1), custom_call_target="tpu_custom_call" | custom-call | flops 1000000 | bytes 459776 | tf_op jit(solution)/shard_map/normals/pallas_call | solution.py:362
  3.3 0.0 copy-start.3
  3.3 13.3 %all-to-all-start = ((f32[64,4,128]{2,1,0:T(4,128)}), f32[64,4,128]{2,1,0:T(4,128)S(1)}, u32[]{:S(2)}, u32[]{:S(2)}) async-start(f32[64,4,128]{2,1,0:T(4,128)} %bitcast.18), calls=%async_computation | async-start | bytes 262144 | tf_op jit(solution)/shard_map/all_to_all | solution.py:399
  16.6 0.0 copy-done.2
  16.6 0.0 copy-done.3
  16.6 7.0 %source_normals.1.after_ref.own_ref = f32[240,256]{1,0:T(8,128)S(1)} custom-call(s32[128,128]{1,0:T(8,128)S(1)} %copy-done.3, f32[640,128]{1,0:T(8,128)S(1)} %bitcast.15), custom_call_target="tpu_custom_call" | custom-call | flops 4026531840 | bytes 393216 | tf_op jit(solution)/shard_map/source_normals/pallas_call | solution.py:362
  23.6 2.9 %all-to-all-done = f32[64,4,128]{2,1,0:T(4,128)S(1)} async-done(((f32[64,4,128]{2,1,0:T(4,128)}), f32[64,4,128]{2,1,0:T(4,128)S(1)}, u32[]{:S(2)}, u32[]{:S(2)}) %all-to-all-start) | async-done | bytes 131104 | tf_op jit(solution)/shard_map/all_to_all | solution.py:399
  26.5 0.3 bins.1
  26.8 0.0 copy-start
  26.8 0.0 copy-start.1
  26.8 9.0 %all_to_all.26.parts_ref = f32[4,88,128]{2,1,0:T(8,128)S(1)} all-to-all(f32[4,88,128]{2,1,0:T(8,128)S(1)} %bins.1), channel_id=1, replica_groups=mesh['src'=16,'win'=4,'ccd'=4] {'ccd'}, dimensions={0} | all-to-all | bytes 360448 | tf_op jit(solution)/shard_map/all_to_all | solution.py:395
  35.9 0.0 copy-done
  35.9 2.7 %attitude.1 = (f32[1,4,128]{2,1,0:T(4,128)}, f32[64,128]{1,0:T(8,128)}) custom-call(f32[4,88,128]{2,1,0:T(8,128)S(1)} %all_to_all.26.parts_ref, f32[256,128]{1,0:T(8,128)S(1)} %bitcast.13, bf16[120,352]{1,0:T(8,128)(2,1)S(1)} %copy-done), custom_call_target="tpu_custom_call" | custom-call | flops 1000000 | bytes 480256 | tf_op jit(solution)/shard_map/attitude/pallas_call | solution.py:362
  38.6 8.8 %all-to-all-start.2 = ((f32[64,1,128]{2,1,0:T(1,128)}), f32[64,1,128]{2,1,0:T(1,128)S(1)}, u32[]{:S(2)}, u32[]{:S(2)}) async-start(f32[64,1,128]{2,1,0:T(1,128)} %bitcast.8), calls=%async_computation.2 | async-start | bytes 65536 | tf_op jit(solution)/shard_map/all_to_all | solution.py:399
  47.4 0.0 copy-start.4
  47.4 1.0 %collective-permute-start.2 = (f32[240,256]{1,0:T(8,128)S(1)}, f32[240,256]{1,0:T(8,128)S(1)}, u32[]{:S(2)}, u32[]{:S(2)}) collective-permute-start(f32[240,256]{1,0:T(8,128)S(1)} %source_normals.1.after_ref.own_ref), channel_id=1, source_target_pairs={{0,3},{1,0},{2,1},{3,2},{4,7},{5,4},{6,5},{7,6},{8,11},{9,8},{10,9... | collective-permute-start | bytes 737288 | tf_op jit(solution)/shard_map/ppermute | solution.py:390
  48.4 1.2 %collective-permute-start.1 = (f32[240,256]{1,0:T(8,128)S(1)}, f32[240,256]{1,0:T(8,128)S(1)}, u32[]{:S(2)}, u32[]{:S(2)}) collective-permute-start(f32[240,256]{1,0:T(8,128)S(1)} %source_normals.1.after_ref.own_ref), channel_id=1, source_target_pairs={{0,2},{1,3},{2,0},{3,1},{4,6},{5,7},{6,4},{7,5},{8,10},{9,11},{10,... | collective-permute-start | bytes 737288 | tf_op jit(solution)/shard_map/ppermute | solution.py:390
  49.6 0.0 collective-permute-start
  49.6 6.9 %all-to-all-done.2 = f32[64,1,128]{2,1,0:T(1,128)S(1)} async-done(((f32[64,1,128]{2,1,0:T(1,128)}), f32[64,1,128]{2,1,0:T(1,128)S(1)}, u32[]{:S(2)}, u32[]{:S(2)}) %all-to-all-start.2) | async-done | bytes 32800 | tf_op jit(solution)/shard_map/all_to_all | solution.py:399
  56.5 0.0 copy-done.1
  56.5 0.0 copy-done.4
  56.5 5.3 %source_right.1 = f32[4,80,256]{2,1,0:T(8,128)} custom-call(f32[64,128]{1,0:T(8,128)S(1)} %bitcast.14, f32[8,128]{1,0:T(8,128)S(1)} %copy-done.4, f32[768,128]{1,0:T(8,128)S(1)} %copy-done.1, s32[128,128]{1,0:T(8,128)S(1)} %copy-done.3, f32[640,128]{1,0:T(8,128)S(1)} %bitcast.16), custom_call_target="tpu_custom_call" | custom-call | flops 1342177280 | bytes 823296 | tf_op jit(solution)/shard_map/source_right/pallas_call | solution.py:362
  61.8 3.5 %all-to-all-start.3 = ((f32[4,80,256]{2,1,0:T(8,128)}), f32[4,80,256]{2,1,0:T(8,128)S(1)}, u32[]{:S(2)}, u32[]{:S(2)}) async-start(f32[4,80,256]{2,1,0:T(8,128)} %source_right.1), calls=%async_computation.3 | async-start | bytes 655360 | tf_op jit(solution)/shard_map/all_to_all | solution.py:395
  65.3 0.0 collective-permute-done.2.three_ref
  65.3 0.0 collective-permute-done.1.two_ref
  65.3 0.0 collective-permute-done.one_ref
  65.3 0.1 factors.1.factor_ref
  65.4 6.0 %all-to-all-done.3.parts_ref = f32[4,80,256]{2,1,0:T(8,128)S(1)} async-done(((f32[4,80,256]{2,1,0:T(8,128)}), f32[4,80,256]{2,1,0:T(8,128)S(1)}, u32[]{:S(2)}, u32[]{:S(2)}) %all-to-all-start.3) | async-done | bytes 327712 | tf_op jit(solution)/shard_map/all_to_all | solution.py:395
  71.4 0.7 %solve.1 = f32[5,4096]{1,0:T(8,128)} custom-call(f32[240,256]{1,0:T(8,128)S(1)} %factors.1.factor_ref, f32[4,80,256]{2,1,0:T(8,128)S(1)} %all-to-all-done.3.parts_ref), custom_call_target="tpu_custom_call" | custom-call | flops 1000000 | bytes 573440 | tf_op jit(solution)/shard_map/solve/pallas_call | solution.py:362
Async XLA Ops:
  0.6 15.9 %copy-start.2 = (f32[128,5,128]{2,0,1:T(8,128)S(1)}, f32[128,5,128]{2,0,1:T(8,128)}, u32[]{:S(2)}) copy-start(f32[128,5,128]{2,0,1:T(8,128)} %param.14) | copy-start | bytes 983044
  3.3 13.3 %copy-start.3 = (s32[128,128]{1,0:T(8,128)S(1)}, s32[128,128]{1,0:T(8,128)}, u32[]{:S(2)}) copy-start(s32[128,128]{1,0:T(8,128)} %get-tuple-element.9.marked_ref) | copy-start | bytes 196612
  3.3 23.2 %all-to-all-start = ((f32[64,4,128]{2,1,0:T(4,128)}), f32[64,4,128]{2,1,0:T(4,128)S(1)}, u32[]{:S(2)}, u32[]{:S(2)}) async-start(f32[64,4,128]{2,1,0:T(4,128)} %bitcast.18), calls=%async_computation | async-start | bytes 262144 | tf_op jit(solution)/shard_map/all_to_all | solution.py:399
  26.8 9.1 %copy-start = (bf16[120,352]{1,0:T(8,128)(2,1)S(1)}, bf16[120,352]{1,0:T(8,128)(2,1)}, u32[]{:S(2)}) copy-start(bf16[120,352]{1,0:T(8,128)(2,1)} %constant.2.clone.table_ref) | copy-start | bytes 253444
  26.8 29.7 %copy-start.1 = (f32[768,128]{1,0:T(8,128)S(1)}, f32[768,128]{1,0:T(8,128)}, u32[]{:S(2)}) copy-start(f32[768,128]{1,0:T(8,128)} %get-tuple-element.13.obs_ref) | copy-start | bytes 1179652
  38.6 17.9 %all-to-all-start.2 = ((f32[64,1,128]{2,1,0:T(1,128)}), f32[64,1,128]{2,1,0:T(1,128)S(1)}, u32[]{:S(2)}, u32[]{:S(2)}) async-start(f32[64,1,128]{2,1,0:T(1,128)} %bitcast.8), calls=%async_computation.2 | async-start | bytes 65536 | tf_op jit(solution)/shard_map/all_to_all | solution.py:399
  47.4 9.1 %copy-start.4 = (f32[8,128]{1,0:T(8,128)S(1)}, f32[8,128]{1,0:T(8,128)}, u32[]{:S(2)}) copy-start(f32[8,128]{1,0:T(8,128)} %get-tuple-element.12.slot_ref) | copy-start | bytes 12292
  47.4 17.9 %collective-permute-start.2 = (f32[240,256]{1,0:T(8,128)S(1)}, f32[240,256]{1,0:T(8,128)S(1)}, u32[]{:S(2)}, u32[]{:S(2)}) collective-permute-start(f32[240,256]{1,0:T(8,128)S(1)} %source_normals.1.after_ref.own_ref), channel_id=1, source_target_pairs={{0,3},{1,0},{2,1},{3,2},{4,7},{5,4},{6,5},{7,6},{8,11},{9,8},{10,9... | collective-permute-start | bytes 737288 | tf_op jit(solution)/shard_map/ppermute | solution.py:390
  48.4 16.9 %collective-permute-start.1 = (f32[240,256]{1,0:T(8,128)S(1)}, f32[240,256]{1,0:T(8,128)S(1)}, u32[]{:S(2)}, u32[]{:S(2)}) collective-permute-start(f32[240,256]{1,0:T(8,128)S(1)} %source_normals.1.after_ref.own_ref), channel_id=1, source_target_pairs={{0,2},{1,3},{2,0},{3,1},{4,6},{5,7},{6,4},{7,5},{8,10},{9,11},{10,... | collective-permute-start | bytes 737288 | tf_op jit(solution)/shard_map/ppermute | solution.py:390
  49.6 15.7 %collective-permute-start = (f32[240,256]{1,0:T(8,128)S(1)}, f32[240,256]{1,0:T(8,128)S(1)}, u32[]{:S(2)}, u32[]{:S(2)}) collective-permute-start(f32[240,256]{1,0:T(8,128)S(1)} %source_normals.1.after_ref.own_ref), channel_id=1, source_target_pairs={{0,1},{1,2},{2,3},{3,0},{4,5},{5,6},{6,7},{7,4},{8,9},{9,10},{10,1... | collective-permute-start | bytes 737288 | tf_op jit(solution)/shard_map/ppermute | solution.py:390
  61.8 9.6 %all-to-all-start.3 = ((f32[4,80,256]{2,1,0:T(8,128)}), f32[4,80,256]{2,1,0:T(8,128)S(1)}, u32[]{:S(2)}, u32[]{:S(2)}) async-start(f32[4,80,256]{2,1,0:T(8,128)} %source_right.1), calls=%async_computation.3 | async-start | bytes 655360 | tf_op jit(solution)/shard_map/all_to_all | solution.py:395

commit v6 on v5

--- a/solution.py
+++ b/solution.py
@@ -94,8 +94,8 @@
 
 
 def normals_kernel(*refs):
-    given, (send_ref, obs_ref, slot_ref, marked_ref), here = refs[:6], refs[6:10], refs[10:16]
-    pay_ref, done_ref = refs[16:]
+    given, (send_ref, obs_out, slot_ref, marked_out), here = refs[:6], refs[6:10], refs[10:16]
+    pay_ref, obs_ref, marked_ref, done_ref = refs[16:]
     bin_ref, rows_ref, phase_ref, att_ref, resid_ref, source_ref = here
     copies = [pltpu.make_async_copy(given[at], here[at], done_ref.at[at]) for at in range(6)]
     for copy in copies:
@@ -123,6 +123,12 @@
     obs_ref[128:256, :] = resid
     for q in range(4):
         obs_ref[256 + 128 * q : 384 + 128 * q, :] = att[q]
+    results = [
+        pltpu.make_async_copy(marked_ref, marked_out, done_ref.at[6]),
+        pltpu.make_async_copy(obs_ref, obs_out, done_ref.at[7]),
+    ]
+    for copy in results:
+        copy.start()
     v = 1.0 - u
     u2, v2 = u * u, v * v
     u3, v3 = u2 * u, v2 * v
@@ -147,6 +153,8 @@
     pay_ref[BIN_AT : BIN_AT + 1, :] = local_bin
     pay_ref[BIN_AT + 1 :, :] = jnp.zeros((NBLK - BIN_AT - 1, NBLK), F32)
     send_ref[...] = exact_dot(pay_ref[...], place, NT, swap=True)
+    for copy in results:
+        copy.wait()
 
 
 def bins_kernel(got_ref, after_ref, out_ref):
@@ -301,9 +309,7 @@
     values = values.T
     for p in range(5):
         put_terms(terms_ref, p, gain_ref[NBLK * p : NBLK * p + NBLK, :] * values)
-    source_sums(5, terms_ref, high_ref, low_ref, out_ref.at[0], *work)
-    for at in range(1, N_CCD):
-        out_ref[at] = out_ref[0]
+    source_sums(5, terms_ref, high_ref, low_ref, out_ref, *work)
 
 
 def factor_kernel(own_ref, one_ref, two_ref, three_ref, out_ref):
@@ -328,14 +334,14 @@
         out_ref[HIGH * at : HIGH * at + HIGH, :] = lower[second, first]
 
 
-def solve_kernel(factor_ref, parts_ref, out_ref):
+def solve_kernel(factor_ref, own_ref, one_ref, two_ref, three_ref, out_ref):
     lower = {}
     for at, (first, second) in enumerate(PAIR_LIST):
         lower[second, first] = factor_ref[HIGH * at : HIGH * at + HIGH, :]
     values = []
     for row in range(5):
         rows = slice(HIGH * row, HIGH * row + HIGH)
-        running = (parts_ref[0, rows, :] + parts_ref[1, rows, :]) + (parts_ref[2, rows, :] + parts_ref[3, rows, :])
+        running = (own_ref[rows, :] + two_ref[rows, :]) + (one_ref[rows, :] + three_ref[rows, :])
         for before in range(row):
             running = running - lower[row, before] * values[before]
         values.append(running * lower[row, row])
@@ -353,10 +359,9 @@
     return jax.ShapeDtypeStruct(shape, F32)
 
 
-def kernel_call(body, name, outs, *args, scratch=(), flops=1_000_000, far=(), grant=32, passed=None):
-    passed = passed or {}
+def kernel_call(body, name, outs, *args, scratch=(), flops=1_000_000, far=(), far_out=(), grant=32):
     place = [pl.ANY if at in far else pltpu.MemorySpace.VMEM for at in range(len(args))]
-    out_place = [pl.ANY if at in passed.values() else pltpu.MemorySpace.VMEM for at in range(len(jax.tree.leaves(outs)))]
+    out_place = [pl.ANY if at in far_out else pltpu.MemorySpace.VMEM for at in range(len(jax.tree.leaves(outs)))]
     out_specs = [pl.BlockSpec(memory_space=at) for at in out_place]
     size = sum(math.prod(a.shape) * 4 for a in args)
     return pl.pallas_call(
@@ -364,7 +369,6 @@
         out_shape=outs,
         in_specs=[pl.BlockSpec(memory_space=at) for at in place],
         out_specs=tuple(out_specs) if isinstance(outs, tuple) else out_specs[0],
-        input_output_aliases=passed,
         scratch_shapes=list(scratch),
         compiler_params=pltpu.CompilerParams(vmem_limit_bytes=grant * 1024 * 1024),
         cost_estimate=pl.CostEstimate(flops=flops, bytes_accessed=size, transcendentals=0),
@@ -421,9 +425,12 @@
             pltpu.VMEM((NBLK, ROWS), F32),
             pltpu.VMEM((NBLK, ROWS), jnp.int32),
             pltpu.VMEM((NBLK, NBLK), F32),
-            pltpu.SemaphoreType.DMA((6,)),
+            pltpu.VMEM((6 * ROWS, NBLK), F32),
+            pltpu.VMEM((NBLK, ROWS), jnp.int32),
+            pltpu.SemaphoreType.DMA((8,)),
         ),
         far=range(6),
+        far_out=(1, 3),
         grant=56,
     )
     got = to_windows(send.reshape(WINDOWS, CAP, 128)).reshape(SLOTS, 128)
@@ -450,7 +457,7 @@
     right = kernel_call(
         source_right_kernel,
         "source_right",
-        f32(N_CCD, 5 * HIGH, LOW),
+        f32(5 * HIGH, LOW),
         knots,
         slots,
         obs,
@@ -459,7 +466,7 @@
         scratch=segment_scratch(5),
         flops=2 * 160 * 256 * 16384,
     )
-    source_delta = kernel_call(solve_kernel, "solve", f32(5, SRC_DEV), factors, among_ccd(right))
+    source_delta = kernel_call(solve_kernel, "solve", f32(5, SRC_DEV), factors, right, *from_others(right))
     return attitude, source_delta
 
 

time: 72.5 us -> 71.6 us (0.988)
  blocking collectives: 9.04 us -> 0 us
  starting transfers between devices: 27.7 us -> 34.6 us
  waiting for transfers between devices: 15.8 us -> 16.6 us
    all_to_all x1 -> x0, blocking collectives: 9.04 us -> none  [among_ccd(): lax.all_to_all(copies, 'ccd', split_axis=0, concat_axis=0, tiled=True)]
    ppermute x3 -> x6, starting transfers between devices: 2.15 us -> 8.33 us  [from_others(): lax.ppermute(values, 'ccd', [(at, (at + shift) % N_CCD) for at in range(N...]
    ppermute x3 -> x6, waiting for transfers between devices: 0.01 us -> 4.7 us  [from_others(): lax.ppermute(values, 'ccd', [(at, (at + shift) % N_CCD) for at in range(N...]
    all_to_all x1, waiting for transfers between devices: 6 us -> 2.42 us  [among_ccd(): lax.all_to_all(copies, 'ccd', split_axis=0, concat_axis=0, tiled=True)]
  transfers between devices with their start and end apart: 6 -> 9, of which waited for: 3 -> 6; matrix products, arithmetic and copies ran while one was open for 0% -> 0% of each run, Pallas kernels for 17% -> 20%
where the time goes in v6:
time: 71.6 us; the launch traced here: 71.3 us
  starting transfers between devices  34.6 us (48%)
  Pallas kernels  19.4 us (27%)
  waiting for transfers between devices  16.6 us (23%)
  between operations  0.73 us (1%)
    all_to_all x2, starting transfers between devices, to_windows(): lax.all_to_all(values, ('src', 'win'), split_axis=0, concat_axis=0, tiled...  22.1 us
    pallas_call x7, Pallas kernels, kernel_call(): pl.pallas_call(body, out_shape=outs, in_specs=[pl.BlockSpec(memory_space=...  19.4 us
    all_to_all x2, waiting for transfers between devices, to_windows(): lax.all_to_all(values, ('src', 'win'), split_axis=0, concat_axis=0, tiled...  9.46 us
    ppermute x6, starting transfers between devices, from_others(): lax.ppermute(values, 'ccd', [(at, (at + shift) % N_CCD) for at in range(N...  8.33 us
    ppermute x6, waiting for transfers between devices, from_others(): lax.ppermute(values, 'ccd', [(at, (at + shift) % N_CCD) for at in range(N...  4.7 us
    all_to_all x1, starting transfers between devices, among_ccd(): lax.all_to_all(copies, 'ccd', split_axis=0, concat_axis=0, tiled=True)  4.14 us
    all_to_all x1, waiting for transfers between devices, among_ccd(): lax.all_to_all(copies, 'ccd', split_axis=0, concat_axis=0, tiled=True)  2.42 us
  transfers between devices with their start and end apart: 9, of which 6 were waited for; matrix products, arithmetic and copies ran while one was open for 0% of the time, Pallas kernels for 20%

profile of v6, /device:TPU:1, one launch (start us, length us, event | category | flops | bytes accessed | tf_op | source)
XLA Modules:
  0.0 71.3 jit_solution(12336959574039100090)
XLA Ops:
  0.6 0.0 copy-start.2
  0.6 3.3 %normals.1 = (f32[256,128]{1,0:T(8,128)}, f32[768,128]{1,0:T(8,128)}, f32[8,128]{1,0:T(8,128)}, s32[128,128]{1,0:T(8,128)}) custom-call(s32[1,128]{1,0:T(1,128)} %bitcast.19, s32[1,128]{1,0:T(1,128)} %bitcast.20, f32[128,128]{1,0:T(8,128)} %refs_2_.1, f32[512,128]{1,0:T(8,128)} %bitcast.17, f32[128,128]{1,0:T(8,128)} %refs_4_.1, s32[128,128]{1,0:T(8,128)} %refs_5_.1), custom_call_target="tpu_custom_call" | custom-call | flops 1000000 | bytes 459776 | tf_op jit(solution)/shard_map/normals/pallas_call | solution.py:367
  3.9 0.0 copy-start.3
  3.9 13.3 %all-to-all-start = ((f32[64,4,128]{2,1,0:T(4,128)}), f32[64,4,128]{2,1,0:T(4,128)S(1)}, u32[]{:S(2)}, u32[]{:S(2)}) async-start(f32[64,4,128]{2,1,0:T(4,128)} %bitcast.18), calls=%async_computation | async-start | bytes 262144 | tf_op jit(solution)/shard_map/all_to_all | solution.py:403
  17.2 0.0 copy-done.2
  17.2 0.0 copy-done.3
  17.3 7.0 %source_normals.1.after_ref.own_ref = f32[240,256]{1,0:T(8,128)S(1)} custom-call(s32[128,128]{1,0:T(8,128)S(1)} %copy-done.3, f32[640,128]{1,0:T(8,128)S(1)} %bitcast.15), custom_call_target="tpu_custom_call" | custom-call | flops 4026531840 | bytes 393216 | tf_op jit(solution)/shard_map/source_normals/pallas_call | solution.py:367
  24.3 2.9 %all-to-all-done = f32[64,4,128]{2,1,0:T(4,128)S(1)} async-done(((f32[64,4,128]{2,1,0:T(4,128)}), f32[64,4,128]{2,1,0:T(4,128)S(1)}, u32[]{:S(2)}, u32[]{:S(2)}) %all-to-all-start) | async-done | bytes 131104 | tf_op jit(solution)/shard_map/all_to_all | solution.py:403
  27.2 1.0 %bins.1 = f32[4,88,128]{2,1,0:T(8,128)} custom-call(f32[256,128]{1,0:T(8,128)S(1)} %bitcast.12, f32[240,256]{1,0:T(8,128)S(1)} %source_normals.1.after_ref.own_ref), custom_call_target="tpu_custom_call" | custom-call | flops 1000000 | bytes 376832 | tf_op jit(solution)/shard_map/bins/pallas_call | solution.py:367
  28.1 0.0 copy-start
  28.1 0.0 copy-start.1
  28.1 4.1 %all-to-all-start.1 = ((f32[4,88,128]{2,1,0:T(8,128)}), f32[4,88,128]{2,1,0:T(8,128)S(1)}, u32[]{:S(2)}, u32[]{:S(2)}) async-start(f32[4,88,128]{2,1,0:T(8,128)} %bins.1), calls=%async_computation.1 | async-start | bytes 360448 | tf_op jit(solution)/shard_map/all_to_all | solution.py:399
  32.3 2.7 %collective-permute-start.2 = (f32[240,256]{1,0:T(8,128)S(1)}, f32[240,256]{1,0:T(8,128)S(1)}, u32[]{:S(2)}, u32[]{:S(2)}) collective-permute-start(f32[240,256]{1,0:T(8,128)S(1)} %source_normals.1.after_ref.own_ref), channel_id=1, source_target_pairs={{0,3},{1,0},{2,1},{3,2},{4,7},{5,4},{6,5},{7,6},{8,11},{9,8},{10,9... | collective-permute-start | bytes 737288 | tf_op jit(solution)/shard_map/ppermute | solution.py:394
  34.9 2.4 %all-to-all-done.1.parts_ref = f32[4,88,128]{2,1,0:T(8,128)S(1)} async-done(((f32[4,88,128]{2,1,0:T(8,128)}), f32[4,88,128]{2,1,0:T(8,128)S(1)}, u32[]{:S(2)}, u32[]{:S(2)}) %all-to-all-start.1) | async-done | bytes 180256 | tf_op jit(solution)/shard_map/all_to_all | solution.py:399
  37.4 0.0 copy-done
  37.4 2.7 %attitude.1 = (f32[1,4,128]{2,1,0:T(4,128)}, f32[64,128]{1,0:T(8,128)}) custom-call(f32[4,88,128]{2,1,0:T(8,128)S(1)} %all-to-all-done.1.parts_ref, f32[256,128]{1,0:T(8,128)S(1)} %bitcast.13, bf16[120,352]{1,0:T(8,128)(2,1)S(1)} %copy-done), custom_call_target="tpu_custom_call" | custom-call | flops 1000000 | bytes 480256 | tf_op jit(solution)/shard_map/attitude/pallas_call | solution.py:367
  40.1 8.8 %all-to-all-start.2 = ((f32[64,1,128]{2,1,0:T(1,128)}), f32[64,1,128]{2,1,0:T(1,128)S(1)}, u32[]{:S(2)}, u32[]{:S(2)}) async-start(f32[64,1,128]{2,1,0:T(1,128)} %bitcast.8), calls=%async_computation.2 | async-start | bytes 65536 | tf_op jit(solution)/shard_map/all_to_all | solution.py:403
  48.9 0.0 copy-start.4
  48.9 1.0 %collective-permute-start.1 = (f32[240,256]{1,0:T(8,128)S(1)}, f32[240,256]{1,0:T(8,128)S(1)}, u32[]{:S(2)}, u32[]{:S(2)}) collective-permute-start(f32[240,256]{1,0:T(8,128)S(1)} %source_normals.1.after_ref.own_ref), channel_id=1, source_target_pairs={{0,2},{1,3},{2,0},{3,1},{4,6},{5,7},{6,4},{7,5},{8,10},{9,11},{10,... | collective-permute-start | bytes 737288 | tf_op jit(solution)/shard_map/ppermute | solution.py:394
  49.9 1.5 %collective-permute-start = (f32[240,256]{1,0:T(8,128)S(1)}, f32[240,256]{1,0:T(8,128)S(1)}, u32[]{:S(2)}, u32[]{:S(2)}) collective-permute-start(f32[240,256]{1,0:T(8,128)S(1)} %source_normals.1.after_ref.own_ref), channel_id=1, source_target_pairs={{0,1},{1,2},{2,3},{3,0},{4,5},{5,6},{6,7},{7,4},{8,9},{9,10},{10,1... | collective-permute-start | bytes 737288 | tf_op jit(solution)/shard_map/ppermute | solution.py:394
  51.5 6.5 %all-to-all-done.2 = f32[64,1,128]{2,1,0:T(1,128)S(1)} async-done(((f32[64,1,128]{2,1,0:T(1,128)}), f32[64,1,128]{2,1,0:T(1,128)S(1)}, u32[]{:S(2)}, u32[]{:S(2)}) %all-to-all-start.2) | async-done | bytes 32800 | tf_op jit(solution)/shard_map/all_to_all | solution.py:403
  58.0 0.0 copy-done.1
  58.0 0.0 copy-done.4
  58.0 4.6 %source_right.1.own_ref = f32[80,256]{1,0:T(8,128)S(1)} custom-call(f32[64,128]{1,0:T(8,128)S(1)} %bitcast.14, f32[8,128]{1,0:T(8,128)S(1)} %copy-done.4, f32[768,128]{1,0:T(8,128)S(1)} %copy-done.1, s32[128,128]{1,0:T(8,128)S(1)} %copy-done.3, f32[640,128]{1,0:T(8,128)S(1)} %bitcast.16), custom_call_target="tpu_custom_call" | custom-call | flops 1342177280 | bytes 823296 | tf_op jit(solution)/shard_map/source_right/pallas_call | solution.py:367
  62.6 1.9 %collective-permute-start.5 = (f32[80,256]{1,0:T(8,128)S(1)}, f32[80,256]{1,0:T(8,128)S(1)}, u32[]{:S(2)}, u32[]{:S(2)}) collective-permute-start(f32[80,256]{1,0:T(8,128)S(1)} %source_right.1.own_ref), channel_id=1, source_target_pairs={{0,3},{1,0},{2,1},{3,2},{4,7},{5,4},{6,5},{7,6},{8,11},{9,8},{10,9... | collective-permute-start | bytes 245768 | tf_op jit(solution)/shard_map/ppermute | solution.py:394
  64.5 1.2 %collective-permute-start.4 = (f32[80,256]{1,0:T(8,128)S(1)}, f32[80,256]{1,0:T(8,128)S(1)}, u32[]{:S(2)}, u32[]{:S(2)}) collective-permute-start(f32[80,256]{1,0:T(8,128)S(1)} %source_right.1.own_ref), channel_id=1, source_target_pairs={{0,2},{1,3},{2,0},{3,1},{4,6},{5,7},{6,4},{7,5},{8,10},{9,11},{10,... | collective-permute-start | bytes 245768 | tf_op jit(solution)/shard_map/ppermute | solution.py:394
  65.7 0.0 collective-permute-done.2.three_ref
  65.7 0.0 collective-permute-start.3
  65.7 0.0 collective-permute-done.1.two_ref
  65.7 0.0 collective-permute-done.one_ref
  65.7 0.1 factors.1.factor_ref
  65.8 0.7 %collective-permute-done.5.three_ref = f32[80,256]{1,0:T(8,128)S(1)} collective-permute-done((f32[80,256]{1,0:T(8,128)S(1)}, f32[80,256]{1,0:T(8,128)S(1)}, u32[]{:S(2)}, u32[]{:S(2)}) %collective-permute-start.5) | collective-permute-done | bytes 81952 | tf_op jit(solution)/shard_map/ppermute | solution.py:394
  66.6 2.7 %collective-permute-done.4.two_ref = f32[80,256]{1,0:T(8,128)S(1)} collective-permute-done((f32[80,256]{1,0:T(8,128)S(1)}, f32[80,256]{1,0:T(8,128)S(1)}, u32[]{:S(2)}, u32[]{:S(2)}) %collective-permute-start.4) | collective-permute-done | bytes 81952 | tf_op jit(solution)/shard_map/ppermute | solution.py:394
  69.3 1.2 %collective-permute-done.3.one_ref = f32[80,256]{1,0:T(8,128)S(1)} collective-permute-done((f32[80,256]{1,0:T(8,128)S(1)}, f32[80,256]{1,0:T(8,128)S(1)}, u32[]{:S(2)}, u32[]{:S(2)}) %collective-permute-start.3) | collective-permute-done | bytes 81952 | tf_op jit(solution)/shard_map/ppermute | solution.py:394
  70.5 0.7 %solve.1 = f32[5,4096]{1,0:T(8,128)} custom-call(f32[240,256]{1,0:T(8,128)S(1)} %factors.1.factor_ref, f32[80,256]{1,0:T(8,128)S(1)} %source_right.1.own_ref, f32[80,256]{1,0:T(8,128)S(1)} %collective-permute-done.3.one_ref, f32[80,256]{1,0:T(8,128)S(1)} %collective-permute-done.4.two_ref, f32[80,256]{1,0:T(8,128)S(1)} %collective-permute-done.5.three_ref), custom_call_target="tpu_custom_call" | custom-call | flops 1000000 | bytes 573440 | tf_op jit(solution)/shard_map/solve/pallas_call | solution.py:367
Async XLA Ops:
  0.6 16.6 %copy-start.2 = (f32[128,5,128]{2,0,1:T(8,128)S(1)}, f32[128,5,128]{2,0,1:T(8,128)}, u32[]{:S(2)}) copy-start(f32[128,5,128]{2,0,1:T(8,128)} %param.14) | copy-start | bytes 983044
  3.9 13.3 %copy-start.3 = (s32[128,128]{1,0:T(8,128)S(1)}, s32[128,128]{1,0:T(8,128)}, u32[]{:S(2)}) copy-start(s32[128,128]{1,0:T(8,128)} %get-tuple-element.9.marked_ref) | copy-start | bytes 196612
  3.9 23.2 %all-to-all-start = ((f32[64,4,128]{2,1,0:T(4,128)}), f32[64,4,128]{2,1,0:T(4,128)S(1)}, u32[]{:S(2)}, u32[]{:S(2)}) async-start(f32[64,4,128]{2,1,0:T(4,128)} %bitcast.18), calls=%async_computation | async-start | bytes 262144 | tf_op jit(solution)/shard_map/all_to_all | solution.py:403
  28.1 9.2 %copy-start = (bf16[120,352]{1,0:T(8,128)(2,1)S(1)}, bf16[120,352]{1,0:T(8,128)(2,1)}, u32[]{:S(2)}) copy-start(bf16[120,352]{1,0:T(8,128)(2,1)} %constant.2.clone.table_ref) | copy-start | bytes 253444
  28.1 29.9 %copy-start.1 = (f32[768,128]{1,0:T(8,128)S(1)}, f32[768,128]{1,0:T(8,128)}, u32[]{:S(2)}) copy-start(f32[768,128]{1,0:T(8,128)} %get-tuple-element.13.obs_ref) | copy-start | bytes 1179652
  28.1 9.2 %all-to-all-start.1 = ((f32[4,88,128]{2,1,0:T(8,128)}), f32[4,88,128]{2,1,0:T(8,128)S(1)}, u32[]{:S(2)}, u32[]{:S(2)}) async-start(f32[4,88,128]{2,1,0:T(8,128)} %bins.1), calls=%async_computation.1 | async-start | bytes 360448 | tf_op jit(solution)/shard_map/all_to_all | solution.py:399
  32.3 33.5 %collective-permute-start.2 = (f32[240,256]{1,0:T(8,128)S(1)}, f32[240,256]{1,0:T(8,128)S(1)}, u32[]{:S(2)}, u32[]{:S(2)}) collective-permute-start(f32[240,256]{1,0:T(8,128)S(1)} %source_normals.1.after_ref.own_ref), channel_id=1, source_target_pairs={{0,3},{1,0},{2,1},{3,2},{4,7},{5,4},{6,5},{7,6},{8,11},{9,8},{10,9... | collective-permute-start | bytes 737288 | tf_op jit(solution)/shard_map/ppermute | solution.py:394
  40.1 17.9 %all-to-all-start.2 = ((f32[64,1,128]{2,1,0:T(1,128)}), f32[64,1,128]{2,1,0:T(1,128)S(1)}, u32[]{:S(2)}, u32[]{:S(2)}) async-start(f32[64,1,128]{2,1,0:T(1,128)} %bitcast.8), calls=%async_computation.2 | async-start | bytes 65536 | tf_op jit(solution)/shard_map/all_to_all | solution.py:403
  48.9 9.1 %copy-start.4 = (f32[8,128]{1,0:T(8,128)S(1)}, f32[8,128]{1,0:T(8,128)}, u32[]{:S(2)}) copy-start(f32[8,128]{1,0:T(8,128)} %get-tuple-element.12.slot_ref) | copy-start | bytes 12292
  48.9 16.8 %collective-permute-start.1 = (f32[240,256]{1,0:T(8,128)S(1)}, f32[240,256]{1,0:T(8,128)S(1)}, u32[]{:S(2)}, u32[]{:S(2)}) collective-permute-start(f32[240,256]{1,0:T(8,128)S(1)} %source_normals.1.after_ref.own_ref), channel_id=1, source_target_pairs={{0,2},{1,3},{2,0},{3,1},{4,6},{5,7},{6,4},{7,5},{8,10},{9,11},{10,... | collective-permute-start | bytes 737288 | tf_op jit(solution)/shard_map/ppermute | solution.py:394
  49.9 15.8 %collective-permute-start = (f32[240,256]{1,0:T(8,128)S(1)}, f32[240,256]{1,0:T(8,128)S(1)}, u32[]{:S(2)}, u32[]{:S(2)}) collective-permute-start(f32[240,256]{1,0:T(8,128)S(1)} %source_normals.1.after_ref.own_ref), channel_id=1, source_target_pairs={{0,1},{1,2},{2,3},{3,0},{4,5},{5,6},{6,7},{7,4},{8,9},{9,10},{10,1... | collective-permute-start | bytes 737288 | tf_op jit(solution)/shard_map/ppermute | solution.py:394
  62.6 4.0 %collective-permute-start.5 = (f32[80,256]{1,0:T(8,128)S(1)}, f32[80,256]{1,0:T(8,128)S(1)}, u32[]{:S(2)}, u32[]{:S(2)}) collective-permute-start(f32[80,256]{1,0:T(8,128)S(1)} %source_right.1.own_ref), channel_id=1, source_target_pairs={{0,3},{1,0},{2,1},{3,2},{4,7},{5,4},{6,5},{7,6},{8,11},{9,8},{10,9... | collective-permute-start | bytes 245768 | tf_op jit(solution)/shard_map/ppermute | solution.py:394
  64.5 4.8 %collective-permute-start.4 = (f32[80,256]{1,0:T(8,128)S(1)}, f32[80,256]{1,0:T(8,128)S(1)}, u32[]{:S(2)}, u32[]{:S(2)}) collective-permute-start(f32[80,256]{1,0:T(8,128)S(1)} %source_right.1.own_ref), channel_id=1, source_target_pairs={{0,2},{1,3},{2,0},{3,1},{4,6},{5,7},{6,4},{7,5},{8,10},{9,11},{10,... | collective-permute-start | bytes 245768 | tf_op jit(solution)/shard_map/ppermute | solution.py:394
  65.7 4.8 %collective-permute-start.3 = (f32[80,256]{1,0:T(8,128)S(1)}, f32[80,256]{1,0:T(8,128)S(1)}, u32[]{:S(2)}, u32[]{:S(2)}) collective-permute-start(f32[80,256]{1,0:T(8,128)S(1)} %source_right.1.own_ref), channel_id=1, source_target_pairs={{0,1},{1,2},{2,3},{3,0},{4,5},{5,6},{6,7},{7,4},{8,9},{9,10},{10,1... | collective-permute-start | bytes 245768 | tf_op jit(solution)/shard_map/ppermute | solution.py:394

commit v7 on v4

--- a/solution.py
+++ b/solution.py
@@ -21,8 +21,7 @@
 N_CCD = 4
 HIGH = 16
 LOW = 256
-STEP_BLOCKS = 16
-STEPS = NBLK // STEP_BLOCKS
+DOT_BLOCKS = 8
 
 KNOT_PRIOR = 1.0
 SOURCE_PRIOR = 1.0
@@ -207,40 +206,30 @@
         reply_ref[:, 16 * s : 16 * s + 16] = knots[WINDOWS * s : WINDOWS * s + WINDOWS]
 
 
-def source_sums(count, terms_ref, high_ref, low_ref, out_ref, acc_ref, *buffers):
+def source_sums(count, chunk, terms_ref, high_ref, low_ref, out_ref, acc_ref):
     high_at = iota_f((HIGH, ROWS), 0)
     low_at = iota_f((LOW, ROWS), 0).astype(BF16)
     one, zero = jnp.ones((), BF16), jnp.zeros((), BF16)
 
-    def build(at, slot):
-        a_ref, b_ref = buffers[slot], buffers[2 + slot]
-        for inner in range(STEP_BLOCKS):
-            block = at * STEP_BLOCKS + inner
-            lanes = slice(inner * ROWS, inner * ROWS + ROWS)
-            here = high_at == high_ref[pl.ds(block, 1), :]
-            low = jnp.broadcast_to(low_ref[pl.ds(block, 1), :], (HIGH, ROWS)).astype(BF16)
-            low = jnp.concatenate([low] * (LOW // HIGH), axis=0)
-            b_ref[:, lanes] = jnp.where(low_at == low, one, zero)
-            for c in range(2 * count):
-                term = jnp.where(here, terms_ref[pl.ds(c * NBLK + block, 1), :], 0.0)
-                a_ref[c * HIGH : (c + 1) * HIGH, lanes] = term.astype(BF16)
-
-    def multiply(slot):
-        acc_ref[...] += lax.dot_general(buffers[2 + slot][...], buffers[slot][...], NT, preferred_element_type=F32)
-
-    def step(pair, carry):
-        multiply(0)
-        build(2 * pair + 1, 1)
-        multiply(1)
-        build(2 * pair + 2, 0)
+    def factors(block):
+        here = high_at == high_ref[pl.ds(block, 1), :]
+        low = jnp.broadcast_to(low_ref[pl.ds(block, 1), :], (HIGH, ROWS)).astype(BF16)
+        low = jnp.concatenate([low] * (LOW // HIGH), axis=0)
+        terms = [
+            jnp.where(here, terms_ref[pl.ds(c * NBLK + block, 1), :], 0.0).astype(BF16) for c in range(2 * count)
+        ]
+        return jnp.concatenate(terms, axis=0), jnp.where(low_at == low, one, zero)
+
+    def step(at, carry):
+        for first in range(0, chunk, DOT_BLOCKS):
+            pairs = [factors(at * chunk + first + inner) for inner in range(DOT_BLOCKS)]
+            terms = jnp.concatenate([pair[0] for pair in pairs], axis=1)
+            ones = jnp.concatenate([pair[1] for pair in pairs], axis=1)
+            acc_ref[...] += lax.dot_general(ones, terms, NT, preferred_element_type=F32)
         return carry
 
     acc_ref[...] = jnp.zeros(acc_ref.shape, F32)
-    build(0, 0)
-    lax.fori_loop(0, STEPS // 2 - 1, step, 0)
-    multiply(0)
-    build(STEPS - 1, 1)
-    multiply(1)
+    lax.fori_loop(0, NBLK // chunk, step, 0)
     sums = acc_ref[...].T
     for c in range(count):
         at = 2 * c * HIGH
@@ -265,7 +254,7 @@
     gains = [gain_ref[NBLK * p : NBLK * p + NBLK, :] for p in range(5)]
     for at, (first, second) in enumerate(PAIR_LIST):
         put_terms(terms_ref, at, gains[first] * gains[second])
-    source_sums(15, terms_ref, high_ref, low_ref, out_ref, *work)
+    source_sums(15, 32, terms_ref, high_ref, low_ref, out_ref, *work)
 
 
 def source_right_kernel(
@@ -299,7 +288,7 @@
     values = values.T
     for p in range(5):
         put_terms(terms_ref, p, gain_ref[NBLK * p : NBLK * p + NBLK, :] * values)
-    source_sums(5, terms_ref, high_ref, low_ref, out_ref, *work)
+    source_sums(5, 64, terms_ref, high_ref, low_ref, out_ref, *work)
 
 
 def factor_kernel(own_ref, one_ref, two_ref, three_ref, out_ref):
@@ -374,10 +363,6 @@
         pltpu.VMEM((NBLK, ROWS), F32),
         pltpu.VMEM((NBLK, ROWS), F32),
         pltpu.VMEM((LOW, 2 * count * HIGH), F32),
-        pltpu.VMEM((2 * count * HIGH, STEP_BLOCKS * ROWS), BF16),
-        pltpu.VMEM((2 * count * HIGH, STEP_BLOCKS * ROWS), BF16),
-        pltpu.VMEM((LOW, STEP_BLOCKS * ROWS), BF16),
-        pltpu.VMEM((LOW, STEP_BLOCKS * ROWS), BF16),
     )
 
 

time: 70.7 us -> 67.9 us (0.960)
  Pallas kernels: 18 us -> 15.2 us
  starting transfers between devices: 37.7 us -> 36.2 us
  waiting for transfers between devices: 14 us -> 15.4 us
    pallas_call x7, Pallas kernels: 18 us -> 15.2 us  [kernel_call(): pl.pallas_call(body, out_shape=outs, in_specs=[pl.BlockSpec(memory_space=...]
    all_to_all x2, waiting for transfers between devices: 5.39 us -> 6.86 us  [to_windows(): lax.all_to_all(values, ('src', 'win'), split_axis=0, concat_axis=0, tiled...]
    all_to_all x2, starting transfers between devices: 23.3 us -> 21.8 us  [to_windows(): lax.all_to_all(values, ('src', 'win'), split_axis=0, concat_axis=0, tiled...]
  transfers between devices with their start and end apart: 11 -> 11, of which waited for: 8 -> 8; matrix products, arithmetic and copies ran while one was open for 0% -> 0% of each run, Pallas kernels for 21% -> 18%
where the time goes in v7:
time: 67.9 us; the launch traced here: 67.6 us
  starting transfers between devices  36.2 us (53%)
  waiting for transfers between devices  15.4 us (23%)
  Pallas kernels  15.2 us (22%)
  between operations  0.73 us (1%)
    all_to_all x2, starting transfers between devices, to_windows(): lax.all_to_all(values, ('src', 'win'), split_axis=0, concat_axis=0, tiled...  21.8 us
    pallas_call x7, Pallas kernels, kernel_call(): pl.pallas_call(body, out_shape=outs, in_specs=[pl.BlockSpec(memory_space=...  15.2 us
    ppermute x9, starting transfers between devices, from_others(): lax.ppermute(values, 'ccd', [(at, (at + shift) % N_CCD) for at in range(N...  14.4 us
    ppermute x9, waiting for transfers between devices, from_others(): lax.ppermute(values, 'ccd', [(at, (at + shift) % N_CCD) for at in range(N...  8.58 us
    all_to_all x2, waiting for transfers between devices, to_windows(): lax.all_to_all(values, ('src', 'win'), split_axis=0, concat_axis=0, tiled...  6.86 us
  transfers between devices with their start and end apart: 11, of which 8 were waited for; matrix products, arithmetic and copies ran while one was open for 0% of the time, Pallas kernels for 18%

profile of v7, /device:TPU:1, one launch (start us, length us, event | category | flops | bytes accessed | tf_op | source)
XLA Modules:
  0.0 67.6 jit_solution(11748430772148729514)
XLA Ops:
  0.6 0.0 copy-start.2
  0.6 2.6 %normals.1 = (f32[256,128]{1,0:T(8,128)}, f32[768,128]{1,0:T(8,128)}, f32[8,128]{1,0:T(8,128)}, s32[128,128]{1,0:T(8,128)}) custom-call(s32[1,128]{1,0:T(1,128)} %bitcast.19, s32[1,128]{1,0:T(1,128)} %bitcast.20, f32[128,128]{1,0:T(8,128)} %refs_2_.1, f32[512,128]{1,0:T(8,128)} %bitcast.17, f32[128,128]{1,0:T(8,128)} %refs_4_.1, s32[128,128]{1,0:T(8,128)} %refs_5_.1), custom_call_target="tpu_custom_call" | custom-call | flops 1000000 | bytes 459776 | tf_op jit(solution)/shard_map/normals/pallas_call | solution.py:347
  3.3 0.0 copy-start.3
  3.3 13.3 %all-to-all-start = ((f32[64,4,128]{2,1,0:T(4,128)}), f32[64,4,128]{2,1,0:T(4,128)S(1)}, u32[]{:S(2)}, u32[]{:S(2)}) async-start(f32[64,4,128]{2,1,0:T(4,128)} %bitcast.18), calls=%async_computation | async-start | bytes 262144 | tf_op jit(solution)/shard_map/all_to_all | solution.py:376
  16.6 0.0 copy-done.2
  16.6 0.0 copy-done.3
  16.6 5.5 %source_normals.1.after_ref.own_ref = f32[240,256]{1,0:T(8,128)S(1)} custom-call(s32[128,128]{1,0:T(8,128)S(1)} %copy-done.3, f32[640,128]{1,0:T(8,128)S(1)} %bitcast.15), custom_call_target="tpu_custom_call" | custom-call | flops 4026531840 | bytes 393216 | tf_op jit(solution)/shard_map/source_normals/pallas_call | solution.py:347
  22.1 2.6 %collective-permute-start.5 = (f32[240,256]{1,0:T(8,128)S(1)}, f32[240,256]{1,0:T(8,128)S(1)}, u32[]{:S(2)}, u32[]{:S(2)}) collective-permute-start(f32[240,256]{1,0:T(8,128)S(1)} %source_normals.1.after_ref.own_ref), channel_id=1, source_target_pairs={{0,3},{1,0},{2,1},{3,2},{4,7},{5,4},{6,5},{7,6},{8,11},{9,8},{10,9... | collective-permute-start | bytes 737288 | tf_op jit(solution)/shard_map/ppermute | solution.py:371
  24.7 1.8 %all-to-all-done = f32[64,4,128]{2,1,0:T(4,128)S(1)} async-done(((f32[64,4,128]{2,1,0:T(4,128)}), f32[64,4,128]{2,1,0:T(4,128)S(1)}, u32[]{:S(2)}, u32[]{:S(2)}) %all-to-all-start) | async-done | bytes 131104 | tf_op jit(solution)/shard_map/all_to_all | solution.py:376
  26.5 0.0 copy-start
  26.5 0.0 copy-start.1
  26.5 0.3 bins.1.own_ref
  26.8 2.6 %collective-permute-start.2 = (f32[88,128]{1,0:T(8,128)S(1)}, f32[88,128]{1,0:T(8,128)S(1)}, u32[]{:S(2)}, u32[]{:S(2)}) collective-permute-start(f32[88,128]{1,0:T(8,128)S(1)} %bins.1.own_ref), channel_id=1, source_target_pairs={{0,3},{1,0},{2,1},{3,2},{4,7},{5,4},{6,5},{7,6},{8,11},{9,8},{10,9... | collective-permute-start | bytes 135176 | tf_op jit(solution)/shard_map/ppermute | solution.py:371
  29.3 0.5 collective-permute-start.1
  29.9 0.6 collective-permute-start
  30.5 0.4 collective-permute-done.2.three_ref
  30.9 2.9 %collective-permute-done.1.two_ref = f32[88,128]{1,0:T(8,128)S(1)} collective-permute-done((f32[88,128]{1,0:T(8,128)S(1)}, f32[88,128]{1,0:T(8,128)S(1)}, u32[]{:S(2)}, u32[]{:S(2)}) %collective-permute-start.1) | collective-permute-done | bytes 45088 | tf_op jit(solution)/shard_map/ppermute | solution.py:371
  33.8 0.5 collective-permute-done.one_ref
  34.2 0.0 copy-done
  34.2 2.7 %attitude.1 = (f32[1,4,128]{2,1,0:T(4,128)}, f32[64,128]{1,0:T(8,128)}) custom-call(f32[88,128]{1,0:T(8,128)S(1)} %bins.1.own_ref, f32[88,128]{1,0:T(8,128)S(1)} %collective-permute-done.one_ref, f32[88,128]{1,0:T(8,128)S(1)} %collective-permute-done.1.two_ref, f32[88,128]{1,0:T(8,128)S(1)} %collective-permute-done.2.three_ref, f32[256,128]{1,0:T(8,128)S(1)} %bitcast.13, ...), custom_call_target="tpu_custom_call" | custom-call | flops 1000000 | bytes 480256 | tf_op jit(solution)/shard_map/attitude/pallas_call | solution.py:347
  37.0 8.5 %all-to-all-start.1 = ((f32[64,1,128]{2,1,0:T(1,128)}), f32[64,1,128]{2,1,0:T(1,128)S(1)}, u32[]{:S(2)}, u32[]{:S(2)}) async-start(f32[64,1,128]{2,1,0:T(1,128)} %bitcast.8), calls=%async_computation.1 | async-start | bytes 65536 | tf_op jit(solution)/shard_map/all_to_all | solution.py:376
  45.5 0.0 copy-start.4
  45.5 2.0 %collective-permute-start.4 = (f32[240,256]{1,0:T(8,128)S(1)}, f32[240,256]{1,0:T(8,128)S(1)}, u32[]{:S(2)}, u32[]{:S(2)}) collective-permute-start(f32[240,256]{1,0:T(8,128)S(1)} %source_normals.1.after_ref.own_ref), channel_id=1, source_target_pairs={{0,2},{1,3},{2,0},{3,1},{4,6},{5,7},{6,4},{7,5},{8,10},{9,11},{10,... | collective-permute-start | bytes 737288 | tf_op jit(solution)/shard_map/ppermute | solution.py:371
  47.5 2.0 %collective-permute-start.3 = (f32[240,256]{1,0:T(8,128)S(1)}, f32[240,256]{1,0:T(8,128)S(1)}, u32[]{:S(2)}, u32[]{:S(2)}) collective-permute-start(f32[240,256]{1,0:T(8,128)S(1)} %source_normals.1.after_ref.own_ref), channel_id=1, source_target_pairs={{0,1},{1,2},{2,3},{3,0},{4,5},{5,6},{6,7},{7,4},{8,9},{9,10},{10,1... | collective-permute-start | bytes 737288 | tf_op jit(solution)/shard_map/ppermute | solution.py:371
  49.6 5.0 %all-to-all-done.1 = f32[64,1,128]{2,1,0:T(1,128)S(1)} async-done(((f32[64,1,128]{2,1,0:T(1,128)}), f32[64,1,128]{2,1,0:T(1,128)S(1)}, u32[]{:S(2)}, u32[]{:S(2)}) %all-to-all-start.1) | async-done | bytes 32800 | tf_op jit(solution)/shard_map/all_to_all | solution.py:376
  54.6 0.0 copy-done.1
  54.6 0.0 copy-done.4
  54.6 3.2 %source_right.1.own_ref = f32[80,256]{1,0:T(8,128)S(1)} custom-call(f32[64,128]{1,0:T(8,128)S(1)} %bitcast.14, f32[8,128]{1,0:T(8,128)S(1)} %copy-done.4, f32[768,128]{1,0:T(8,128)S(1)} %copy-done.1, s32[128,128]{1,0:T(8,128)S(1)} %copy-done.3, f32[640,128]{1,0:T(8,128)S(1)} %bitcast.16), custom_call_target="tpu_custom_call" | custom-call | flops 1342177280 | bytes 823296 | tf_op jit(solution)/shard_map/source_right/pallas_call | solution.py:347
  57.8 3.5 %collective-permute-start.8 = (f32[80,256]{1,0:T(8,128)S(1)}, f32[80,256]{1,0:T(8,128)S(1)}, u32[]{:S(2)}, u32[]{:S(2)}) collective-permute-start(f32[80,256]{1,0:T(8,128)S(1)} %source_right.1.own_ref), channel_id=1, source_target_pairs={{0,3},{1,0},{2,1},{3,2},{4,7},{5,4},{6,5},{7,6},{8,11},{9,8},{10,9... | collective-permute-start | bytes 245768 | tf_op jit(solution)/shard_map/ppermute | solution.py:371
  61.3 0.2 collective-permute-start.7
  61.5 0.0 collective-permute-done.5.three_ref
  61.5 0.5 collective-permute-start.6
  62.0 0.0 collective-permute-done.4.two_ref
  62.0 0.0 collective-permute-done.3.one_ref
  62.0 0.1 factors.1.factor_ref
  62.1 1.6 %collective-permute-done.8.three_ref = f32[80,256]{1,0:T(8,128)S(1)} collective-permute-done((f32[80,256]{1,0:T(8,128)S(1)}, f32[80,256]{1,0:T(8,128)S(1)}, u32[]{:S(2)}, u32[]{:S(2)}) %collective-permute-start.8) | collective-permute-done | bytes 81952 | tf_op jit(solution)/shard_map/ppermute | solution.py:371
  63.7 2.5 %collective-permute-done.7.two_ref = f32[80,256]{1,0:T(8,128)S(1)} collective-permute-done((f32[80,256]{1,0:T(8,128)S(1)}, f32[80,256]{1,0:T(8,128)S(1)}, u32[]{:S(2)}, u32[]{:S(2)}) %collective-permute-start.7) | collective-permute-done | bytes 81952 | tf_op jit(solution)/shard_map/ppermute | solution.py:371
  66.2 0.7 %collective-permute-done.6.one_ref = f32[80,256]{1,0:T(8,128)S(1)} collective-permute-done((f32[80,256]{1,0:T(8,128)S(1)}, f32[80,256]{1,0:T(8,128)S(1)}, u32[]{:S(2)}, u32[]{:S(2)}) %collective-permute-start.6) | collective-permute-done | bytes 81952 | tf_op jit(solution)/shard_map/ppermute | solution.py:371
  66.9 0.7 %solve.1 = f32[5,4096]{1,0:T(8,128)} custom-call(f32[240,256]{1,0:T(8,128)S(1)} %factors.1.factor_ref, f32[80,256]{1,0:T(8,128)S(1)} %source_right.1.own_ref, f32[80,256]{1,0:T(8,128)S(1)} %collective-permute-done.6.one_ref, f32[80,256]{1,0:T(8,128)S(1)} %collective-permute-done.7.two_ref, f32[80,256]{1,0:T(8,128)S(1)} %collective-permute-done.8.three_ref), custom_call_target="tpu_custom_call" | custom-call | flops 1000000 | bytes 573440 | tf_op jit(solution)/shard_map/solve/pallas_call | solution.py:347
Async XLA Ops:
  0.6 15.9 %copy-start.2 = (f32[128,5,128]{2,0,1:T(8,128)S(1)}, f32[128,5,128]{2,0,1:T(8,128)}, u32[]{:S(2)}) copy-start(f32[128,5,128]{2,0,1:T(8,128)} %param.14) | copy-start | bytes 983044
  3.3 13.3 %copy-start.3 = (s32[128,128]{1,0:T(8,128)S(1)}, s32[128,128]{1,0:T(8,128)}, u32[]{:S(2)}) copy-start(s32[128,128]{1,0:T(8,128)} %get-tuple-element.9.marked_ref) | copy-start | bytes 196612
  3.3 23.2 %all-to-all-start = ((f32[64,4,128]{2,1,0:T(4,128)}), f32[64,4,128]{2,1,0:T(4,128)S(1)}, u32[]{:S(2)}, u32[]{:S(2)}) async-start(f32[64,4,128]{2,1,0:T(4,128)} %bitcast.18), calls=%async_computation | async-start | bytes 262144 | tf_op jit(solution)/shard_map/all_to_all | solution.py:376
  22.1 39.4 %collective-permute-start.5 = (f32[240,256]{1,0:T(8,128)S(1)}, f32[240,256]{1,0:T(8,128)S(1)}, u32[]{:S(2)}, u32[]{:S(2)}) collective-permute-start(f32[240,256]{1,0:T(8,128)S(1)} %source_normals.1.after_ref.own_ref), channel_id=1, source_target_pairs={{0,3},{1,0},{2,1},{3,2},{4,7},{5,4},{6,5},{7,6},{8,11},{9,8},{10,9... | collective-permute-start | bytes 737288 | tf_op jit(solution)/shard_map/ppermute | solution.py:371
  26.5 7.7 %copy-start = (bf16[120,352]{1,0:T(8,128)(2,1)S(1)}, bf16[120,352]{1,0:T(8,128)(2,1)}, u32[]{:S(2)}) copy-start(bf16[120,352]{1,0:T(8,128)(2,1)} %constant.2.clone.table_ref) | copy-start | bytes 253444
  26.5 28.1 %copy-start.1 = (f32[768,128]{1,0:T(8,128)S(1)}, f32[768,128]{1,0:T(8,128)}, u32[]{:S(2)}) copy-start(f32[768,128]{1,0:T(8,128)} %get-tuple-element.13.obs_ref) | copy-start | bytes 1179652
  26.8 4.1 %collective-permute-start.2 = (f32[88,128]{1,0:T(8,128)S(1)}, f32[88,128]{1,0:T(8,128)S(1)}, u32[]{:S(2)}, u32[]{:S(2)}) collective-permute-start(f32[88,128]{1,0:T(8,128)S(1)} %bins.1.own_ref), channel_id=1, source_target_pairs={{0,3},{1,0},{2,1},{3,2},{4,7},{5,4},{6,5},{7,6},{8,11},{9,8},{10,9... | collective-permute-start | bytes 135176 | tf_op jit(solution)/shard_map/ppermute | solution.py:371
  29.3 4.4 %collective-permute-start.1 = (f32[88,128]{1,0:T(8,128)S(1)}, f32[88,128]{1,0:T(8,128)S(1)}, u32[]{:S(2)}, u32[]{:S(2)}) collective-permute-start(f32[88,128]{1,0:T(8,128)S(1)} %bins.1.own_ref), channel_id=1, source_target_pairs={{0,2},{1,3},{2,0},{3,1},{4,6},{5,7},{6,4},{7,5},{8,10},{9,11},{10,... | collective-permute-start | bytes 135176 | tf_op jit(solution)/shard_map/ppermute | solution.py:371
  29.9 4.4 %collective-permute-start = (f32[88,128]{1,0:T(8,128)S(1)}, f32[88,128]{1,0:T(8,128)S(1)}, u32[]{:S(2)}, u32[]{:S(2)}) collective-permute-start(f32[88,128]{1,0:T(8,128)S(1)} %bins.1.own_ref), channel_id=1, source_target_pairs={{0,1},{1,2},{2,3},{3,0},{4,5},{5,6},{6,7},{7,4},{8,9},{9,10},{10,1... | collective-permute-start | bytes 135176 | tf_op jit(solution)/shard_map/ppermute | solution.py:371
  37.0 17.6 %all-to-all-start.1 = ((f32[64,1,128]{2,1,0:T(1,128)}), f32[64,1,128]{2,1,0:T(1,128)S(1)}, u32[]{:S(2)}, u32[]{:S(2)}) async-start(f32[64,1,128]{2,1,0:T(1,128)} %bitcast.8), calls=%async_computation.1 | async-start | bytes 65536 | tf_op jit(solution)/shard_map/all_to_all | solution.py:376
  45.5 9.1 %copy-start.4 = (f32[8,128]{1,0:T(8,128)S(1)}, f32[8,128]{1,0:T(8,128)}, u32[]{:S(2)}) copy-start(f32[8,128]{1,0:T(8,128)} %get-tuple-element.12.slot_ref) | copy-start | bytes 12292
  45.5 16.5 %collective-permute-start.4 = (f32[240,256]{1,0:T(8,128)S(1)}, f32[240,256]{1,0:T(8,128)S(1)}, u32[]{:S(2)}, u32[]{:S(2)}) collective-permute-start(f32[240,256]{1,0:T(8,128)S(1)} %source_normals.1.after_ref.own_ref), channel_id=1, source_target_pairs={{0,2},{1,3},{2,0},{3,1},{4,6},{5,7},{6,4},{7,5},{8,10},{9,11},{10,... | collective-permute-start | bytes 737288 | tf_op jit(solution)/shard_map/ppermute | solution.py:371
  47.5 14.5 %collective-permute-start.3 = (f32[240,256]{1,0:T(8,128)S(1)}, f32[240,256]{1,0:T(8,128)S(1)}, u32[]{:S(2)}, u32[]{:S(2)}) collective-permute-start(f32[240,256]{1,0:T(8,128)S(1)} %source_normals.1.after_ref.own_ref), channel_id=1, source_target_pairs={{0,1},{1,2},{2,3},{3,0},{4,5},{5,6},{6,7},{7,4},{8,9},{9,10},{10,1... | collective-permute-start | bytes 737288 | tf_op jit(solution)/shard_map/ppermute | solution.py:371
  57.8 5.9 %collective-permute-start.8 = (f32[80,256]{1,0:T(8,128)S(1)}, f32[80,256]{1,0:T(8,128)S(1)}, u32[]{:S(2)}, u32[]{:S(2)}) collective-permute-start(f32[80,256]{1,0:T(8,128)S(1)} %source_right.1.own_ref), channel_id=1, source_target_pairs={{0,3},{1,0},{2,1},{3,2},{4,7},{5,4},{6,5},{7,6},{8,11},{9,8},{10,9... | collective-permute-start | bytes 245768 | tf_op jit(solution)/shard_map/ppermute | solution.py:371
  61.3 4.9 %collective-permute-start.7 = (f32[80,256]{1,0:T(8,128)S(1)}, f32[80,256]{1,0:T(8,128)S(1)}, u32[]{:S(2)}, u32[]{:S(2)}) collective-permute-start(f32[80,256]{1,0:T(8,128)S(1)} %source_right.1.own_ref), channel_id=1, source_target_pairs={{0,2},{1,3},{2,0},{3,1},{4,6},{5,7},{6,4},{7,5},{8,10},{9,11},{10,... | collective-permute-start | bytes 245768 | tf_op jit(solution)/shard_map/ppermute | solution.py:371
  61.5 5.4 %collective-permute-start.6 = (f32[80,256]{1,0:T(8,128)S(1)}, f32[80,256]{1,0:T(8,128)S(1)}, u32[]{:S(2)}, u32[]{:S(2)}) collective-permute-start(f32[80,256]{1,0:T(8,128)S(1)} %source_right.1.own_ref), channel_id=1, source_target_pairs={{0,1},{1,2},{2,3},{3,0},{4,5},{5,6},{6,7},{7,4},{8,9},{9,10},{10,1... | collective-permute-start | bytes 245768 | tf_op jit(solution)/shard_map/ppermute | solution.py:371

commit v8 on v7

--- a/solution.py
+++ b/solution.py
@@ -152,11 +152,14 @@
     del after_ref
     got = got_ref[...].T
     place = indicator(iota_f((KNOTS_W, SLOTS), 0) == got[BIN_AT : BIN_AT + 1, :])
-    out_ref[...] = exact_dot(got[:FEATS], place, NT)
-
-
-def attitude_kernel(own_ref, one_ref, two_ref, three_ref, got_ref, table_ref, att_ref, reply_ref):
-    total = ((own_ref[...] + two_ref[...]) + (one_ref[...] + three_ref[...])) * (1.0 / 36.0)
+    moments = exact_dot(got[:FEATS], place, NT)
+    for at in range(N_CCD):
+        out_ref[at] = moments
+
+
+def attitude_kernel(parts_ref, got_ref, table_ref, normal_ref, att_ref, reply_ref, passed_ref):
+    del normal_ref, passed_ref
+    total = ((parts_ref[0] + parts_ref[1]) + (parts_ref[2] + parts_ref[3])) * (1.0 / 36.0)
     moved = jnp.concatenate([total] + [pltpu.roll(total, l, 1) for l in range(1, 4)], axis=0)
     band = exact_dot(moved, table_ref[...], NN, swap=True)
     groups = [band[8 * at : 8 * at + 8] for at in range(14)]
@@ -288,7 +291,7 @@
     values = values.T
     for p in range(5):
         put_terms(terms_ref, p, gain_ref[NBLK * p : NBLK * p + NBLK, :] * values)
-    source_sums(5, 64, terms_ref, high_ref, low_ref, out_ref, *work)
+    source_sums(5, NBLK, terms_ref, high_ref, low_ref, out_ref, *work)
 
 
 def factor_kernel(own_ref, one_ref, two_ref, three_ref, out_ref):
@@ -370,6 +373,10 @@
     return [
         lax.ppermute(values, "ccd", [(at, (at + shift) % N_CCD) for at in range(N_CCD)]) for shift in range(1, N_CCD)
     ]
+
+
+def among_ccd(copies):
+    return lax.all_to_all(copies, "ccd", split_axis=0, concat_axis=0, tiled=True)
 
 
 def to_windows(values):
@@ -413,15 +420,17 @@
         scratch=segment_scratch(15),
         flops=2 * 480 * 256 * 16384,
     )
-    moments = kernel_call(bins_kernel, "bins", f32(FEATS, KNOTS_W), got, normal, far=(1,))
-    attitude, reply = kernel_call(
+    moments = kernel_call(bins_kernel, "bins", f32(N_CCD, FEATS, KNOTS_W), got, normal, far=(1,))
+    attitude, reply, normal = kernel_call(
         attitude_kernel,
         "attitude",
-        (f32(1, 4, KNOTS_W), f32(WINDOWS, 128)),
-        moments,
-        *from_others(moments),
+        (f32(1, 4, KNOTS_W), f32(WINDOWS, 128), f32(15 * HIGH, LOW)),
+        among_ccd(moments),
         got,
         jnp.asarray(knot_matrix()),
+        normal,
+        far=(3,),
+        passed={3: 2},
     )
     knots = to_windows(reply)
     factors = kernel_call(factor_kernel, "factors", f32(15 * HIGH, LOW), normal, *from_others(normal))

time: 67.9 us -> 68 us (level)
  starting transfers between devices: 36.2 us -> 25.6 us
  blocking collectives: 0 us -> 9.04 us
  waiting for transfers between devices: 15.4 us -> 17.3 us
    ppermute x9 -> x6, starting transfers between devices: 14.4 us -> 4.6 us  [from_others(): lax.ppermute(values, 'ccd', [(at, (at + shift) % N_CCD) for at in range(N...]
    all_to_all x0 -> x1, blocking collectives: none -> 9.04 us  [among_ccd(): lax.all_to_all(copies, 'ccd', split_axis=0, concat_axis=0, tiled=True)]
    all_to_all x2, waiting for transfers between devices: 6.86 us -> 12.3 us  [to_windows(): lax.all_to_all(values, ('src', 'win'), split_axis=0, concat_axis=0, tiled...]
    ppermute x9 -> x6, waiting for transfers between devices: 8.58 us -> 5.01 us  [from_others(): lax.ppermute(values, 'ccd', [(at, (at + shift) % N_CCD) for at in range(N...]
    all_to_all x2, starting transfers between devices: 21.8 us -> 20.9 us  [to_windows(): lax.all_to_all(values, ('src', 'win'), split_axis=0, concat_axis=0, tiled...]
  transfers between devices with their start and end apart: 11 -> 8, of which waited for: 8 -> 6; matrix products, arithmetic and copies ran while one was open for 0% -> 0% of each run, Pallas kernels for 18% -> 13%
where the time goes in v8:
time: 68 us; the launch traced here: 67.7 us
  starting transfers between devices  25.6 us (38%)
  waiting for transfers between devices  17.3 us (25%)
  Pallas kernels  15 us (22%)
  blocking collectives  9.04 us (13%)
  between operations  0.74 us (1%)
    all_to_all x2, starting transfers between devices, to_windows(): lax.all_to_all(values, ('src', 'win'), split_axis=0, concat_axis=0, tiled...  20.9 us
    pallas_call x7, Pallas kernels, kernel_call(): pl.pallas_call(body, out_shape=outs, in_specs=[pl.BlockSpec(memory_space=...  15 us
    all_to_all x2, waiting for transfers between devices, to_windows(): lax.all_to_all(values, ('src', 'win'), split_axis=0, concat_axis=0, tiled...  12.3 us
    all_to_all x1, blocking collectives, among_ccd(): lax.all_to_all(copies, 'ccd', split_axis=0, concat_axis=0, tiled=True)  9.04 us
    ppermute x6, waiting for transfers between devices, from_others(): lax.ppermute(values, 'ccd', [(at, (at + shift) % N_CCD) for at in range(N...  5.01 us
    ppermute x6, starting transfers between devices, from_others(): lax.ppermute(values, 'ccd', [(at, (at + shift) % N_CCD) for at in range(N...  4.6 us
  transfers between devices with their start and end apart: 8, of which 6 were waited for; matrix products, arithmetic and copies ran while one was open for 0% of the time, Pallas kernels for 13%

profile of v8, /device:TPU:1, one launch (start us, length us, event | category | flops | bytes accessed | tf_op | source)
XLA Modules:
  0.0 67.7 jit_solution(14632637315390371069)
XLA Ops:
  0.6 0.0 copy-start.2
  0.6 2.6 %normals.1 = (f32[256,128]{1,0:T(8,128)}, f32[768,128]{1,0:T(8,128)}, f32[8,128]{1,0:T(8,128)}, s32[128,128]{1,0:T(8,128)}) custom-call(s32[1,128]{1,0:T(1,128)} %bitcast.19, s32[1,128]{1,0:T(1,128)} %bitcast.20, f32[128,128]{1,0:T(8,128)} %refs_2_.1, f32[512,128]{1,0:T(8,128)} %bitcast.17, f32[128,128]{1,0:T(8,128)} %refs_4_.1, s32[128,128]{1,0:T(8,128)} %refs_5_.1), custom_call_target="tpu_custom_call" | custom-call | flops 1000000 | bytes 459776 | tf_op jit(solution)/shard_map/normals/pallas_call | solution.py:350
  3.3 0.0 copy-start.3
  3.3 13.3 %all-to-all-start = ((f32[64,4,128]{2,1,0:T(4,128)}), f32[64,4,128]{2,1,0:T(4,128)S(1)}, u32[]{:S(2)}, u32[]{:S(2)}) async-start(f32[64,4,128]{2,1,0:T(4,128)} %bitcast.18), calls=%async_computation | async-start | bytes 262144 | tf_op jit(solution)/shard_map/all_to_all | solution.py:383
  16.6 0.0 copy-done.2
  16.6 0.0 copy-done.3
  16.6 5.5 %source_normals.1.after_ref.normal_ref = f32[240,256]{1,0:T(8,128)S(1)} custom-call(s32[128,128]{1,0:T(8,128)S(1)} %copy-done.3, f32[640,128]{1,0:T(8,128)S(1)} %bitcast.15), custom_call_target="tpu_custom_call" | custom-call | flops 4026531840 | bytes 393216 | tf_op jit(solution)/shard_map/source_normals/pallas_call | solution.py:350
  22.1 4.4 %all-to-all-done = f32[64,4,128]{2,1,0:T(4,128)S(1)} async-done(((f32[64,4,128]{2,1,0:T(4,128)}), f32[64,4,128]{2,1,0:T(4,128)S(1)}, u32[]{:S(2)}, u32[]{:S(2)}) %all-to-all-start) | async-done | bytes 131104 | tf_op jit(solution)/shard_map/all_to_all | solution.py:383
  26.5 0.3 bins.1
  26.8 0.0 copy-start
  26.8 9.0 %all_to_all.21.parts_ref = f32[4,88,128]{2,1,0:T(8,128)S(1)} all-to-all(f32[4,88,128]{2,1,0:T(8,128)S(1)} %bins.1), channel_id=1, replica_groups=mesh['src'=16,'win'=4,'ccd'=4] {'ccd'}, dimensions={0} | all-to-all | bytes 360448 | tf_op jit(solution)/shard_map/all_to_all | solution.py:379
  35.9 0.0 copy-done
  35.9 0.0 copy-start.1
  35.9 2.7 %attitude.1 = (f32[1,4,128]{2,1,0:T(4,128)}, f32[64,128]{1,0:T(8,128)}, f32[240,256]{1,0:T(8,128)S(1)}) custom-call(f32[4,88,128]{2,1,0:T(8,128)S(1)} %all_to_all.21.parts_ref, f32[256,128]{1,0:T(8,128)S(1)} %bitcast.13, bf16[120,352]{1,0:T(8,128)(2,1)S(1)} %copy-done, f32[240,256]{1,0:T(8,128)S(1)} %source_normals.1.after_ref.normal_ref), custom_call_target="tpu_custom_call", output_to_operand_aliasing={{2}: (3, {})} | custom-call | flops 1000000 | bytes 726016 | tf_op jit(solution)/shard_map/attitude/pallas_call | solution.py:350
  38.6 0.9 %collective-permute-start.2 = (f32[240,256]{1,0:T(8,128)S(1)}, f32[240,256]{1,0:T(8,128)S(1)}, u32[]{:S(2)}, u32[]{:S(2)}) collective-permute-start(f32[240,256]{1,0:T(8,128)S(1)} %get-tuple-element.12.own_ref), channel_id=1, source_target_pairs={{0,3},{1,0},{2,1},{3,2},{4,7},{5,4},{6,5},{7,6},{8,11},{9,8},{10,9... | collective-permute-start | bytes 737288 | tf_op jit(solution)/shard_map/ppermute | solution.py:374
  39.5 7.6 %all-to-all-start.2 = ((f32[64,1,128]{2,1,0:T(1,128)}), f32[64,1,128]{2,1,0:T(1,128)S(1)}, u32[]{:S(2)}, u32[]{:S(2)}) async-start(f32[64,1,128]{2,1,0:T(1,128)} %bitcast.8), calls=%async_computation.2 | async-start | bytes 65536 | tf_op jit(solution)/shard_map/all_to_all | solution.py:383
  47.1 0.0 copy-start.4
  47.1 1.3 %collective-permute-start.1 = (f32[240,256]{1,0:T(8,128)S(1)}, f32[240,256]{1,0:T(8,128)S(1)}, u32[]{:S(2)}, u32[]{:S(2)}) collective-permute-start(f32[240,256]{1,0:T(8,128)S(1)} %get-tuple-element.12.own_ref), channel_id=1, source_target_pairs={{0,2},{1,3},{2,0},{3,1},{4,6},{5,7},{6,4},{7,5},{8,10},{9,11},{10,... | collective-permute-start | bytes 737288 | tf_op jit(solution)/shard_map/ppermute | solution.py:374
  48.4 0.0 collective-permute-start
  48.4 7.9 %all-to-all-done.2 = f32[64,1,128]{2,1,0:T(1,128)S(1)} async-done(((f32[64,1,128]{2,1,0:T(1,128)}), f32[64,1,128]{2,1,0:T(1,128)S(1)}, u32[]{:S(2)}, u32[]{:S(2)}) %all-to-all-start.2) | async-done | bytes 32800 | tf_op jit(solution)/shard_map/all_to_all | solution.py:383
  56.3 0.0 copy-done.1
  56.3 0.0 copy-done.4
  56.3 3.0 %source_right.1.own_ref = f32[80,256]{1,0:T(8,128)S(1)} custom-call(f32[64,128]{1,0:T(8,128)S(1)} %bitcast.14, f32[8,128]{1,0:T(8,128)S(1)} %copy-done.4, f32[768,128]{1,0:T(8,128)S(1)} %copy-done.1, s32[128,128]{1,0:T(8,128)S(1)} %copy-done.3, f32[640,128]{1,0:T(8,128)S(1)} %bitcast.16), custom_call_target="tpu_custom_call" | custom-call | flops 1342177280 | bytes 823296 | tf_op jit(solution)/shard_map/source_right/pallas_call | solution.py:350
  59.4 0.2 collective-permute-start.5
  59.6 2.2 %collective-permute-start.4 = (f32[80,256]{1,0:T(8,128)S(1)}, f32[80,256]{1,0:T(8,128)S(1)}, u32[]{:S(2)}, u32[]{:S(2)}) collective-permute-start(f32[80,256]{1,0:T(8,128)S(1)} %source_right.1.own_ref), channel_id=1, source_target_pairs={{0,2},{1,3},{2,0},{3,1},{4,6},{5,7},{6,4},{7,5},{8,10},{9,11},{10,... | collective-permute-start | bytes 245768 | tf_op jit(solution)/shard_map/ppermute | solution.py:374
  61.8 0.0 collective-permute-done.2.three_ref
  61.8 0.0 collective-permute-start.3
  61.8 0.0 collective-permute-done.1.two_ref
  61.8 0.1 collective-permute-done.one_ref
  61.9 0.1 factors.1.factor_ref
  62.0 0.8 %collective-permute-done.5.three_ref = f32[80,256]{1,0:T(8,128)S(1)} collective-permute-done((f32[80,256]{1,0:T(8,128)S(1)}, f32[80,256]{1,0:T(8,128)S(1)}, u32[]{:S(2)}, u32[]{:S(2)}) %collective-permute-start.5) | collective-permute-done | bytes 81952 | tf_op jit(solution)/shard_map/ppermute | solution.py:374
  62.7 1.7 %collective-permute-done.4.two_ref = f32[80,256]{1,0:T(8,128)S(1)} collective-permute-done((f32[80,256]{1,0:T(8,128)S(1)}, f32[80,256]{1,0:T(8,128)S(1)}, u32[]{:S(2)}, u32[]{:S(2)}) %collective-permute-start.4) | collective-permute-done | bytes 81952 | tf_op jit(solution)/shard_map/ppermute | solution.py:374
  64.4 2.5 %collective-permute-done.3.one_ref = f32[80,256]{1,0:T(8,128)S(1)} collective-permute-done((f32[80,256]{1,0:T(8,128)S(1)}, f32[80,256]{1,0:T(8,128)S(1)}, u32[]{:S(2)}, u32[]{:S(2)}) %collective-permute-start.3) | collective-permute-done | bytes 81952 | tf_op jit(solution)/shard_map/ppermute | solution.py:374
  66.9 0.7 %solve.1 = f32[5,4096]{1,0:T(8,128)} custom-call(f32[240,256]{1,0:T(8,128)S(1)} %factors.1.factor_ref, f32[80,256]{1,0:T(8,128)S(1)} %source_right.1.own_ref, f32[80,256]{1,0:T(8,128)S(1)} %collective-permute-done.3.one_ref, f32[80,256]{1,0:T(8,128)S(1)} %collective-permute-done.4.two_ref, f32[80,256]{1,0:T(8,128)S(1)} %collective-permute-done.5.three_ref), custom_call_target="tpu_custom_call" | custom-call | flops 1000000 | bytes 573440 | tf_op jit(solution)/shard_map/solve/pallas_call | solution.py:350
Async XLA Ops:
  0.6 15.9 %copy-start.2 = (f32[128,5,128]{2,0,1:T(8,128)S(1)}, f32[128,5,128]{2,0,1:T(8,128)}, u32[]{:S(2)}) copy-start(f32[128,5,128]{2,0,1:T(8,128)} %param.14) | copy-start | bytes 983044
  3.3 13.3 %copy-start.3 = (s32[128,128]{1,0:T(8,128)S(1)}, s32[128,128]{1,0:T(8,128)}, u32[]{:S(2)}) copy-start(s32[128,128]{1,0:T(8,128)} %get-tuple-element.10.marked_ref) | copy-start | bytes 196612
  3.3 23.2 %all-to-all-start = ((f32[64,4,128]{2,1,0:T(4,128)}), f32[64,4,128]{2,1,0:T(4,128)S(1)}, u32[]{:S(2)}, u32[]{:S(2)}) async-start(f32[64,4,128]{2,1,0:T(4,128)} %bitcast.18), calls=%async_computation | async-start | bytes 262144 | tf_op jit(solution)/shard_map/all_to_all | solution.py:383
  26.8 9.1 %copy-start = (bf16[120,352]{1,0:T(8,128)(2,1)S(1)}, bf16[120,352]{1,0:T(8,128)(2,1)}, u32[]{:S(2)}) copy-start(bf16[120,352]{1,0:T(8,128)(2,1)} %constant.2.clone.table_ref) | copy-start | bytes 253444
  35.9 20.5 %copy-start.1 = (f32[768,128]{1,0:T(8,128)S(1)}, f32[768,128]{1,0:T(8,128)}, u32[]{:S(2)}) copy-start(f32[768,128]{1,0:T(8,128)} %get-tuple-element.15.obs_ref) | copy-start | bytes 1179652
  38.6 23.2 %collective-permute-start.2 = (f32[240,256]{1,0:T(8,128)S(1)}, f32[240,256]{1,0:T(8,128)S(1)}, u32[]{:S(2)}, u32[]{:S(2)}) collective-permute-start(f32[240,256]{1,0:T(8,128)S(1)} %get-tuple-element.12.own_ref), channel_id=1, source_target_pairs={{0,3},{1,0},{2,1},{3,2},{4,7},{5,4},{6,5},{7,6},{8,11},{9,8},{10,9... | collective-permute-start | bytes 737288 | tf_op jit(solution)/shard_map/ppermute | solution.py:374
  39.5 16.9 %all-to-all-start.2 = ((f32[64,1,128]{2,1,0:T(1,128)}), f32[64,1,128]{2,1,0:T(1,128)S(1)}, u32[]{:S(2)}, u32[]{:S(2)}) async-start(f32[64,1,128]{2,1,0:T(1,128)} %bitcast.8), calls=%async_computation.2 | async-start | bytes 65536 | tf_op jit(solution)/shard_map/all_to_all | solution.py:383
  47.1 9.2 %copy-start.4 = (f32[8,128]{1,0:T(8,128)S(1)}, f32[8,128]{1,0:T(8,128)}, u32[]{:S(2)}) copy-start(f32[8,128]{1,0:T(8,128)} %get-tuple-element.14.slot_ref) | copy-start | bytes 12292
  47.1 14.7 %collective-permute-start.1 = (f32[240,256]{1,0:T(8,128)S(1)}, f32[240,256]{1,0:T(8,128)S(1)}, u32[]{:S(2)}, u32[]{:S(2)}) collective-permute-start(f32[240,256]{1,0:T(8,128)S(1)} %get-tuple-element.12.own_ref), channel_id=1, source_target_pairs={{0,2},{1,3},{2,0},{3,1},{4,6},{5,7},{6,4},{7,5},{8,10},{9,11},{10,... | collective-permute-start | bytes 737288 | tf_op jit(solution)/shard_map/ppermute | solution.py:374
  48.4 13.5 %collective-permute-start = (f32[240,256]{1,0:T(8,128)S(1)}, f32[240,256]{1,0:T(8,128)S(1)}, u32[]{:S(2)}, u32[]{:S(2)}) collective-permute-start(f32[240,256]{1,0:T(8,128)S(1)} %get-tuple-element.12.own_ref), channel_id=1, source_target_pairs={{0,1},{1,2},{2,3},{3,0},{4,5},{5,6},{6,7},{7,4},{8,9},{9,10},{10,1... | collective-permute-start | bytes 737288 | tf_op jit(solution)/shard_map/ppermute | solution.py:374
  59.4 3.4 %collective-permute-start.5 = (f32[80,256]{1,0:T(8,128)S(1)}, f32[80,256]{1,0:T(8,128)S(1)}, u32[]{:S(2)}, u32[]{:S(2)}) collective-permute-start(f32[80,256]{1,0:T(8,128)S(1)} %source_right.1.own_ref), channel_id=1, source_target_pairs={{0,3},{1,0},{2,1},{3,2},{4,7},{5,4},{6,5},{7,6},{8,11},{9,8},{10,9... | collective-permute-start | bytes 245768 | tf_op jit(solution)/shard_map/ppermute | solution.py:374
  59.6 4.8 %collective-permute-start.4 = (f32[80,256]{1,0:T(8,128)S(1)}, f32[80,256]{1,0:T(8,128)S(1)}, u32[]{:S(2)}, u32[]{:S(2)}) collective-permute-start(f32[80,256]{1,0:T(8,128)S(1)} %source_right.1.own_ref), channel_id=1, source_target_pairs={{0,2},{1,3},{2,0},{3,1},{4,6},{5,7},{6,4},{7,5},{8,10},{9,11},{10,... | collective-permute-start | bytes 245768 | tf_op jit(solution)/shard_map/ppermute | solution.py:374
  61.8 5.1 %collective-permute-start.3 = (f32[80,256]{1,0:T(8,128)S(1)}, f32[80,256]{1,0:T(8,128)S(1)}, u32[]{:S(2)}, u32[]{:S(2)}) collective-permute-start(f32[80,256]{1,0:T(8,128)S(1)} %source_right.1.own_ref), channel_id=1, source_target_pairs={{0,1},{1,2},{2,3},{3,0},{4,5},{5,6},{6,7},{7,4},{8,9},{9,10},{10,1... | collective-permute-start | bytes 245768 | tf_op jit(solution)/shard_map/ppermute | solution.py:374

commit v9 on v7

--- a/solution.py
+++ b/solution.py
@@ -155,7 +155,8 @@
     out_ref[...] = exact_dot(got[:FEATS], place, NT)
 
 
-def attitude_kernel(own_ref, one_ref, two_ref, three_ref, got_ref, table_ref, att_ref, reply_ref):
+def attitude_kernel(own_ref, one_ref, two_ref, three_ref, got_ref, table_ref, after_ref, att_ref, reply_ref):
+    del after_ref
     total = ((own_ref[...] + two_ref[...]) + (one_ref[...] + three_ref[...])) * (1.0 / 36.0)
     moved = jnp.concatenate([total] + [pltpu.roll(total, l, 1) for l in range(1, 4)], axis=0)
     band = exact_dot(moved, table_ref[...], NN, swap=True)
@@ -288,14 +289,19 @@
     values = values.T
     for p in range(5):
         put_terms(terms_ref, p, gain_ref[NBLK * p : NBLK * p + NBLK, :] * values)
-    source_sums(5, 64, terms_ref, high_ref, low_ref, out_ref, *work)
-
-
-def factor_kernel(own_ref, one_ref, two_ref, three_ref, out_ref):
+    source_sums(5, NBLK, terms_ref, high_ref, low_ref, out_ref, *work)
+
+
+def pair_kernel(own_ref, other_ref, out_ref):
+    out_ref[...] = own_ref[...] + other_ref[...]
+
+
+def factor_kernel(own_ref, other_ref, after_ref, out_ref):
+    del after_ref
     entries = {}
     for at, pair in enumerate(PAIR_LIST):
         rows = slice(HIGH * at, HIGH * at + HIGH)
-        total = (own_ref[rows, :] + two_ref[rows, :]) + (one_ref[rows, :] + three_ref[rows, :])
+        total = own_ref[rows, :] + other_ref[rows, :]
         entries[pair] = total + SOURCE_PRIOR if pair[0] == pair[1] else total
     lower = {}
     for column in range(5):
@@ -364,6 +370,10 @@
         pltpu.VMEM((NBLK, ROWS), F32),
         pltpu.VMEM((LOW, 2 * count * HIGH), F32),
     )
+
+
+def swapped(values, partner):
+    return lax.ppermute(values, "ccd", list(enumerate(partner)))
 
 
 def from_others(values):
@@ -414,6 +424,8 @@
         flops=2 * 480 * 256 * 16384,
     )
     moments = kernel_call(bins_kernel, "bins", f32(FEATS, KNOTS_W), got, normal, far=(1,))
+    normal = kernel_call(pair_kernel, "pairs", f32(15 * HIGH, LOW), normal, swapped(normal, (1, 0, 3, 2)))
+    other = swapped(normal, (3, 2, 1, 0))
     attitude, reply = kernel_call(
         attitude_kernel,
         "attitude",
@@ -422,9 +434,10 @@
         *from_others(moments),
         got,
         jnp.asarray(knot_matrix()),
+        normal,
+        far=(6,),
     )
     knots = to_windows(reply)
-    factors = kernel_call(factor_kernel, "factors", f32(15 * HIGH, LOW), normal, *from_others(normal))
     right = kernel_call(
         source_right_kernel,
         "source_right",
@@ -437,6 +450,7 @@
         scratch=segment_scratch(5),
         flops=2 * 160 * 256 * 16384,
     )
+    factors = kernel_call(factor_kernel, "factors", f32(15 * HIGH, LOW), normal, other, right, far=(2,))
     source_delta = kernel_call(solve_kernel, "solve", f32(5, SRC_DEV), factors, right, *from_others(right))
     return attitude, source_delta
 

time: 67.9 us -> 67.2 us (0.990)
  starting transfers between devices: 36.2 us -> 33.4 us
  waiting for transfers between devices: 15.4 us -> 17.4 us
    ppermute x9 -> x6, starting transfers between devices: 14.4 us -> 7.64 us  [from_others(): lax.ppermute(values, 'ccd', [(at, (at + shift) % N_CCD) for at in range(N...]
    all_to_all x2, waiting for transfers between devices: 6.86 us -> 11.9 us  [to_windows(): lax.all_to_all(values, ('src', 'win'), split_axis=0, concat_axis=0, tiled...]
    ppermute x9 -> x6, waiting for transfers between devices: 8.58 us -> 5.47 us  [from_others(): lax.ppermute(values, 'ccd', [(at, (at + shift) % N_CCD) for at in range(N...]
    all_to_all x2, starting transfers between devices: 21.8 us -> 24.2 us  [to_windows(): lax.all_to_all(values, ('src', 'win'), split_axis=0, concat_axis=0, tiled...]
    ppermute x0 -> x2, starting transfers between devices: none -> 1.56 us  [swapped(): return lax.ppermute(values, 'ccd', list(enumerate(partner)))]
    pallas_call x7 -> x8, Pallas kernels: 15.2 us -> 15 us  [kernel_call(): pl.pallas_call(body, out_shape=outs, in_specs=[pl.BlockSpec(memory_space=...]
  transfers between devices with their start and end apart: 11 -> 10, of which waited for: 8 -> 7; matrix products, arithmetic and copies ran while one was open for 0% -> 0% of each run, Pallas kernels for 18% -> 13%
where the time goes in v9:
time: 67.2 us; the launch traced here: 66.6 us
  starting transfers between devices  33.4 us (50%)
  waiting for transfers between devices  17.4 us (26%)
  Pallas kernels  15 us (22%)
  between operations  0.76 us (1%)
    all_to_all x2, starting transfers between devices, to_windows(): lax.all_to_all(values, ('src', 'win'), split_axis=0, concat_axis=0, tiled...  24.2 us
    pallas_call x8, Pallas kernels, kernel_call(): pl.pallas_call(body, out_shape=outs, in_specs=[pl.BlockSpec(memory_space=...  15 us
    all_to_all x2, waiting for transfers between devices, to_windows(): lax.all_to_all(values, ('src', 'win'), split_axis=0, concat_axis=0, tiled...  11.9 us
    ppermute x6, starting transfers between devices, from_others(): lax.ppermute(values, 'ccd', [(at, (at + shift) % N_CCD) for at in range(N...  7.64 us
    ppermute x6, waiting for transfers between devices, from_others(): lax.ppermute(values, 'ccd', [(at, (at + shift) % N_CCD) for at in range(N...  5.47 us
    ppermute x2, starting transfers between devices, swapped(): return lax.ppermute(values, 'ccd', list(enumerate(partner)))  1.56 us
  transfers between devices with their start and end apart: 10, of which 7 were waited for; matrix products, arithmetic and copies ran while one was open for 0% of the time, Pallas kernels for 13%

profile of v9, /device:TPU:1, one launch (start us, length us, event | category | flops | bytes accessed | tf_op | source)
XLA Modules:
  0.0 66.6 jit_solution(15625658894440302168)
XLA Ops:
  0.6 0.0 copy-start.2
  0.6 2.6 %normals.1 = (f32[256,128]{1,0:T(8,128)}, f32[768,128]{1,0:T(8,128)}, f32[8,128]{1,0:T(8,128)}, s32[128,128]{1,0:T(8,128)}) custom-call(s32[1,128]{1,0:T(1,128)} %bitcast.19, s32[1,128]{1,0:T(1,128)} %bitcast.20, f32[128,128]{1,0:T(8,128)} %refs_2_.1, f32[512,128]{1,0:T(8,128)} %bitcast.17, f32[128,128]{1,0:T(8,128)} %refs_4_.1, s32[128,128]{1,0:T(8,128)} %refs_5_.1), custom_call_target="tpu_custom_call" | custom-call | flops 1000000 | bytes 459776 | tf_op jit(solution)/shard_map/normals/pallas_call | solution.py:353
  3.3 0.0 copy-start.3
  3.3 13.3 %all-to-all-start = ((f32[64,4,128]{2,1,0:T(4,128)}), f32[64,4,128]{2,1,0:T(4,128)S(1)}, u32[]{:S(2)}, u32[]{:S(2)}) async-start(f32[64,4,128]{2,1,0:T(4,128)} %bitcast.18), calls=%async_computation | async-start | bytes 262144 | tf_op jit(solution)/shard_map/all_to_all | solution.py:386
  16.6 0.0 copy-done.2
  16.6 0.0 copy-done.3
  16.6 5.5 %source_normals.1.after_ref.own_ref = f32[240,256]{1,0:T(8,128)S(1)} custom-call(s32[128,128]{1,0:T(8,128)S(1)} %copy-done.3, f32[640,128]{1,0:T(8,128)S(1)} %bitcast.15), custom_call_target="tpu_custom_call" | custom-call | flops 4026531840 | bytes 393216 | tf_op jit(solution)/shard_map/source_normals/pallas_call | solution.py:353
  22.1 1.3 %collective-permute-start.3 = (f32[240,256]{1,0:T(8,128)S(1)}, f32[240,256]{1,0:T(8,128)S(1)}, u32[]{:S(2)}, u32[]{:S(2)}) collective-permute-start(f32[240,256]{1,0:T(8,128)S(1)} %source_normals.1.after_ref.own_ref), channel_id=1, source_target_pairs={{0,1},{1,0},{2,3},{3,2},{4,5},{5,4},{6,7},{7,6},{8,9},{9,8},{10,11... | collective-permute-start | bytes 737288 | tf_op jit(solution)/shard_map/ppermute | solution.py:376
  23.4 3.1 %all-to-all-done = f32[64,4,128]{2,1,0:T(4,128)S(1)} async-done(((f32[64,4,128]{2,1,0:T(4,128)}), f32[64,4,128]{2,1,0:T(4,128)S(1)}, u32[]{:S(2)}, u32[]{:S(2)}) %all-to-all-start) | async-done | bytes 131104 | tf_op jit(solution)/shard_map/all_to_all | solution.py:386
  26.5 0.3 bins.1.own_ref
  26.8 0.0 copy-start
  26.8 1.3 %collective-permute-start = (f32[88,128]{1,0:T(8,128)S(1)}, f32[88,128]{1,0:T(8,128)S(1)}, u32[]{:S(2)}, u32[]{:S(2)}) collective-permute-start(f32[88,128]{1,0:T(8,128)S(1)} %bins.1.own_ref), channel_id=1, source_target_pairs={{0,1},{1,2},{2,3},{3,0},{4,5},{5,6},{6,7},{7,4},{8,9},{9,10},{10,1... | collective-permute-start | bytes 135176 | tf_op jit(solution)/shard_map/ppermute | solution.py:381
  28.1 2.5 %collective-permute-start.1 = (f32[88,128]{1,0:T(8,128)S(1)}, f32[88,128]{1,0:T(8,128)S(1)}, u32[]{:S(2)}, u32[]{:S(2)}) collective-permute-start(f32[88,128]{1,0:T(8,128)S(1)} %bins.1.own_ref), channel_id=1, source_target_pairs={{0,2},{1,3},{2,0},{3,1},{4,6},{5,7},{6,4},{7,5},{8,10},{9,11},{10,... | collective-permute-start | bytes 135176 | tf_op jit(solution)/shard_map/ppermute | solution.py:381
  30.5 1.2 %collective-permute-start.2 = (f32[88,128]{1,0:T(8,128)S(1)}, f32[88,128]{1,0:T(8,128)S(1)}, u32[]{:S(2)}, u32[]{:S(2)}) collective-permute-start(f32[88,128]{1,0:T(8,128)S(1)} %bins.1.own_ref), channel_id=1, source_target_pairs={{0,3},{1,0},{2,1},{3,2},{4,7},{5,4},{6,5},{7,6},{8,11},{9,8},{10,9... | collective-permute-start | bytes 135176 | tf_op jit(solution)/shard_map/ppermute | solution.py:381
  31.7 0.0 collective-permute-done.3.other_ref
  31.7 0.0 copy-start.1
  31.7 0.0 collective-permute-done.one_ref
  31.7 1.3 %collective-permute-done.1.two_ref = f32[88,128]{1,0:T(8,128)S(1)} collective-permute-done((f32[88,128]{1,0:T(8,128)S(1)}, f32[88,128]{1,0:T(8,128)S(1)}, u32[]{:S(2)}, u32[]{:S(2)}) %collective-permute-start.1) | collective-permute-done | bytes 45088 | tf_op jit(solution)/shard_map/ppermute | solution.py:381
  33.1 0.7 %collective-permute-done.2.three_ref = f32[88,128]{1,0:T(8,128)S(1)} collective-permute-done((f32[88,128]{1,0:T(8,128)S(1)}, f32[88,128]{1,0:T(8,128)S(1)}, u32[]{:S(2)}, u32[]{:S(2)}) %collective-permute-start.2) | collective-permute-done | bytes 45088 | tf_op jit(solution)/shard_map/ppermute | solution.py:381
  33.7 0.0 copy-done
  33.7 2.7 %attitude.1 = (f32[1,4,128]{2,1,0:T(4,128)}, f32[64,128]{1,0:T(8,128)}) custom-call(f32[88,128]{1,0:T(8,128)S(1)} %bins.1.own_ref, f32[88,128]{1,0:T(8,128)S(1)} %collective-permute-done.one_ref, f32[88,128]{1,0:T(8,128)S(1)} %collective-permute-done.1.two_ref, f32[88,128]{1,0:T(8,128)S(1)} %collective-permute-done.2.three_ref, f32[256,128]{1,0:T(8,128)S(1)} %bitcast.13, ...), custom_call_target="tpu_custom_call" | custom-call | flops 1000000 | bytes 726016 | tf_op jit(solution)/shard_map/attitude/pallas_call | solution.py:353
  36.5 10.9 %all-to-all-start.1 = ((f32[64,1,128]{2,1,0:T(1,128)}), f32[64,1,128]{2,1,0:T(1,128)S(1)}, u32[]{:S(2)}, u32[]{:S(2)}) async-start(f32[64,1,128]{2,1,0:T(1,128)} %bitcast.8), calls=%async_computation.1 | async-start | bytes 65536 | tf_op jit(solution)/shard_map/all_to_all | solution.py:386
  47.4 0.0 copy-start.4
  47.4 0.3 collective-permute-start.4
  47.7 8.8 %all-to-all-done.1 = f32[64,1,128]{2,1,0:T(1,128)S(1)} async-done(((f32[64,1,128]{2,1,0:T(1,128)}), f32[64,1,128]{2,1,0:T(1,128)S(1)}, u32[]{:S(2)}, u32[]{:S(2)}) %all-to-all-start.1) | async-done | bytes 32800 | tf_op jit(solution)/shard_map/all_to_all | solution.py:386
  56.5 0.0 copy-done.1
  56.5 0.0 copy-done.4
  56.5 3.0 %source_right.1.after_ref.own_ref = f32[80,256]{1,0:T(8,128)S(1)} custom-call(f32[64,128]{1,0:T(8,128)S(1)} %bitcast.14, f32[8,128]{1,0:T(8,128)S(1)} %copy-done.4, f32[768,128]{1,0:T(8,128)S(1)} %copy-done.1, s32[128,128]{1,0:T(8,128)S(1)} %copy-done.3, f32[640,128]{1,0:T(8,128)S(1)} %bitcast.16), custom_call_target="tpu_custom_call" | custom-call | flops 1342177280 | bytes 823296 | tf_op jit(solution)/shard_map/source_right/pallas_call | solution.py:353
  59.5 0.1 collective-permute-start.5
  59.6 1.3 %collective-permute-start.6 = (f32[80,256]{1,0:T(8,128)S(1)}, f32[80,256]{1,0:T(8,128)S(1)}, u32[]{:S(2)}, u32[]{:S(2)}) collective-permute-start(f32[80,256]{1,0:T(8,128)S(1)} %source_right.1.after_ref.own_ref), channel_id=1, source_target_pairs={{0,2},{1,3},{2,0},{3,1},{4,6},{5,7},{6,4},{7,5},{8,10},{9,11},{10,... | collective-permute-start | bytes 245768 | tf_op jit(solution)/shard_map/ppermute | solution.py:381
  60.9 1.3 %collective-permute-start.7 = (f32[80,256]{1,0:T(8,128)S(1)}, f32[80,256]{1,0:T(8,128)S(1)}, u32[]{:S(2)}, u32[]{:S(2)}) collective-permute-start(f32[80,256]{1,0:T(8,128)S(1)} %source_right.1.after_ref.own_ref), channel_id=1, source_target_pairs={{0,3},{1,0},{2,1},{3,2},{4,7},{5,4},{6,5},{7,6},{8,11},{9,8},{10,9... | collective-permute-start | bytes 245768 | tf_op jit(solution)/shard_map/ppermute | solution.py:381
  62.3 0.0 collective-permute-done.4.other_ref
  62.3 0.1 factors.1.factor_ref
  62.4 2.2 %collective-permute-done.5.one_ref = f32[80,256]{1,0:T(8,128)S(1)} collective-permute-done((f32[80,256]{1,0:T(8,128)S(1)}, f32[80,256]{1,0:T(8,128)S(1)}, u32[]{:S(2)}, u32[]{:S(2)}) %collective-permute-start.5) | collective-permute-done | bytes 81952 | tf_op jit(solution)/shard_map/ppermute | solution.py:381
  64.6 0.6 collective-permute-done.6.two_ref
  65.1 0.7 %collective-permute-done.7.three_ref = f32[80,256]{1,0:T(8,128)S(1)} collective-permute-done((f32[80,256]{1,0:T(8,128)S(1)}, f32[80,256]{1,0:T(8,128)S(1)}, u32[]{:S(2)}, u32[]{:S(2)}) %collective-permute-start.7) | collective-permute-done | bytes 81952 | tf_op jit(solution)/shard_map/ppermute | solution.py:381
  65.8 0.7 %solve.1 = f32[5,4096]{1,0:T(8,128)} custom-call(f32[240,256]{1,0:T(8,128)S(1)} %factors.1.factor_ref, f32[80,256]{1,0:T(8,128)S(1)} %source_right.1.after_ref.own_ref, f32[80,256]{1,0:T(8,128)S(1)} %collective-permute-done.5.one_ref, f32[80,256]{1,0:T(8,128)S(1)} %collective-permute-done.6.two_ref, f32[80,256]{1,0:T(8,128)S(1)} %collective-permute-done.7.three_ref), custom_call_target="tpu_custom_call" | custom-call | flops 1000000 | bytes 573440 | tf_op jit(solution)/shard_map/solve/pallas_call | solution.py:353
  (1 shorter events, 0.0 us)
Async XLA Ops:
  0.6 15.9 %copy-start.2 = (f32[128,5,128]{2,0,1:T(8,128)S(1)}, f32[128,5,128]{2,0,1:T(8,128)}, u32[]{:S(2)}) copy-start(f32[128,5,128]{2,0,1:T(8,128)} %param.14) | copy-start | bytes 983044
  3.3 13.3 %copy-start.3 = (s32[128,128]{1,0:T(8,128)S(1)}, s32[128,128]{1,0:T(8,128)}, u32[]{:S(2)}) copy-start(s32[128,128]{1,0:T(8,128)} %get-tuple-element.9.marked_ref) | copy-start | bytes 196612
  3.3 23.2 %all-to-all-start = ((f32[64,4,128]{2,1,0:T(4,128)}), f32[64,4,128]{2,1,0:T(4,128)S(1)}, u32[]{:S(2)}, u32[]{:S(2)}) async-start(f32[64,4,128]{2,1,0:T(4,128)} %bitcast.18), calls=%async_computation | async-start | bytes 262144 | tf_op jit(solution)/shard_map/all_to_all | solution.py:386
  22.1 9.6 %collective-permute-start.3 = (f32[240,256]{1,0:T(8,128)S(1)}, f32[240,256]{1,0:T(8,128)S(1)}, u32[]{:S(2)}, u32[]{:S(2)}) collective-permute-start(f32[240,256]{1,0:T(8,128)S(1)} %source_normals.1.after_ref.own_ref), channel_id=1, source_target_pairs={{0,1},{1,0},{2,3},{3,2},{4,5},{5,4},{6,7},{7,6},{8,9},{9,8},{10,11... | collective-permute-start | bytes 737288 | tf_op jit(solution)/shard_map/ppermute | solution.py:376
  26.8 6.9 %copy-start = (bf16[120,352]{1,0:T(8,128)(2,1)S(1)}, bf16[120,352]{1,0:T(8,128)(2,1)}, u32[]{:S(2)}) copy-start(bf16[120,352]{1,0:T(8,128)(2,1)} %constant.2.clone.table_ref) | copy-start | bytes 253444
  26.8 4.9 %collective-permute-start = (f32[88,128]{1,0:T(8,128)S(1)}, f32[88,128]{1,0:T(8,128)S(1)}, u32[]{:S(2)}, u32[]{:S(2)}) collective-permute-start(f32[88,128]{1,0:T(8,128)S(1)} %bins.1.own_ref), channel_id=1, source_target_pairs={{0,1},{1,2},{2,3},{3,0},{4,5},{5,6},{6,7},{7,4},{8,9},{9,10},{10,1... | collective-permute-start | bytes 135176 | tf_op jit(solution)/shard_map/ppermute | solution.py:381
  28.1 5.0 %collective-permute-start.1 = (f32[88,128]{1,0:T(8,128)S(1)}, f32[88,128]{1,0:T(8,128)S(1)}, u32[]{:S(2)}, u32[]{:S(2)}) collective-permute-start(f32[88,128]{1,0:T(8,128)S(1)} %bins.1.own_ref), channel_id=1, source_target_pairs={{0,2},{1,3},{2,0},{3,1},{4,6},{5,7},{6,4},{7,5},{8,10},{9,11},{10,... | collective-permute-start | bytes 135176 | tf_op jit(solution)/shard_map/ppermute | solution.py:381
  30.5 3.2 %collective-permute-start.2 = (f32[88,128]{1,0:T(8,128)S(1)}, f32[88,128]{1,0:T(8,128)S(1)}, u32[]{:S(2)}, u32[]{:S(2)}) collective-permute-start(f32[88,128]{1,0:T(8,128)S(1)} %bins.1.own_ref), channel_id=1, source_target_pairs={{0,3},{1,0},{2,1},{3,2},{4,7},{5,4},{6,5},{7,6},{8,11},{9,8},{10,9... | collective-permute-start | bytes 135176 | tf_op jit(solution)/shard_map/ppermute | solution.py:381
  31.7 24.7 %copy-start.1 = (f32[768,128]{1,0:T(8,128)S(1)}, f32[768,128]{1,0:T(8,128)}, u32[]{:S(2)}) copy-start(f32[768,128]{1,0:T(8,128)} %get-tuple-element.13.obs_ref) | copy-start | bytes 1179652
  36.5 20.0 %all-to-all-start.1 = ((f32[64,1,128]{2,1,0:T(1,128)}), f32[64,1,128]{2,1,0:T(1,128)S(1)}, u32[]{:S(2)}, u32[]{:S(2)}) async-start(f32[64,1,128]{2,1,0:T(1,128)} %bitcast.8), calls=%async_computation.1 | async-start | bytes 65536 | tf_op jit(solution)/shard_map/all_to_all | solution.py:386
  47.4 9.1 %copy-start.4 = (f32[8,128]{1,0:T(8,128)S(1)}, f32[8,128]{1,0:T(8,128)}, u32[]{:S(2)}) copy-start(f32[8,128]{1,0:T(8,128)} %get-tuple-element.12.slot_ref) | copy-start | bytes 12292
  47.4 14.9 %collective-permute-start.4 = (f32[240,256]{1,0:T(8,128)S(1)}, f32[240,256]{1,0:T(8,128)S(1)}, u32[]{:S(2)}, u32[]{:S(2)}) collective-permute-start(f32[240,256]{1,0:T(8,128)S(1)} %pairs.1.after_ref.own_ref), channel_id=1, source_target_pairs={{0,3},{1,2},{2,1},{3,0},{4,7},{5,6},{6,5},{7,4},{8,11},{9,10},{10,... | collective-permute-start | bytes 737288 | tf_op jit(solution)/shard_map/ppermute | solution.py:376
  59.5 5.1 %collective-permute-start.5 = (f32[80,256]{1,0:T(8,128)S(1)}, f32[80,256]{1,0:T(8,128)S(1)}, u32[]{:S(2)}, u32[]{:S(2)}) collective-permute-start(f32[80,256]{1,0:T(8,128)S(1)} %source_right.1.after_ref.own_ref), channel_id=1, source_target_pairs={{0,1},{1,2},{2,3},{3,0},{4,5},{5,6},{6,7},{7,4},{8,9},{9,10},{10,1... | collective-permute-start | bytes 245768 | tf_op jit(solution)/shard_map/ppermute | solution.py:381
  59.6 5.6 %collective-permute-start.6 = (f32[80,256]{1,0:T(8,128)S(1)}, f32[80,256]{1,0:T(8,128)S(1)}, u32[]{:S(2)}, u32[]{:S(2)}) collective-permute-start(f32[80,256]{1,0:T(8,128)S(1)} %source_right.1.after_ref.own_ref), channel_id=1, source_target_pairs={{0,2},{1,3},{2,0},{3,1},{4,6},{5,7},{6,4},{7,5},{8,10},{9,11},{10,... | collective-permute-start | bytes 245768 | tf_op jit(solution)/shard_map/ppermute | solution.py:381
  60.9 4.9 %collective-permute-start.7 = (f32[80,256]{1,0:T(8,128)S(1)}, f32[80,256]{1,0:T(8,128)S(1)}, u32[]{:S(2)}, u32[]{:S(2)}) collective-permute-start(f32[80,256]{1,0:T(8,128)S(1)} %source_right.1.after_ref.own_ref), channel_id=1, source_target_pairs={{0,3},{1,0},{2,1},{3,2},{4,7},{5,4},{6,5},{7,6},{8,11},{9,8},{10,9... | collective-permute-start | bytes 245768 | tf_op jit(solution)/shard_map/ppermute | solution.py:381

commit v10 on v9

--- a/solution.py
+++ b/solution.py
@@ -155,8 +155,10 @@
     out_ref[...] = exact_dot(got[:FEATS], place, NT)
 
 
-def attitude_kernel(own_ref, one_ref, two_ref, three_ref, got_ref, table_ref, after_ref, att_ref, reply_ref):
-    del after_ref
+def attitude_kernel(
+    own_ref, one_ref, two_ref, three_ref, got_ref, table_ref, normal_ref, other_ref, att_ref, reply_ref, pair_ref
+):
+    pair_ref[...] = normal_ref[...] + other_ref[...]
     total = ((own_ref[...] + two_ref[...]) + (one_ref[...] + three_ref[...])) * (1.0 / 36.0)
     moved = jnp.concatenate([total] + [pltpu.roll(total, l, 1) for l in range(1, 4)], axis=0)
     band = exact_dot(moved, table_ref[...], NN, swap=True)
@@ -255,11 +257,11 @@
     gains = [gain_ref[NBLK * p : NBLK * p + NBLK, :] for p in range(5)]
     for at, (first, second) in enumerate(PAIR_LIST):
         put_terms(terms_ref, at, gains[first] * gains[second])
-    source_sums(15, 32, terms_ref, high_ref, low_ref, out_ref, *work)
+    source_sums(15, 64, terms_ref, high_ref, low_ref, out_ref, *work)
 
 
 def source_right_kernel(
-    reply_ref, slot_ref, obs_ref, marked_ref, gain_ref, out_ref, terms_ref, high_ref, low_ref, *work
+    reply_ref, slot_ref, obs_ref, marked_ref, gain_ref, after_ref, out_ref, terms_ref, high_ref, low_ref, *work
 ):
     put_sources(marked_ref, high_ref, low_ref)
     place = indicator(iota_f((WINDOWS, NBLK), 0) == slot_ref[0:1, :])
@@ -292,10 +294,6 @@
     source_sums(5, NBLK, terms_ref, high_ref, low_ref, out_ref, *work)
 
 
-def pair_kernel(own_ref, other_ref, out_ref):
-    out_ref[...] = own_ref[...] + other_ref[...]
-
-
 def factor_kernel(own_ref, other_ref, after_ref, out_ref):
     del after_ref
     entries = {}
@@ -424,19 +422,18 @@
         flops=2 * 480 * 256 * 16384,
     )
     moments = kernel_call(bins_kernel, "bins", f32(FEATS, KNOTS_W), got, normal, far=(1,))
-    normal = kernel_call(pair_kernel, "pairs", f32(15 * HIGH, LOW), normal, swapped(normal, (1, 0, 3, 2)))
-    other = swapped(normal, (3, 2, 1, 0))
-    attitude, reply = kernel_call(
+    attitude, reply, normal = kernel_call(
         attitude_kernel,
         "attitude",
-        (f32(1, 4, KNOTS_W), f32(WINDOWS, 128)),
+        (f32(1, 4, KNOTS_W), f32(WINDOWS, 128), f32(15 * HIGH, LOW)),
         moments,
         *from_others(moments),
         got,
         jnp.asarray(knot_matrix()),
         normal,
-        far=(6,),
-    )
+        swapped(normal, (1, 0, 3, 2)),
+    )
+    other = swapped(normal, (3, 2, 1, 0))
     knots = to_windows(reply)
     right = kernel_call(
         source_right_kernel,
@@ -447,6 +444,8 @@
         obs,
         marked,
         gains,
+        other,
+        far=(5,),
         scratch=segment_scratch(5),
         flops=2 * 160 * 256 * 16384,
     )

time: 67.2 us -> 68.5 us (1.019)
  blocking collectives: 0 us -> 19.2 us
  starting transfers between devices: 33.4 us -> 21.3 us
  waiting for transfers between devices: 17.4 us -> 12.1 us
  Pallas kernels: 15 us -> 14.2 us
    all_to_all x0 -> x1, blocking collectives: none -> 19.2 us  [to_windows(): lax.all_to_all(values, ('src', 'win'), split_axis=0, concat_axis=0, tiled...]
    all_to_all x2 -> x1, starting transfers between devices: 24.2 us -> 13.3 us  [to_windows(): lax.all_to_all(values, ('src', 'win'), split_axis=0, concat_axis=0, tiled...]
    all_to_all x2 -> x1, waiting for transfers between devices: 11.9 us -> 3.47 us  [to_windows(): lax.all_to_all(values, ('src', 'win'), split_axis=0, concat_axis=0, tiled...]
    ppermute x6, waiting for transfers between devices: 5.47 us -> 8.66 us  [from_others(): lax.ppermute(values, 'ccd', [(at, (at + shift) % N_CCD) for at in range(N...]
    ppermute x6, starting transfers between devices: 7.64 us -> 6.35 us  [from_others(): lax.ppermute(values, 'ccd', [(at, (at + shift) % N_CCD) for at in range(N...]
    pallas_call x8 -> x7, Pallas kernels: 15 us -> 14.2 us  [kernel_call(): pl.pallas_call(body, out_shape=outs, in_specs=[pl.BlockSpec(memory_space=...]
  transfers between devices with their start and end apart: 10 -> 9, of which waited for: 7 -> 6; matrix products, arithmetic and copies ran while one was open for 0% -> 0% of each run, Pallas kernels for 13% -> 8%
where the time goes in v10:
time: 68.5 us; the launch traced here: 68.2 us
  starting transfers between devices  21.3 us (31%)
  blocking collectives  19.2 us (28%)
  Pallas kernels  14.2 us (21%)
  waiting for transfers between devices  12.1 us (18%)
  between operations  0.73 us (1%)
  local copies, waits for them, and re-layouts  0.7 us (1%)
    all_to_all x1, blocking collectives, to_windows(): lax.all_to_all(values, ('src', 'win'), split_axis=0, concat_axis=0, tiled...  19.2 us
    pallas_call x7, Pallas kernels, kernel_call(): pl.pallas_call(body, out_shape=outs, in_specs=[pl.BlockSpec(memory_space=...  14.2 us
    all_to_all x1, starting transfers between devices, to_windows(): lax.all_to_all(values, ('src', 'win'), split_axis=0, concat_axis=0, tiled...  13.3 us
    ppermute x6, waiting for transfers between devices, from_others(): lax.ppermute(values, 'ccd', [(at, (at + shift) % N_CCD) for at in range(N...  8.66 us
    ppermute x6, starting transfers between devices, from_others(): lax.ppermute(values, 'ccd', [(at, (at + shift) % N_CCD) for at in range(N...  6.35 us
    all_to_all x1, waiting for transfers between devices, to_windows(): lax.all_to_all(values, ('src', 'win'), split_axis=0, concat_axis=0, tiled...  3.47 us
    ppermute x2, starting transfers between devices, swapped(): return lax.ppermute(values, 'ccd', list(enumerate(partner)))  1.64 us
  transfers between devices with their start and end apart: 9, of which 6 were waited for; matrix products, arithmetic and copies ran while one was open for 0% of the time, Pallas kernels for 8%

profile of v10, /device:TPU:1, one launch (start us, length us, event | category | flops | bytes accessed | tf_op | source)
XLA Modules:
  0.0 68.2 jit_solution(9279408102100582864)
XLA Ops:
  0.6 0.0 copy-start.2
  0.6 2.6 %normals.1 = (f32[256,128]{1,0:T(8,128)}, f32[768,128]{1,0:T(8,128)}, f32[8,128]{1,0:T(8,128)}, s32[128,128]{1,0:T(8,128)}) custom-call(s32[1,128]{1,0:T(1,128)} %bitcast.20, s32[1,128]{1,0:T(1,128)} %bitcast.21, f32[128,128]{1,0:T(8,128)} %refs_2_.1, f32[512,128]{1,0:T(8,128)} %bitcast.18, f32[128,128]{1,0:T(8,128)} %refs_4_.1, s32[128,128]{1,0:T(8,128)} %refs_5_.1), custom_call_target="tpu_custom_call" | custom-call | flops 1000000 | bytes 459776 | tf_op jit(solution)/shard_map/normals/pallas_call | solution.py:351
  3.3 0.0 copy-start.3
  3.3 13.3 %all-to-all-start = ((f32[64,4,128]{2,1,0:T(4,128)}), f32[64,4,128]{2,1,0:T(4,128)S(1)}, u32[]{:S(2)}, u32[]{:S(2)}) async-start(f32[64,4,128]{2,1,0:T(4,128)} %bitcast.19), calls=%async_computation | async-start | bytes 262144 | tf_op jit(solution)/shard_map/all_to_all | solution.py:384
  16.6 0.0 copy-done.2
  16.6 0.0 copy-done.3
  16.6 5.1 %source_normals.1.after_ref.normal_ref = f32[240,256]{1,0:T(8,128)S(1)} custom-call(s32[128,128]{1,0:T(8,128)S(1)} %copy-done.3, f32[640,128]{1,0:T(8,128)S(1)} %bitcast.16), custom_call_target="tpu_custom_call" | custom-call | flops 4026531840 | bytes 393216 | tf_op jit(solution)/shard_map/source_normals/pallas_call | solution.py:351
  21.7 1.3 %collective-permute-start.3 = (f32[240,256]{1,0:T(8,128)S(1)}, f32[240,256]{1,0:T(8,128)S(1)}, u32[]{:S(2)}, u32[]{:S(2)}) collective-permute-start(f32[240,256]{1,0:T(8,128)S(1)} %source_normals.1.after_ref.normal_ref), channel_id=1, source_target_pairs={{0,1},{1,0},{2,3},{3,2},{4,5},{5,4},{6,7},{7,6},{8,9},{9,8},{10,11... | collective-permute-start | bytes 737288 | tf_op jit(solution)/shard_map/ppermute | solution.py:374
  23.0 3.5 %all-to-all-done = f32[64,4,128]{2,1,0:T(4,128)S(1)} async-done(((f32[64,4,128]{2,1,0:T(4,128)}), f32[64,4,128]{2,1,0:T(4,128)S(1)}, u32[]{:S(2)}, u32[]{:S(2)}) %all-to-all-start) | async-done | bytes 131104 | tf_op jit(solution)/shard_map/all_to_all | solution.py:384
  26.5 0.0 copy-start
  26.5 0.3 bins.1.own_ref
  26.8 0.0 copy-start.1
  26.8 2.6 %collective-permute-start.2 = (f32[88,128]{1,0:T(8,128)S(1)}, f32[88,128]{1,0:T(8,128)S(1)}, u32[]{:S(2)}, u32[]{:S(2)}) collective-permute-start(f32[88,128]{1,0:T(8,128)S(1)} %bins.1.own_ref), channel_id=1, source_target_pairs={{0,3},{1,0},{2,1},{3,2},{4,7},{5,4},{6,5},{7,6},{8,11},{9,8},{10,9... | collective-permute-start | bytes 135176 | tf_op jit(solution)/shard_map/ppermute | solution.py:379
  29.4 0.5 collective-permute-start.1
  29.9 0.6 collective-permute-start
  30.5 0.0 collective-permute-done.3.other_ref
  30.5 0.0 collective-permute-done.2.three_ref
  30.5 3.3 %collective-permute-done.1.two_ref = f32[88,128]{1,0:T(8,128)S(1)} collective-permute-done((f32[88,128]{1,0:T(8,128)S(1)}, f32[88,128]{1,0:T(8,128)S(1)}, u32[]{:S(2)}, u32[]{:S(2)}) %collective-permute-start.1) | collective-permute-done | bytes 45088 | tf_op jit(solution)/shard_map/ppermute | solution.py:379
  33.8 0.5 collective-permute-done.one_ref
  34.2 0.0 copy-done
  34.2 2.4 %attitude.1 = (f32[1,4,128]{2,1,0:T(4,128)}, f32[64,128]{1,0:T(8,128)S(1)}, f32[240,256]{1,0:T(8,128)S(1)}) custom-call(f32[88,128]{1,0:T(8,128)S(1)} %bins.1.own_ref, f32[88,128]{1,0:T(8,128)S(1)} %collective-permute-done.one_ref, f32[88,128]{1,0:T(8,128)S(1)} %collective-permute-done.1.two_ref, f32[88,128]{1,0:T(8,128)S(1)} %collective-permute-done.2.three_ref, ...), custom_call_target="tpu_custom_call" | custom-call | flops 1000000 | bytes 971776 | tf_op jit(solution)/shard_map/attitude/pallas_call | solution.py:351
  36.6 0.3 collective-permute-start.4
  36.9 19.2 %all_to_all.16 = f32[64,1,128]{2,1,0:T(1,128)S(1)} all-to-all(f32[64,1,128]{2,1,0:T(1,128)S(1)} %bitcast.14), channel_id=1, replica_groups=mesh['src'=16,'win'=4,'ccd'=4] {'src','win'}, dimensions={0} | all-to-all | bytes 65536 | tf_op jit(solution)/shard_map/all_to_all | solution.py:384
  56.1 0.0 copy-start.4
  56.1 0.0 collective-permute-done.4.after_ref.other_ref
  56.1 0.0 copy-done.1
  56.1 0.7 copy-done.4
  56.8 3.0 %source_right.1.after_ref.own_ref = f32[80,256]{1,0:T(8,128)S(1)} custom-call(f32[64,128]{1,0:T(8,128)S(1)} %bitcast.15, f32[8,128]{1,0:T(8,128)S(1)} %copy-done.4, f32[768,128]{1,0:T(8,128)S(1)} %copy-done.1, s32[128,128]{1,0:T(8,128)S(1)} %copy-done.3, f32[640,128]{1,0:T(8,128)S(1)} %bitcast.17, f32[240,256]{1,0:T(8,128)S(1)} %collective-permute-done.4.after_ref.other_ref), custom_call_target="tpu_custom_call" | custom-call | flops 1342177280 | bytes 1069056 | tf_op jit(solution)/shard_map/source_right/pallas_call | solution.py:351
  59.8 2.0 %collective-permute-start.7 = (f32[80,256]{1,0:T(8,128)S(1)}, f32[80,256]{1,0:T(8,128)S(1)}, u32[]{:S(2)}, u32[]{:S(2)}) collective-permute-start(f32[80,256]{1,0:T(8,128)S(1)} %source_right.1.after_ref.own_ref), channel_id=1, source_target_pairs={{0,3},{1,0},{2,1},{3,2},{4,7},{5,4},{6,5},{7,6},{8,11},{9,8},{10,9... | collective-permute-start | bytes 245768 | tf_op jit(solution)/shard_map/ppermute | solution.py:379
  61.8 0.0 collective-permute-start.6
  61.8 0.7 collective-permute-start.5
  62.5 0.1 factors.1.factor_ref
  62.6 1.2 %collective-permute-done.7.three_ref = f32[80,256]{1,0:T(8,128)S(1)} collective-permute-done((f32[80,256]{1,0:T(8,128)S(1)}, f32[80,256]{1,0:T(8,128)S(1)}, u32[]{:S(2)}, u32[]{:S(2)}) %collective-permute-start.7) | collective-permute-done | bytes 81952 | tf_op jit(solution)/shard_map/ppermute | solution.py:379
  63.8 2.9 %collective-permute-done.6.two_ref = f32[80,256]{1,0:T(8,128)S(1)} collective-permute-done((f32[80,256]{1,0:T(8,128)S(1)}, f32[80,256]{1,0:T(8,128)S(1)}, u32[]{:S(2)}, u32[]{:S(2)}) %collective-permute-start.6) | collective-permute-done | bytes 81952 | tf_op jit(solution)/shard_map/ppermute | solution.py:379
  66.7 0.8 %collective-permute-done.5.one_ref = f32[80,256]{1,0:T(8,128)S(1)} collective-permute-done((f32[80,256]{1,0:T(8,128)S(1)}, f32[80,256]{1,0:T(8,128)S(1)}, u32[]{:S(2)}, u32[]{:S(2)}) %collective-permute-start.5) | collective-permute-done | bytes 81952 | tf_op jit(solution)/shard_map/ppermute | solution.py:379
  67.5 0.7 %solve.1 = f32[5,4096]{1,0:T(8,128)} custom-call(f32[240,256]{1,0:T(8,128)S(1)} %factors.1.factor_ref, f32[80,256]{1,0:T(8,128)S(1)} %source_right.1.after_ref.own_ref, f32[80,256]{1,0:T(8,128)S(1)} %collective-permute-done.5.one_ref, f32[80,256]{1,0:T(8,128)S(1)} %collective-permute-done.6.two_ref, f32[80,256]{1,0:T(8,128)S(1)} %collective-permute-done.7.three_ref), custom_call_target="tpu_custom_call" | custom-call | flops 1000000 | bytes 573440 | tf_op jit(solution)/shard_map/solve/pallas_call | solution.py:351
Async XLA Ops:
  0.6 15.9 %copy-start.2 = (f32[128,5,128]{2,0,1:T(8,128)S(1)}, f32[128,5,128]{2,0,1:T(8,128)}, u32[]{:S(2)}) copy-start(f32[128,5,128]{2,0,1:T(8,128)} %param.14) | copy-start | bytes 983044
  3.3 13.3 %copy-start.3 = (s32[128,128]{1,0:T(8,128)S(1)}, s32[128,128]{1,0:T(8,128)}, u32[]{:S(2)}) copy-start(s32[128,128]{1,0:T(8,128)} %get-tuple-element.10.marked_ref) | copy-start | bytes 196612
  3.3 23.2 %all-to-all-start = ((f32[64,4,128]{2,1,0:T(4,128)}), f32[64,4,128]{2,1,0:T(4,128)S(1)}, u32[]{:S(2)}, u32[]{:S(2)}) async-start(f32[64,4,128]{2,1,0:T(4,128)} %bitcast.19), calls=%async_computation | async-start | bytes 262144 | tf_op jit(solution)/shard_map/all_to_all | solution.py:384
  21.7 8.8 %collective-permute-start.3 = (f32[240,256]{1,0:T(8,128)S(1)}, f32[240,256]{1,0:T(8,128)S(1)}, u32[]{:S(2)}, u32[]{:S(2)}) collective-permute-start(f32[240,256]{1,0:T(8,128)S(1)} %source_normals.1.after_ref.normal_ref), channel_id=1, source_target_pairs={{0,1},{1,0},{2,3},{3,2},{4,5},{5,4},{6,7},{7,6},{8,9},{9,8},{10,11... | collective-permute-start | bytes 737288 | tf_op jit(solution)/shard_map/ppermute | solution.py:374
  26.5 7.7 %copy-start = (bf16[120,352]{1,0:T(8,128)(2,1)S(1)}, bf16[120,352]{1,0:T(8,128)(2,1)}, u32[]{:S(2)}) copy-start(bf16[120,352]{1,0:T(8,128)(2,1)} %constant.2.clone.table_ref) | copy-start | bytes 253444
  26.8 29.3 %copy-start.1 = (f32[768,128]{1,0:T(8,128)S(1)}, f32[768,128]{1,0:T(8,128)}, u32[]{:S(2)}) copy-start(f32[768,128]{1,0:T(8,128)} %get-tuple-element.15.obs_ref) | copy-start | bytes 1179652
  26.8 3.7 %collective-permute-start.2 = (f32[88,128]{1,0:T(8,128)S(1)}, f32[88,128]{1,0:T(8,128)S(1)}, u32[]{:S(2)}, u32[]{:S(2)}) collective-permute-start(f32[88,128]{1,0:T(8,128)S(1)} %bins.1.own_ref), channel_id=1, source_target_pairs={{0,3},{1,0},{2,1},{3,2},{4,7},{5,4},{6,5},{7,6},{8,11},{9,8},{10,9... | collective-permute-start | bytes 135176 | tf_op jit(solution)/shard_map/ppermute | solution.py:379
  29.4 4.4 %collective-permute-start.1 = (f32[88,128]{1,0:T(8,128)S(1)}, f32[88,128]{1,0:T(8,128)S(1)}, u32[]{:S(2)}, u32[]{:S(2)}) collective-permute-start(f32[88,128]{1,0:T(8,128)S(1)} %bins.1.own_ref), channel_id=1, source_target_pairs={{0,2},{1,3},{2,0},{3,1},{4,6},{5,7},{6,4},{7,5},{8,10},{9,11},{10,... | collective-permute-start | bytes 135176 | tf_op jit(solution)/shard_map/ppermute | solution.py:379
  29.9 4.4 %collective-permute-start = (f32[88,128]{1,0:T(8,128)S(1)}, f32[88,128]{1,0:T(8,128)S(1)}, u32[]{:S(2)}, u32[]{:S(2)}) collective-permute-start(f32[88,128]{1,0:T(8,128)S(1)} %bins.1.own_ref), channel_id=1, source_target_pairs={{0,1},{1,2},{2,3},{3,0},{4,5},{5,6},{6,7},{7,4},{8,9},{9,10},{10,1... | collective-permute-start | bytes 135176 | tf_op jit(solution)/shard_map/ppermute | solution.py:379
  36.6 19.5 %collective-permute-start.4 = (f32[240,256]{1,0:T(8,128)S(1)}, f32[240,256]{1,0:T(8,128)S(1)}, u32[]{:S(2)}, u32[]{:S(2)}) collective-permute-start(f32[240,256]{1,0:T(8,128)S(1)} %get-tuple-element.12.own_ref), channel_id=1, source_target_pairs={{0,3},{1,2},{2,1},{3,0},{4,7},{5,6},{6,5},{7,4},{8,11},{9,10},{10,... | collective-permute-start | bytes 737288 | tf_op jit(solution)/shard_map/ppermute | solution.py:374
  56.1 0.7 %copy-start.4 = (f32[8,128]{1,0:T(8,128)S(1)}, f32[8,128]{1,0:T(8,128)}, u32[]{:S(2)}) copy-start(f32[8,128]{1,0:T(8,128)} %get-tuple-element.14.slot_ref) | copy-start | bytes 12292
  59.8 4.0 %collective-permute-start.7 = (f32[80,256]{1,0:T(8,128)S(1)}, f32[80,256]{1,0:T(8,128)S(1)}, u32[]{:S(2)}, u32[]{:S(2)}) collective-permute-start(f32[80,256]{1,0:T(8,128)S(1)} %source_right.1.after_ref.own_ref), channel_id=1, source_target_pairs={{0,3},{1,0},{2,1},{3,2},{4,7},{5,4},{6,5},{7,6},{8,11},{9,8},{10,9... | collective-permute-start | bytes 245768 | tf_op jit(solution)/shard_map/ppermute | solution.py:379
  61.8 4.9 %collective-permute-start.6 = (f32[80,256]{1,0:T(8,128)S(1)}, f32[80,256]{1,0:T(8,128)S(1)}, u32[]{:S(2)}, u32[]{:S(2)}) collective-permute-start(f32[80,256]{1,0:T(8,128)S(1)} %source_right.1.after_ref.own_ref), channel_id=1, source_target_pairs={{0,2},{1,3},{2,0},{3,1},{4,6},{5,7},{6,4},{7,5},{8,10},{9,11},{10,... | collective-permute-start | bytes 245768 | tf_op jit(solution)/shard_map/ppermute | solution.py:379
  61.8 5.7 %collective-permute-start.5 = (f32[80,256]{1,0:T(8,128)S(1)}, f32[80,256]{1,0:T(8,128)S(1)}, u32[]{:S(2)}, u32[]{:S(2)}) collective-permute-start(f32[80,256]{1,0:T(8,128)S(1)} %source_right.1.after_ref.own_ref), channel_id=1, source_target_pairs={{0,1},{1,2},{2,3},{3,0},{4,5},{5,6},{6,7},{7,4},{8,9},{9,10},{10,1... | collective-permute-start | bytes 245768 | tf_op jit(solution)/shard_map/ppermute | solution.py:379

commit v11 on v10

--- a/solution.py
+++ b/solution.py
@@ -261,7 +261,7 @@
 
 
 def source_right_kernel(
-    reply_ref, slot_ref, obs_ref, marked_ref, gain_ref, after_ref, out_ref, terms_ref, high_ref, low_ref, *work
+    reply_ref, slot_ref, obs_ref, marked_ref, gain_ref, out_ref, terms_ref, high_ref, low_ref, *work
 ):
     put_sources(marked_ref, high_ref, low_ref)
     place = indicator(iota_f((WINDOWS, NBLK), 0) == slot_ref[0:1, :])
@@ -444,8 +444,6 @@
         obs,
         marked,
         gains,
-        other,
-        far=(5,),
         scratch=segment_scratch(5),
         flops=2 * 160 * 256 * 16384,
     )

time: 68.5 us -> 67.1 us (0.980)
  blocking collectives: 19.2 us -> 0 us
  starting transfers between devices: 21.3 us -> 30.9 us
  waiting for transfers between devices: 12.1 us -> 20.6 us
    all_to_all x1 -> x0, blocking collectives: 19.2 us -> none  [to_windows(): lax.all_to_all(values, ('src', 'win'), split_axis=0, concat_axis=0, tiled...]
    all_to_all x1 -> x2, starting transfers between devices: 13.3 us -> 22.8 us  [to_windows(): lax.all_to_all(values, ('src', 'win'), split_axis=0, concat_axis=0, tiled...]
    all_to_all x1 -> x2, waiting for transfers between devices: 3.47 us -> 11.7 us  [to_windows(): lax.all_to_all(values, ('src', 'win'), split_axis=0, concat_axis=0, tiled...]
  transfers between devices with their start and end apart: 9 -> 10, of which waited for: 6 -> 7; matrix products, arithmetic and copies ran while one was open for 0% -> 0% of each run, Pallas kernels for 8% -> 13%
where the time goes in v11:
time: 67.1 us; the launch traced here: 66.9 us
  starting transfers between devices  30.9 us (46%)
  waiting for transfers between devices  20.6 us (31%)
  Pallas kernels  14.6 us (22%)
  between operations  0.74 us (1%)
    all_to_all x2, starting transfers between devices, to_windows(): lax.all_to_all(values, ('src', 'win'), split_axis=0, concat_axis=0, tiled...  22.8 us
    pallas_call x7, Pallas kernels, kernel_call(): pl.pallas_call(body, out_shape=outs, in_specs=[pl.BlockSpec(memory_space=...  14.6 us
    all_to_all x2, waiting for transfers between devices, to_windows(): lax.all_to_all(values, ('src', 'win'), split_axis=0, concat_axis=0, tiled...  11.7 us
    ppermute x6, waiting for transfers between devices, from_others(): lax.ppermute(values, 'ccd', [(at, (at + shift) % N_CCD) for at in range(N...  8.89 us
    ppermute x6, starting transfers between devices, from_others(): lax.ppermute(values, 'ccd', [(at, (at + shift) % N_CCD) for at in range(N...  5.98 us
    ppermute x2, starting transfers between devices, swapped(): return lax.ppermute(values, 'ccd', list(enumerate(partner)))  2.15 us
  transfers between devices with their start and end apart: 10, of which 7 were waited for; matrix products, arithmetic and copies ran while one was open for 0% of the time, Pallas kernels for 13%

profile of v11, /device:TPU:1, one launch (start us, length us, event | category | flops | bytes accessed | tf_op | source)
XLA Modules:
  0.0 66.9 jit_solution(8348662084300455528)
XLA Ops:
  0.6 0.0 copy-start.2
  0.6 2.6 %normals.1 = (f32[256,128]{1,0:T(8,128)}, f32[768,128]{1,0:T(8,128)}, f32[8,128]{1,0:T(8,128)}, s32[128,128]{1,0:T(8,128)}) custom-call(s32[1,128]{1,0:T(1,128)} %bitcast.19, s32[1,128]{1,0:T(1,128)} %bitcast.20, f32[128,128]{1,0:T(8,128)} %refs_2_.1, f32[512,128]{1,0:T(8,128)} %bitcast.17, f32[128,128]{1,0:T(8,128)} %refs_4_.1, s32[128,128]{1,0:T(8,128)} %refs_5_.1), custom_call_target="tpu_custom_call" | custom-call | flops 1000000 | bytes 459776 | tf_op jit(solution)/shard_map/normals/pallas_call | solution.py:351
  3.3 0.0 copy-start.3
  3.3 13.3 %all-to-all-start = ((f32[64,4,128]{2,1,0:T(4,128)}), f32[64,4,128]{2,1,0:T(4,128)S(1)}, u32[]{:S(2)}, u32[]{:S(2)}) async-start(f32[64,4,128]{2,1,0:T(4,128)} %bitcast.18), calls=%async_computation | async-start | bytes 262144 | tf_op jit(solution)/shard_map/all_to_all | solution.py:384
  16.6 0.0 copy-done.2
  16.6 0.0 copy-done.3
  16.6 5.1 %source_normals.1.after_ref.normal_ref = f32[240,256]{1,0:T(8,128)S(1)} custom-call(s32[128,128]{1,0:T(8,128)S(1)} %copy-done.3, f32[640,128]{1,0:T(8,128)S(1)} %bitcast.15), custom_call_target="tpu_custom_call" | custom-call | flops 4026531840 | bytes 393216 | tf_op jit(solution)/shard_map/source_normals/pallas_call | solution.py:351
  21.7 1.3 %collective-permute-start.3 = (f32[240,256]{1,0:T(8,128)S(1)}, f32[240,256]{1,0:T(8,128)S(1)}, u32[]{:S(2)}, u32[]{:S(2)}) collective-permute-start(f32[240,256]{1,0:T(8,128)S(1)} %source_normals.1.after_ref.normal_ref), channel_id=1, source_target_pairs={{0,1},{1,0},{2,3},{3,2},{4,5},{5,4},{6,7},{7,6},{8,9},{9,8},{10,11... | collective-permute-start | bytes 737288 | tf_op jit(solution)/shard_map/ppermute | solution.py:374
  23.0 3.5 %all-to-all-done = f32[64,4,128]{2,1,0:T(4,128)S(1)} async-done(((f32[64,4,128]{2,1,0:T(4,128)}), f32[64,4,128]{2,1,0:T(4,128)S(1)}, u32[]{:S(2)}, u32[]{:S(2)}) %all-to-all-start) | async-done | bytes 131104 | tf_op jit(solution)/shard_map/all_to_all | solution.py:384
  26.5 0.0 copy-start
  26.5 0.3 bins.1.own_ref
  26.8 0.0 copy-start.1
  26.8 2.6 %collective-permute-start.2 = (f32[88,128]{1,0:T(8,128)S(1)}, f32[88,128]{1,0:T(8,128)S(1)}, u32[]{:S(2)}, u32[]{:S(2)}) collective-permute-start(f32[88,128]{1,0:T(8,128)S(1)} %bins.1.own_ref), channel_id=1, source_target_pairs={{0,3},{1,0},{2,1},{3,2},{4,7},{5,4},{6,5},{7,6},{8,11},{9,8},{10,9... | collective-permute-start | bytes 135176 | tf_op jit(solution)/shard_map/ppermute | solution.py:379
  29.4 0.5 collective-permute-start.1
  29.9 0.6 collective-permute-start
  30.5 0.0 collective-permute-done.3.other_ref
  30.5 0.0 collective-permute-done.2.three_ref
  30.5 3.3 %collective-permute-done.1.two_ref = f32[88,128]{1,0:T(8,128)S(1)} collective-permute-done((f32[88,128]{1,0:T(8,128)S(1)}, f32[88,128]{1,0:T(8,128)S(1)}, u32[]{:S(2)}, u32[]{:S(2)}) %collective-permute-start.1) | collective-permute-done | bytes 45088 | tf_op jit(solution)/shard_map/ppermute | solution.py:379
  33.8 0.5 collective-permute-done.one_ref
  34.2 0.0 copy-done
  34.2 2.7 %attitude.1 = (f32[1,4,128]{2,1,0:T(4,128)}, f32[64,128]{1,0:T(8,128)}, f32[240,256]{1,0:T(8,128)S(1)}) custom-call(f32[88,128]{1,0:T(8,128)S(1)} %bins.1.own_ref, f32[88,128]{1,0:T(8,128)S(1)} %collective-permute-done.one_ref, f32[88,128]{1,0:T(8,128)S(1)} %collective-permute-done.1.two_ref, f32[88,128]{1,0:T(8,128)S(1)} %collective-permute-done.2.three_ref, ...), custom_call_target="tpu_custom_call" | custom-call | flops 1000000 | bytes 971776 | tf_op jit(solution)/shard_map/attitude/pallas_call | solution.py:351
  37.0 9.5 %all-to-all-start.1 = ((f32[64,1,128]{2,1,0:T(1,128)}), f32[64,1,128]{2,1,0:T(1,128)S(1)}, u32[]{:S(2)}, u32[]{:S(2)}) async-start(f32[64,1,128]{2,1,0:T(1,128)} %bitcast.8), calls=%async_computation.1 | async-start | bytes 65536 | tf_op jit(solution)/shard_map/all_to_all | solution.py:384
  46.5 0.0 copy-start.4
  46.5 0.8 %collective-permute-start.4 = (f32[240,256]{1,0:T(8,128)S(1)}, f32[240,256]{1,0:T(8,128)S(1)}, u32[]{:S(2)}, u32[]{:S(2)}) collective-permute-start(f32[240,256]{1,0:T(8,128)S(1)} %get-tuple-element.12.own_ref), channel_id=1, source_target_pairs={{0,3},{1,2},{2,1},{3,0},{4,7},{5,6},{6,5},{7,4},{8,11},{9,10},{10,... | collective-permute-start | bytes 737288 | tf_op jit(solution)/shard_map/ppermute | solution.py:374
  47.4 8.2 %all-to-all-done.1 = f32[64,1,128]{2,1,0:T(1,128)S(1)} async-done(((f32[64,1,128]{2,1,0:T(1,128)}), f32[64,1,128]{2,1,0:T(1,128)S(1)}, u32[]{:S(2)}, u32[]{:S(2)}) %all-to-all-start.1) | async-done | bytes 32800 | tf_op jit(solution)/shard_map/all_to_all | solution.py:384
  55.6 0.0 copy-done.1
  55.6 0.0 copy-done.4
  55.6 3.0 %source_right.1.after_ref.own_ref = f32[80,256]{1,0:T(8,128)S(1)} custom-call(f32[64,128]{1,0:T(8,128)S(1)} %bitcast.14, f32[8,128]{1,0:T(8,128)S(1)} %copy-done.4, f32[768,128]{1,0:T(8,128)S(1)} %copy-done.1, s32[128,128]{1,0:T(8,128)S(1)} %copy-done.3, f32[640,128]{1,0:T(8,128)S(1)} %bitcast.16), custom_call_target="tpu_custom_call" | custom-call | flops 1342177280 | bytes 823296 | tf_op jit(solution)/shard_map/source_right/pallas_call | solution.py:351
  58.6 0.8 %collective-permute-start.7 = (f32[80,256]{1,0:T(8,128)S(1)}, f32[80,256]{1,0:T(8,128)S(1)}, u32[]{:S(2)}, u32[]{:S(2)}) collective-permute-start(f32[80,256]{1,0:T(8,128)S(1)} %source_right.1.after_ref.own_ref), channel_id=1, source_target_pairs={{0,3},{1,0},{2,1},{3,2},{4,7},{5,4},{6,5},{7,6},{8,11},{9,8},{10,9... | collective-permute-start | bytes 245768 | tf_op jit(solution)/shard_map/ppermute | solution.py:379
  59.5 1.5 %collective-permute-start.6 = (f32[80,256]{1,0:T(8,128)S(1)}, f32[80,256]{1,0:T(8,128)S(1)}, u32[]{:S(2)}, u32[]{:S(2)}) collective-permute-start(f32[80,256]{1,0:T(8,128)S(1)} %source_right.1.after_ref.own_ref), channel_id=1, source_target_pairs={{0,2},{1,3},{2,0},{3,1},{4,6},{5,7},{6,4},{7,5},{8,10},{9,11},{10,... | collective-permute-start | bytes 245768 | tf_op jit(solution)/shard_map/ppermute | solution.py:379
  60.9 0.0 collective-permute-start.5
  60.9 0.0 collective-permute-done.4.other_ref
  60.9 0.1 factors.1.factor_ref
  61.0 1.0 %collective-permute-done.7.three_ref = f32[80,256]{1,0:T(8,128)S(1)} collective-permute-done((f32[80,256]{1,0:T(8,128)S(1)}, f32[80,256]{1,0:T(8,128)S(1)}, u32[]{:S(2)}, u32[]{:S(2)}) %collective-permute-start.7) | collective-permute-done | bytes 81952 | tf_op jit(solution)/shard_map/ppermute | solution.py:379
  62.0 2.3 %collective-permute-done.6.two_ref = f32[80,256]{1,0:T(8,128)S(1)} collective-permute-done((f32[80,256]{1,0:T(8,128)S(1)}, f32[80,256]{1,0:T(8,128)S(1)}, u32[]{:S(2)}, u32[]{:S(2)}) %collective-permute-start.6) | collective-permute-done | bytes 81952 | tf_op jit(solution)/shard_map/ppermute | solution.py:379
  64.3 1.9 %collective-permute-done.5.one_ref = f32[80,256]{1,0:T(8,128)S(1)} collective-permute-done((f32[80,256]{1,0:T(8,128)S(1)}, f32[80,256]{1,0:T(8,128)S(1)}, u32[]{:S(2)}, u32[]{:S(2)}) %collective-permute-start.5) | collective-permute-done | bytes 81952 | tf_op jit(solution)/shard_map/ppermute | solution.py:379
  66.2 0.7 %solve.1 = f32[5,4096]{1,0:T(8,128)} custom-call(f32[240,256]{1,0:T(8,128)S(1)} %factors.1.factor_ref, f32[80,256]{1,0:T(8,128)S(1)} %source_right.1.after_ref.own_ref, f32[80,256]{1,0:T(8,128)S(1)} %collective-permute-done.5.one_ref, f32[80,256]{1,0:T(8,128)S(1)} %collective-permute-done.6.two_ref, f32[80,256]{1,0:T(8,128)S(1)} %collective-permute-done.7.three_ref), custom_call_target="tpu_custom_call" | custom-call | flops 1000000 | bytes 573440 | tf_op jit(solution)/shard_map/solve/pallas_call | solution.py:351
Async XLA Ops:
  0.6 15.9 %copy-start.2 = (f32[128,5,128]{2,0,1:T(8,128)S(1)}, f32[128,5,128]{2,0,1:T(8,128)}, u32[]{:S(2)}) copy-start(f32[128,5,128]{2,0,1:T(8,128)} %param.14) | copy-start | bytes 983044
  3.3 13.3 %copy-start.3 = (s32[128,128]{1,0:T(8,128)S(1)}, s32[128,128]{1,0:T(8,128)}, u32[]{:S(2)}) copy-start(s32[128,128]{1,0:T(8,128)} %get-tuple-element.10.marked_ref) | copy-start | bytes 196612
  3.3 23.2 %all-to-all-start = ((f32[64,4,128]{2,1,0:T(4,128)}), f32[64,4,128]{2,1,0:T(4,128)S(1)}, u32[]{:S(2)}, u32[]{:S(2)}) async-start(f32[64,4,128]{2,1,0:T(4,128)} %bitcast.18), calls=%async_computation | async-start | bytes 262144 | tf_op jit(solution)/shard_map/all_to_all | solution.py:384
  21.7 8.8 %collective-permute-start.3 = (f32[240,256]{1,0:T(8,128)S(1)}, f32[240,256]{1,0:T(8,128)S(1)}, u32[]{:S(2)}, u32[]{:S(2)}) collective-permute-start(f32[240,256]{1,0:T(8,128)S(1)} %source_normals.1.after_ref.normal_ref), channel_id=1, source_target_pairs={{0,1},{1,0},{2,3},{3,2},{4,5},{5,4},{6,7},{7,6},{8,9},{9,8},{10,11... | collective-permute-start | bytes 737288 | tf_op jit(solution)/shard_map/ppermute | solution.py:374
  26.5 7.7 %copy-start = (bf16[120,352]{1,0:T(8,128)(2,1)S(1)}, bf16[120,352]{1,0:T(8,128)(2,1)}, u32[]{:S(2)}) copy-start(bf16[120,352]{1,0:T(8,128)(2,1)} %constant.2.clone.table_ref) | copy-start | bytes 253444
  26.8 28.8 %copy-start.1 = (f32[768,128]{1,0:T(8,128)S(1)}, f32[768,128]{1,0:T(8,128)}, u32[]{:S(2)}) copy-start(f32[768,128]{1,0:T(8,128)} %get-tuple-element.15.obs_ref) | copy-start | bytes 1179652
  26.8 3.7 %collective-permute-start.2 = (f32[88,128]{1,0:T(8,128)S(1)}, f32[88,128]{1,0:T(8,128)S(1)}, u32[]{:S(2)}, u32[]{:S(2)}) collective-permute-start(f32[88,128]{1,0:T(8,128)S(1)} %bins.1.own_ref), channel_id=1, source_target_pairs={{0,3},{1,0},{2,1},{3,2},{4,7},{5,4},{6,5},{7,6},{8,11},{9,8},{10,9... | collective-permute-start | bytes 135176 | tf_op jit(solution)/shard_map/ppermute | solution.py:379
  29.4 4.4 %collective-permute-start.1 = (f32[88,128]{1,0:T(8,128)S(1)}, f32[88,128]{1,0:T(8,128)S(1)}, u32[]{:S(2)}, u32[]{:S(2)}) collective-permute-start(f32[88,128]{1,0:T(8,128)S(1)} %bins.1.own_ref), channel_id=1, source_target_pairs={{0,2},{1,3},{2,0},{3,1},{4,6},{5,7},{6,4},{7,5},{8,10},{9,11},{10,... | collective-permute-start | bytes 135176 | tf_op jit(solution)/shard_map/ppermute | solution.py:379
  29.9 4.4 %collective-permute-start = (f32[88,128]{1,0:T(8,128)S(1)}, f32[88,128]{1,0:T(8,128)S(1)}, u32[]{:S(2)}, u32[]{:S(2)}) collective-permute-start(f32[88,128]{1,0:T(8,128)S(1)} %bins.1.own_ref), channel_id=1, source_target_pairs={{0,1},{1,2},{2,3},{3,0},{4,5},{5,6},{6,7},{7,4},{8,9},{9,10},{10,1... | collective-permute-start | bytes 135176 | tf_op jit(solution)/shard_map/ppermute | solution.py:379
  37.0 18.6 %all-to-all-start.1 = ((f32[64,1,128]{2,1,0:T(1,128)}), f32[64,1,128]{2,1,0:T(1,128)S(1)}, u32[]{:S(2)}, u32[]{:S(2)}) async-start(f32[64,1,128]{2,1,0:T(1,128)} %bitcast.8), calls=%async_computation.1 | async-start | bytes 65536 | tf_op jit(solution)/shard_map/all_to_all | solution.py:384
  46.5 9.1 %copy-start.4 = (f32[8,128]{1,0:T(8,128)S(1)}, f32[8,128]{1,0:T(8,128)}, u32[]{:S(2)}) copy-start(f32[8,128]{1,0:T(8,128)} %get-tuple-element.14.slot_ref) | copy-start | bytes 12292
  46.5 14.4 %collective-permute-start.4 = (f32[240,256]{1,0:T(8,128)S(1)}, f32[240,256]{1,0:T(8,128)S(1)}, u32[]{:S(2)}, u32[]{:S(2)}) collective-permute-start(f32[240,256]{1,0:T(8,128)S(1)} %get-tuple-element.12.own_ref), channel_id=1, source_target_pairs={{0,3},{1,2},{2,1},{3,0},{4,7},{5,6},{6,5},{7,4},{8,11},{9,10},{10,... | collective-permute-start | bytes 737288 | tf_op jit(solution)/shard_map/ppermute | solution.py:374
  58.6 3.4 %collective-permute-start.7 = (f32[80,256]{1,0:T(8,128)S(1)}, f32[80,256]{1,0:T(8,128)S(1)}, u32[]{:S(2)}, u32[]{:S(2)}) collective-permute-start(f32[80,256]{1,0:T(8,128)S(1)} %source_right.1.after_ref.own_ref), channel_id=1, source_target_pairs={{0,3},{1,0},{2,1},{3,2},{4,7},{5,4},{6,5},{7,6},{8,11},{9,8},{10,9... | collective-permute-start | bytes 245768 | tf_op jit(solution)/shard_map/ppermute | solution.py:379
  59.5 4.8 %collective-permute-start.6 = (f32[80,256]{1,0:T(8,128)S(1)}, f32[80,256]{1,0:T(8,128)S(1)}, u32[]{:S(2)}, u32[]{:S(2)}) collective-permute-start(f32[80,256]{1,0:T(8,128)S(1)} %source_right.1.after_ref.own_ref), channel_id=1, source_target_pairs={{0,2},{1,3},{2,0},{3,1},{4,6},{5,7},{6,4},{7,5},{8,10},{9,11},{10,... | collective-permute-start | bytes 245768 | tf_op jit(solution)/shard_map/ppermute | solution.py:379
  60.9 5.2 %collective-permute-start.5 = (f32[80,256]{1,0:T(8,128)S(1)}, f32[80,256]{1,0:T(8,128)S(1)}, u32[]{:S(2)}, u32[]{:S(2)}) collective-permute-start(f32[80,256]{1,0:T(8,128)S(1)} %source_right.1.after_ref.own_ref), channel_id=1, source_target_pairs={{0,1},{1,2},{2,3},{3,0},{4,5},{5,6},{6,7},{7,4},{8,9},{9,10},{10,1... | collective-permute-start | bytes 245768 | tf_op jit(solution)/shard_map/ppermute | solution.py:379

commit v12 on v11

--- a/solution.py
+++ b/solution.py
@@ -21,7 +21,7 @@
 N_CCD = 4
 HIGH = 16
 LOW = 256
-DOT_BLOCKS = 8
+DOT_BLOCKS = 16
 
 KNOT_PRIOR = 1.0
 SOURCE_PRIOR = 1.0
@@ -257,7 +257,7 @@
     gains = [gain_ref[NBLK * p : NBLK * p + NBLK, :] for p in range(5)]
     for at, (first, second) in enumerate(PAIR_LIST):
         put_terms(terms_ref, at, gains[first] * gains[second])
-    source_sums(15, 64, terms_ref, high_ref, low_ref, out_ref, *work)
+    source_sums(15, NBLK, terms_ref, high_ref, low_ref, out_ref, *work)
 
 
 def source_right_kernel(

time: 67.1 us -> 66.6 us (level)
  transfers between devices with their start and end apart: 10 -> 10, of which waited for: 7 -> 7; matrix products, arithmetic and copies ran while one was open for 0% -> 0% of each run, Pallas kernels for 13% -> 12%
where the time goes in v12:
time: 66.6 us; the launch traced here: 66.3 us
  starting transfers between devices  30.7 us (46%)
  waiting for transfers between devices  20.9 us (31%)
  Pallas kernels  14 us (21%)
  between operations  0.74 us (1%)
    all_to_all x2, starting transfers between devices, to_windows(): lax.all_to_all(values, ('src', 'win'), split_axis=0, concat_axis=0, tiled...  22.4 us
    pallas_call x7, Pallas kernels, kernel_call(): pl.pallas_call(body, out_shape=outs, in_specs=[pl.BlockSpec(memory_space=...  14 us
    all_to_all x2, waiting for transfers between devices, to_windows(): lax.all_to_all(values, ('src', 'win'), split_axis=0, concat_axis=0, tiled...  12 us
    ppermute x6, waiting for transfers between devices, from_others(): lax.ppermute(values, 'ccd', [(at, (at + shift) % N_CCD) for at in range(N...  8.88 us
    ppermute x6, starting transfers between devices, from_others(): lax.ppermute(values, 'ccd', [(at, (at + shift) % N_CCD) for at in range(N...  5.97 us
    ppermute x2, starting transfers between devices, swapped(): return lax.ppermute(values, 'ccd', list(enumerate(partner)))  2.33 us
  transfers between devices with their start and end apart: 10, of which 7 were waited for; matrix products, arithmetic and copies ran while one was open for 0% of the time, Pallas kernels for 12%

profile of v12, /device:TPU:1, one launch (start us, length us, event | category | flops | bytes accessed | tf_op | source)
XLA Modules:
  0.0 66.3 jit_solution(13535272093733403786)
XLA Ops:
  0.6 0.0 copy-start.2
  0.6 2.6 %normals.1 = (f32[256,128]{1,0:T(8,128)}, f32[768,128]{1,0:T(8,128)}, f32[8,128]{1,0:T(8,128)}, s32[128,128]{1,0:T(8,128)}) custom-call(s32[1,128]{1,0:T(1,128)} %bitcast.19, s32[1,128]{1,0:T(1,128)} %bitcast.20, f32[128,128]{1,0:T(8,128)} %refs_2_.1, f32[512,128]{1,0:T(8,128)} %bitcast.17, f32[128,128]{1,0:T(8,128)} %refs_4_.1, s32[128,128]{1,0:T(8,128)} %refs_5_.1), custom_call_target="tpu_custom_call" | custom-call | flops 1000000 | bytes 459776 | tf_op jit(solution)/shard_map/normals/pallas_call | solution.py:351
  3.3 0.0 copy-start.3
  3.3 13.3 %all-to-all-start = ((f32[64,4,128]{2,1,0:T(4,128)}), f32[64,4,128]{2,1,0:T(4,128)S(1)}, u32[]{:S(2)}, u32[]{:S(2)}) async-start(f32[64,4,128]{2,1,0:T(4,128)} %bitcast.18), calls=%async_computation | async-start | bytes 262144 | tf_op jit(solution)/shard_map/all_to_all | solution.py:384
  16.6 0.0 copy-done.2
  16.6 0.0 copy-done.3
  16.6 4.7 %source_normals.1.after_ref.normal_ref = f32[240,256]{1,0:T(8,128)S(1)} custom-call(s32[128,128]{1,0:T(8,128)S(1)} %copy-done.3, f32[640,128]{1,0:T(8,128)S(1)} %bitcast.15), custom_call_target="tpu_custom_call" | custom-call | flops 4026531840 | bytes 393216 | tf_op jit(solution)/shard_map/source_normals/pallas_call | solution.py:351
  21.3 1.3 %collective-permute-start.3 = (f32[240,256]{1,0:T(8,128)S(1)}, f32[240,256]{1,0:T(8,128)S(1)}, u32[]{:S(2)}, u32[]{:S(2)}) collective-permute-start(f32[240,256]{1,0:T(8,128)S(1)} %source_normals.1.after_ref.normal_ref), channel_id=1, source_target_pairs={{0,1},{1,0},{2,3},{3,2},{4,5},{5,4},{6,7},{7,6},{8,9},{9,8},{10,11... | collective-permute-start | bytes 737288 | tf_op jit(solution)/shard_map/ppermute | solution.py:374
  22.6 3.9 %all-to-all-done = f32[64,4,128]{2,1,0:T(4,128)S(1)} async-done(((f32[64,4,128]{2,1,0:T(4,128)}), f32[64,4,128]{2,1,0:T(4,128)S(1)}, u32[]{:S(2)}, u32[]{:S(2)}) %all-to-all-start) | async-done | bytes 131104 | tf_op jit(solution)/shard_map/all_to_all | solution.py:384
  26.5 0.0 copy-start
  26.5 0.3 bins.1.own_ref
  26.8 0.0 copy-start.1
  26.8 2.6 %collective-permute-start.2 = (f32[88,128]{1,0:T(8,128)S(1)}, f32[88,128]{1,0:T(8,128)S(1)}, u32[]{:S(2)}, u32[]{:S(2)}) collective-permute-start(f32[88,128]{1,0:T(8,128)S(1)} %bins.1.own_ref), channel_id=1, source_target_pairs={{0,3},{1,0},{2,1},{3,2},{4,7},{5,4},{6,5},{7,6},{8,11},{9,8},{10,9... | collective-permute-start | bytes 135176 | tf_op jit(solution)/shard_map/ppermute | solution.py:379
  29.4 0.5 collective-permute-start.1
  29.9 0.6 collective-permute-start
  30.5 0.0 collective-permute-done.3.other_ref
  30.5 0.0 collective-permute-done.2.three_ref
  30.5 3.3 %collective-permute-done.1.two_ref = f32[88,128]{1,0:T(8,128)S(1)} collective-permute-done((f32[88,128]{1,0:T(8,128)S(1)}, f32[88,128]{1,0:T(8,128)S(1)}, u32[]{:S(2)}, u32[]{:S(2)}) %collective-permute-start.1) | collective-permute-done | bytes 45088 | tf_op jit(solution)/shard_map/ppermute | solution.py:379
  33.8 0.5 collective-permute-done.one_ref
  34.2 0.0 copy-done
  34.2 2.7 %attitude.1 = (f32[1,4,128]{2,1,0:T(4,128)}, f32[64,128]{1,0:T(8,128)}, f32[240,256]{1,0:T(8,128)S(1)}) custom-call(f32[88,128]{1,0:T(8,128)S(1)} %bins.1.own_ref, f32[88,128]{1,0:T(8,128)S(1)} %collective-permute-done.one_ref, f32[88,128]{1,0:T(8,128)S(1)} %collective-permute-done.1.two_ref, f32[88,128]{1,0:T(8,128)S(1)} %collective-permute-done.2.three_ref, ...), custom_call_target="tpu_custom_call" | custom-call | flops 1000000 | bytes 971776 | tf_op jit(solution)/shard_map/attitude/pallas_call | solution.py:351
  37.0 9.1 %all-to-all-start.1 = ((f32[64,1,128]{2,1,0:T(1,128)}), f32[64,1,128]{2,1,0:T(1,128)S(1)}, u32[]{:S(2)}, u32[]{:S(2)}) async-start(f32[64,1,128]{2,1,0:T(1,128)} %bitcast.8), calls=%async_computation.1 | async-start | bytes 65536 | tf_op jit(solution)/shard_map/all_to_all | solution.py:384
  46.1 0.0 copy-start.4
  46.1 1.0 %collective-permute-start.4 = (f32[240,256]{1,0:T(8,128)S(1)}, f32[240,256]{1,0:T(8,128)S(1)}, u32[]{:S(2)}, u32[]{:S(2)}) collective-permute-start(f32[240,256]{1,0:T(8,128)S(1)} %get-tuple-element.12.own_ref), channel_id=1, source_target_pairs={{0,3},{1,2},{2,1},{3,0},{4,7},{5,6},{6,5},{7,4},{8,11},{9,10},{10,... | collective-permute-start | bytes 737288 | tf_op jit(solution)/shard_map/ppermute | solution.py:374
  47.1 8.0 %all-to-all-done.1 = f32[64,1,128]{2,1,0:T(1,128)S(1)} async-done(((f32[64,1,128]{2,1,0:T(1,128)}), f32[64,1,128]{2,1,0:T(1,128)S(1)}, u32[]{:S(2)}, u32[]{:S(2)}) %all-to-all-start.1) | async-done | bytes 32800 | tf_op jit(solution)/shard_map/all_to_all | solution.py:384
  55.2 0.0 copy-done.1
  55.2 0.0 copy-done.4
  55.2 2.9 %source_right.1.after_ref.own_ref = f32[80,256]{1,0:T(8,128)S(1)} custom-call(f32[64,128]{1,0:T(8,128)S(1)} %bitcast.14, f32[8,128]{1,0:T(8,128)S(1)} %copy-done.4, f32[768,128]{1,0:T(8,128)S(1)} %copy-done.1, s32[128,128]{1,0:T(8,128)S(1)} %copy-done.3, f32[640,128]{1,0:T(8,128)S(1)} %bitcast.16), custom_call_target="tpu_custom_call" | custom-call | flops 1342177280 | bytes 823296 | tf_op jit(solution)/shard_map/source_right/pallas_call | solution.py:351
  58.1 0.8 %collective-permute-start.7 = (f32[80,256]{1,0:T(8,128)S(1)}, f32[80,256]{1,0:T(8,128)S(1)}, u32[]{:S(2)}, u32[]{:S(2)}) collective-permute-start(f32[80,256]{1,0:T(8,128)S(1)} %source_right.1.after_ref.own_ref), channel_id=1, source_target_pairs={{0,3},{1,0},{2,1},{3,2},{4,7},{5,4},{6,5},{7,6},{8,11},{9,8},{10,9... | collective-permute-start | bytes 245768 | tf_op jit(solution)/shard_map/ppermute | solution.py:379
  58.9 1.4 %collective-permute-start.6 = (f32[80,256]{1,0:T(8,128)S(1)}, f32[80,256]{1,0:T(8,128)S(1)}, u32[]{:S(2)}, u32[]{:S(2)}) collective-permute-start(f32[80,256]{1,0:T(8,128)S(1)} %source_right.1.after_ref.own_ref), channel_id=1, source_target_pairs={{0,2},{1,3},{2,0},{3,1},{4,6},{5,7},{6,4},{7,5},{8,10},{9,11},{10,... | collective-permute-start | bytes 245768 | tf_op jit(solution)/shard_map/ppermute | solution.py:379
  60.4 0.0 collective-permute-start.5
  60.4 0.0 collective-permute-done.4.other_ref
  60.4 0.1 factors.1.factor_ref
  60.5 1.0 %collective-permute-done.7.three_ref = f32[80,256]{1,0:T(8,128)S(1)} collective-permute-done((f32[80,256]{1,0:T(8,128)S(1)}, f32[80,256]{1,0:T(8,128)S(1)}, u32[]{:S(2)}, u32[]{:S(2)}) %collective-permute-start.7) | collective-permute-done | bytes 81952 | tf_op jit(solution)/shard_map/ppermute | solution.py:379
  61.4 2.3 %collective-permute-done.6.two_ref = f32[80,256]{1,0:T(8,128)S(1)} collective-permute-done((f32[80,256]{1,0:T(8,128)S(1)}, f32[80,256]{1,0:T(8,128)S(1)}, u32[]{:S(2)}, u32[]{:S(2)}) %collective-permute-start.6) | collective-permute-done | bytes 81952 | tf_op jit(solution)/shard_map/ppermute | solution.py:379
  63.7 1.9 %collective-permute-done.5.one_ref = f32[80,256]{1,0:T(8,128)S(1)} collective-permute-done((f32[80,256]{1,0:T(8,128)S(1)}, f32[80,256]{1,0:T(8,128)S(1)}, u32[]{:S(2)}, u32[]{:S(2)}) %collective-permute-start.5) | collective-permute-done | bytes 81952 | tf_op jit(solution)/shard_map/ppermute | solution.py:379
  65.6 0.7 %solve.1 = f32[5,4096]{1,0:T(8,128)} custom-call(f32[240,256]{1,0:T(8,128)S(1)} %factors.1.factor_ref, f32[80,256]{1,0:T(8,128)S(1)} %source_right.1.after_ref.own_ref, f32[80,256]{1,0:T(8,128)S(1)} %collective-permute-done.5.one_ref, f32[80,256]{1,0:T(8,128)S(1)} %collective-permute-done.6.two_ref, f32[80,256]{1,0:T(8,128)S(1)} %collective-permute-done.7.three_ref), custom_call_target="tpu_custom_call" | custom-call | flops 1000000 | bytes 573440 | tf_op jit(solution)/shard_map/solve/pallas_call | solution.py:351
Async XLA Ops:
  0.6 15.9 %copy-start.2 = (f32[128,5,128]{2,0,1:T(8,128)S(1)}, f32[128,5,128]{2,0,1:T(8,128)}, u32[]{:S(2)}) copy-start(f32[128,5,128]{2,0,1:T(8,128)} %param.14) | copy-start | bytes 983044
  3.3 13.3 %copy-start.3 = (s32[128,128]{1,0:T(8,128)S(1)}, s32[128,128]{1,0:T(8,128)}, u32[]{:S(2)}) copy-start(s32[128,128]{1,0:T(8,128)} %get-tuple-element.10.marked_ref) | copy-start | bytes 196612
  3.3 23.2 %all-to-all-start = ((f32[64,4,128]{2,1,0:T(4,128)}), f32[64,4,128]{2,1,0:T(4,128)S(1)}, u32[]{:S(2)}, u32[]{:S(2)}) async-start(f32[64,4,128]{2,1,0:T(4,128)} %bitcast.18), calls=%async_computation | async-start | bytes 262144 | tf_op jit(solution)/shard_map/all_to_all | solution.py:384
  21.3 9.2 %collective-permute-start.3 = (f32[240,256]{1,0:T(8,128)S(1)}, f32[240,256]{1,0:T(8,128)S(1)}, u32[]{:S(2)}, u32[]{:S(2)}) collective-permute-start(f32[240,256]{1,0:T(8,128)S(1)} %source_normals.1.after_ref.normal_ref), channel_id=1, source_target_pairs={{0,1},{1,0},{2,3},{3,2},{4,5},{5,4},{6,7},{7,6},{8,9},{9,8},{10,11... | collective-permute-start | bytes 737288 | tf_op jit(solution)/shard_map/ppermute | solution.py:374
  26.5 7.7 %copy-start = (bf16[120,352]{1,0:T(8,128)(2,1)S(1)}, bf16[120,352]{1,0:T(8,128)(2,1)}, u32[]{:S(2)}) copy-start(bf16[120,352]{1,0:T(8,128)(2,1)} %constant.2.clone.table_ref) | copy-start | bytes 253444
  26.8 28.4 %copy-start.1 = (f32[768,128]{1,0:T(8,128)S(1)}, f32[768,128]{1,0:T(8,128)}, u32[]{:S(2)}) copy-start(f32[768,128]{1,0:T(8,128)} %get-tuple-element.15.obs_ref) | copy-start | bytes 1179652
  26.8 3.7 %collective-permute-start.2 = (f32[88,128]{1,0:T(8,128)S(1)}, f32[88,128]{1,0:T(8,128)S(1)}, u32[]{:S(2)}, u32[]{:S(2)}) collective-permute-start(f32[88,128]{1,0:T(8,128)S(1)} %bins.1.own_ref), channel_id=1, source_target_pairs={{0,3},{1,0},{2,1},{3,2},{4,7},{5,4},{6,5},{7,6},{8,11},{9,8},{10,9... | collective-permute-start | bytes 135176 | tf_op jit(solution)/shard_map/ppermute | solution.py:379
  29.4 4.4 %collective-permute-start.1 = (f32[88,128]{1,0:T(8,128)S(1)}, f32[88,128]{1,0:T(8,128)S(1)}, u32[]{:S(2)}, u32[]{:S(2)}) collective-permute-start(f32[88,128]{1,0:T(8,128)S(1)} %bins.1.own_ref), channel_id=1, source_target_pairs={{0,2},{1,3},{2,0},{3,1},{4,6},{5,7},{6,4},{7,5},{8,10},{9,11},{10,... | collective-permute-start | bytes 135176 | tf_op jit(solution)/shard_map/ppermute | solution.py:379
  29.9 4.4 %collective-permute-start = (f32[88,128]{1,0:T(8,128)S(1)}, f32[88,128]{1,0:T(8,128)S(1)}, u32[]{:S(2)}, u32[]{:S(2)}) collective-permute-start(f32[88,128]{1,0:T(8,128)S(1)} %bins.1.own_ref), channel_id=1, source_target_pairs={{0,1},{1,2},{2,3},{3,0},{4,5},{5,6},{6,7},{7,4},{8,9},{9,10},{10,1... | collective-permute-start | bytes 135176 | tf_op jit(solution)/shard_map/ppermute | solution.py:379
  37.0 18.2 %all-to-all-start.1 = ((f32[64,1,128]{2,1,0:T(1,128)}), f32[64,1,128]{2,1,0:T(1,128)S(1)}, u32[]{:S(2)}, u32[]{:S(2)}) async-start(f32[64,1,128]{2,1,0:T(1,128)} %bitcast.8), calls=%async_computation.1 | async-start | bytes 65536 | tf_op jit(solution)/shard_map/all_to_all | solution.py:384
  46.1 9.1 %copy-start.4 = (f32[8,128]{1,0:T(8,128)S(1)}, f32[8,128]{1,0:T(8,128)}, u32[]{:S(2)}) copy-start(f32[8,128]{1,0:T(8,128)} %get-tuple-element.14.slot_ref) | copy-start | bytes 12292
  46.1 14.3 %collective-permute-start.4 = (f32[240,256]{1,0:T(8,128)S(1)}, f32[240,256]{1,0:T(8,128)S(1)}, u32[]{:S(2)}, u32[]{:S(2)}) collective-permute-start(f32[240,256]{1,0:T(8,128)S(1)} %get-tuple-element.12.own_ref), channel_id=1, source_target_pairs={{0,3},{1,2},{2,1},{3,0},{4,7},{5,6},{6,5},{7,4},{8,11},{9,10},{10,... | collective-permute-start | bytes 737288 | tf_op jit(solution)/shard_map/ppermute | solution.py:374
  58.1 3.4 %collective-permute-start.7 = (f32[80,256]{1,0:T(8,128)S(1)}, f32[80,256]{1,0:T(8,128)S(1)}, u32[]{:S(2)}, u32[]{:S(2)}) collective-permute-start(f32[80,256]{1,0:T(8,128)S(1)} %source_right.1.after_ref.own_ref), channel_id=1, source_target_pairs={{0,3},{1,0},{2,1},{3,2},{4,7},{5,4},{6,5},{7,6},{8,11},{9,8},{10,9... | collective-permute-start | bytes 245768 | tf_op jit(solution)/shard_map/ppermute | solution.py:379
  58.9 4.8 %collective-permute-start.6 = (f32[80,256]{1,0:T(8,128)S(1)}, f32[80,256]{1,0:T(8,128)S(1)}, u32[]{:S(2)}, u32[]{:S(2)}) collective-permute-start(f32[80,256]{1,0:T(8,128)S(1)} %source_right.1.after_ref.own_ref), channel_id=1, source_target_pairs={{0,2},{1,3},{2,0},{3,1},{4,6},{5,7},{6,4},{7,5},{8,10},{9,11},{10,... | collective-permute-start | bytes 245768 | tf_op jit(solution)/shard_map/ppermute | solution.py:379
  60.4 5.2 %collective-permute-start.5 = (f32[80,256]{1,0:T(8,128)S(1)}, f32[80,256]{1,0:T(8,128)S(1)}, u32[]{:S(2)}, u32[]{:S(2)}) collective-permute-start(f32[80,256]{1,0:T(8,128)S(1)} %source_right.1.after_ref.own_ref), channel_id=1, source_target_pairs={{0,1},{1,2},{2,3},{3,0},{4,5},{5,6},{6,7},{7,4},{8,9},{9,10},{10,1... | collective-permute-start | bytes 245768 | tf_op jit(solution)/shard_map/ppermute | solution.py:379
